TPU v7x, 32 devices: a whole 2x2x4 slice. The times are simulated.
32 devices in a mesh: dp: 8 (over y, x, core), ctx: 4 (over z).
Axes of the slice: x: 2, y: 2, z: 4, core: 2. Of those that a mesh axis runs over, the one named last changes fastest.
Arguments:
- hidden_in: bfloat16 [2, 8, 1024, 1024], P(None, 'dp', 'ctx'), may hold values from -6 to 6
- out_grad: bfloat16 [2, 8, 1024, 1024], P(None, 'dp', 'ctx'), may hold values from -6 to 6
- segment_ids: int32 [2, 8, 1024], P(None, 'dp', 'ctx'), may hold values from 0 to 5, as said below
- doc_positions: int32 [2, 8, 1024], P(None, 'dp', 'ctx'), may hold values from 0 to 1021, as said below
- attn_gain: bfloat16 [1024], P(('dp', 'ctx')), may hold values from 0.5 to 1.5
- head_gains: bfloat16 [128], P(('dp', 'ctx')), may hold values from 0.5 to 1.5
- w_query: bfloat16 [1024, 1024], P(('dp', 'ctx')), may hold values from -0.1875 to 0.1875
- w_key: bfloat16 [1024, 512], P(('dp', 'ctx')), may hold values from -0.1875 to 0.1875
- w_value: bfloat16 [1024, 512], P(('dp', 'ctx')), may hold values from -0.1875 to 0.1875
- w_out: bfloat16 [1024, 1024], P(('dp', 'ctx')), may hold values from -1.5 to 1.5
- ffn_gain: bfloat16 [1024], P(('dp', 'ctx')), may hold values from 0.5 to 1.5
- w_gate: bfloat16 [1024, 4608], P(('dp', 'ctx')), may hold values from -0.1875 to 0.1875
- w_up: bfloat16 [1024, 4608], P(('dp', 'ctx')), may hold values from -0.1875 to 0.1875
- w_down: bfloat16 [4608, 1024], P(('dp', 'ctx')), may hold values from -0.09375 to 0.09375
Outputs:
- block_out: bfloat16 [2, 8, 1024, 1024], P(None, 'dp', 'ctx')
- in_grad: bfloat16 [2, 8, 1024, 1024], P(None, 'dp', 'ctx')
- attn_gain_grad: float32 [1024], P(('dp', 'ctx'))
- head_gains_grad: float32 [128], P(('dp', 'ctx'))
- w_query_grad: float32 [1024, 1024], P(('dp', 'ctx'))
- w_key_grad: float32 [1024, 512], P(('dp', 'ctx'))
- w_value_grad: float32 [1024, 512], P(('dp', 'ctx'))
- w_out_grad: float32 [1024, 1024], P(('dp', 'ctx'))
- ffn_gain_grad: float32 [1024], P(('dp', 'ctx'))
- w_gate_grad: float32 [1024, 4608], P(('dp', 'ctx'))
- w_up_grad: float32 [1024, 4608], P(('dp', 'ctx'))
- w_down_grad: float32 [4608, 1024], P(('dp', 'ctx'))
Inputs may be any that keep to these rules, and one draw needn't show every extreme that they name: `segment_ids`: in each sequence the ids start at 0, rise by one at each new document and never fall. In one sequence of each index of the second dimension a single document starts within the first 256 tokens and ends within the last 256, the tokens before and after it forming one document each; in the sequence at index 0 of the second dimension that document runs from token 1 to token 1022, and the other sequence there packs documents of 200 tokens. The other sequences pack documents of 200 to 2000 tokens and at most 1022, the last one cut at the sequence's end. `doc_positions`: each token's place within its document, counting from 0 at the document's first token.
All inputs are finite; a program needn't handle non-finite values.
Results may differ from a plain program's by a relative error of at most 0.022.
Values may be sent and summed in bfloat16 or wider, within the bound.
No kernel may reach another device: no remote copies, remote signals or barrier semaphores. Data moves between devices by JAX's collectives and lax.ppermute only.
A program may use at most 320 MiB of HBM per device.

v0:
```python
import jax
import jax.numpy as jnp
from jax import lax
from jax.sharding import PartitionSpec as P

EPS = 1e-05
THETA = 1000000.0


def matmul(left, right):
    return jnp.dot(left, right, preferred_element_type=jnp.float32)


def left_trans(left, right):
    return lax.dot_general(
        left, right, (((0,), (0,)), ((), ())), preferred_element_type=jnp.float32
    )


def right_trans(left, right):
    return lax.dot_general(
        left, right, (((1,), (1,)), ((), ())), preferred_element_type=jnp.float32
    )


def norm_forward(values, gain):
    factor = lax.rsqrt(jnp.mean(values * values, -1, keepdims=True) + EPS)
    unit = values * factor
    return (unit * gain, unit, factor)


def norm_backward(incoming, unit, factor, gain):
    scaled = incoming * gain
    result = factor * (scaled - unit * jnp.mean(scaled * unit, -1, keepdims=True))
    return (result, incoming * unit)


def angles(places, half):
    freq = THETA ** (-(jnp.arange(half, dtype=jnp.float32) * 2.0 / (2 * half)))
    turn = places.astype(jnp.float32)[:, None] * freq[None, :]
    return (jnp.cos(turn)[:, None, :], jnp.sin(turn)[:, None, :])


def rotate(values, cosine, sine, sign):
    half = values.shape[-1] // 2
    first = values[..., :half]
    second = values[..., half:]
    return jnp.concatenate(
        [first * cosine - sign * second * sine, second * cosine + sign * first * sine], -1
    )


def fetch_weights(shards):
    return (
        lax.all_gather(shards[0], ("dp", "ctx"), axis=0, tiled=True),
        lax.all_gather(shards[1], ("dp", "ctx"), axis=0, tiled=True),
        lax.all_gather(shards[2], ("dp", "ctx"), axis=0, tiled=True),
        lax.all_gather(shards[3], ("dp", "ctx"), axis=0, tiled=True),
        lax.all_gather(shards[4], ("dp", "ctx"), axis=0, tiled=True),
        lax.all_gather(shards[5], ("dp", "ctx"), axis=0, tiled=True),
        lax.all_gather(shards[6], ("dp", "ctx"), axis=0, tiled=True),
        lax.all_gather(shards[7], ("dp", "ctx"), axis=0, tiled=True),
        lax.all_gather(shards[8], ("dp", "ctx"), axis=0, tiled=True),
        lax.all_gather(shards[9], ("dp", "ctx"), axis=0, tiled=True),
    )


def fetch_again(shards):
    return (
        lax.all_gather(shards[0], ("dp", "ctx"), axis=0, tiled=True),
        lax.all_gather(shards[1], ("dp", "ctx"), axis=0, tiled=True),
        lax.all_gather(shards[2], ("dp", "ctx"), axis=0, tiled=True),
        lax.all_gather(shards[3], ("dp", "ctx"), axis=0, tiled=True),
        lax.all_gather(shards[4], ("dp", "ctx"), axis=0, tiled=True),
        lax.all_gather(shards[5], ("dp", "ctx"), axis=0, tiled=True),
        lax.all_gather(shards[6], ("dp", "ctx"), axis=0, tiled=True),
        lax.all_gather(shards[7], ("dp", "ctx"), axis=0, tiled=True),
        lax.all_gather(shards[8], ("dp", "ctx"), axis=0, tiled=True),
        lax.all_gather(shards[9], ("dp", "ctx"), axis=0, tiled=True),
    )


def attention_forward(query_low, key_low, value_low, segments, again):
    rows, heads, head = query_low.shape
    kv_heads = key_low.shape[1] // head
    group = heads // kv_heads
    scale = head ** (-0.5)
    grouped = query_low.reshape(rows, kv_heads, group, head)
    query_index = lax.axis_index("ctx") * rows + jnp.arange(rows, dtype=jnp.int32)

    def visit(carry, piece):
        highest, total, summed = carry
        key_piece, value_piece, segment_piece = piece
        width = key_piece.shape[0]
        key_heads = key_piece.reshape(width, kv_heads, head)
        value_heads = value_piece.reshape(width, kv_heads, head)
        scores = (
            jnp.einsum("qkgd,skd->kgqs", grouped, key_heads, preferred_element_type=jnp.float32)
            * scale
        )
        key_index = jnp.arange(width, dtype=jnp.int32)
        allowed = (segments[:, None] == segment_piece[None, :]) & (
            query_index[:, None] >= key_index[None, :]
        )
        scores = jnp.where(allowed, scores, -1e30)
        peak = jnp.maximum(highest, jnp.max(scores, -1))
        weight = jnp.where(allowed, jnp.exp(scores - peak[..., None]), 0.0)
        total = jnp.sum(weight, -1)
        summed = jnp.einsum(
            "kgqs,skd->qkgd",
            weight.astype(jnp.bfloat16),
            value_heads,
            preferred_element_type=jnp.float32,
        )
        return (peak, total, summed)

    initial = (
        jnp.full((kv_heads, group, rows), -1e30, jnp.float32),
        jnp.zeros((kv_heads, group, rows), jnp.float32),
        jnp.zeros((rows, kv_heads, group, head), jnp.float32),
    )
    if again:
        highest, total, summed = visit(
            initial,
            (
                lax.all_gather(key_low, "ctx", axis=0, tiled=True),
                lax.all_gather(value_low, "ctx", axis=0, tiled=True),
                lax.all_gather(segments, "ctx", axis=0, tiled=True),
            ),
        )
    else:
        highest, total, summed = visit(
            initial,
            (
                lax.all_gather(key_low, "ctx", axis=0, tiled=True),
                lax.all_gather(value_low, "ctx", axis=0, tiled=True),
                lax.all_gather(segments, "ctx", axis=0, tiled=True),
            ),
        )
    attended = (summed / jnp.transpose(total, (2, 0, 1))[..., None]).reshape(rows, heads, head)
    return (attended, highest + jnp.log(total))


def forward(values_row, segments, places, weights, again):
    attn_gain, head_gains, w_query, w_key, w_value, w_out, ffn_gain, w_gate, w_up, w_down = weights
    rows = values_row.shape[0]
    head = head_gains.shape[0] // 2
    heads = w_query.shape[1] // head
    kv_heads = w_key.shape[1] // head
    gains = head_gains.astype(jnp.float32)
    state = {}
    state["values"] = values_row.astype(jnp.float32)
    normed, state["x_unit"], state["x_factor"] = norm_forward(
        state["values"], attn_gain.astype(jnp.float32)
    )
    state["a_low"] = normed.astype(jnp.bfloat16)
    query = matmul(state["a_low"], w_query).reshape(rows, heads, head)
    keys = matmul(state["a_low"], w_key).reshape(rows, kv_heads, head)
    state["value_low"] = matmul(state["a_low"], w_value).astype(jnp.bfloat16)
    state["cosine"], state["sine"] = angles(places, head // 2)
    query_normed, state["q_unit"], state["q_factor"] = norm_forward(query, gains[:head])
    key_normed, state["k_unit"], state["k_factor"] = norm_forward(keys, gains[head:])
    state["query_low"] = rotate(query_normed, state["cosine"], state["sine"], 1.0).astype(
        jnp.bfloat16
    )
    state["key_low"] = (
        rotate(key_normed, state["cosine"], state["sine"], 1.0)
        .astype(jnp.bfloat16)
        .reshape(rows, kv_heads * head)
    )
    state["attended"], state["log_total"] = attention_forward(
        state["query_low"], state["key_low"], state["value_low"], segments, again
    )
    state["attended_low"] = state["attended"].astype(jnp.bfloat16).reshape(rows, heads * head)
    hidden = state["values"] + matmul(state["attended_low"], w_out)
    normed_two, state["h_unit"], state["h_factor"] = norm_forward(
        hidden, ffn_gain.astype(jnp.float32)
    )
    state["b_low"] = normed_two.astype(jnp.bfloat16)
    state["gate"] = matmul(state["b_low"], w_gate)
    state["upper"] = matmul(state["b_low"], w_up)
    state["act_low"] = (jax.nn.silu(state["gate"]) * state["upper"]).astype(jnp.bfloat16)
    state["output"] = hidden + matmul(state["act_low"], w_down)
    return state


def backward(grad_row, segments, weights, state):
    attn_gain, head_gains, w_query, w_key, w_value, w_out, ffn_gain, w_gate, w_up, w_down = weights
    query_low = state["query_low"]
    rows, heads, head = query_low.shape
    kv_heads = state["key_low"].shape[1] // head
    group = heads // kv_heads
    scale = head ** (-0.5)
    gains = head_gains.astype(jnp.float32)
    incoming = grad_row.astype(jnp.float32)
    down_low = incoming.astype(jnp.bfloat16)
    g_down = left_trans(state["act_low"], down_low)
    d_act = right_trans(down_low, w_down)
    sigma = jax.nn.sigmoid(state["gate"])
    d_upper = (d_act * state["gate"] * sigma).astype(jnp.bfloat16)
    d_gate = (d_act * state["upper"] * sigma * (1.0 + state["gate"] * (1.0 - sigma))).astype(
        jnp.bfloat16
    )
    g_gate = left_trans(state["b_low"], d_gate)
    g_up = left_trans(state["b_low"], d_upper)
    d_normed = right_trans(d_gate, w_gate) + right_trans(d_upper, w_up)
    d_hidden, terms = norm_backward(
        d_normed, state["h_unit"], state["h_factor"], ffn_gain.astype(jnp.float32)
    )
    g_ffn = jnp.sum(terms, 0)
    d_hidden = incoming + d_hidden
    branch_low = d_hidden.astype(jnp.bfloat16)
    g_out = left_trans(state["attended_low"], branch_low)
    d_attended = (
        right_trans(branch_low, w_out).astype(jnp.bfloat16).reshape(rows, kv_heads, group, head)
    )
    delta = jnp.sum(
        d_attended.astype(jnp.float32) * state["attended"].reshape(rows, kv_heads, group, head), -1
    )
    delta = jnp.transpose(delta, (1, 2, 0))
    log_total = state["log_total"]
    grouped = query_low.reshape(rows, kv_heads, group, head)
    query_index = lax.axis_index("ctx") * rows + jnp.arange(rows, dtype=jnp.int32)
    key_piece = lax.all_gather(state["key_low"], "ctx", axis=0, tiled=True)
    value_piece = lax.all_gather(state["value_low"], "ctx", axis=0, tiled=True)
    segment_piece = lax.all_gather(segments, "ctx", axis=0, tiled=True)
    width = key_piece.shape[0]
    key_heads = key_piece.reshape(width, kv_heads, head)
    value_heads = value_piece.reshape(width, kv_heads, head)
    scores = (
        jnp.einsum("qkgd,skd->kgqs", grouped, key_heads, preferred_element_type=jnp.float32) * scale
    )
    key_index = jnp.arange(width, dtype=jnp.int32)
    allowed = (segments[:, None] == segment_piece[None, :]) & (
        query_index[:, None] >= key_index[None, :]
    )
    probs = jnp.where(allowed, jnp.exp(scores - log_total[..., None]), 0.0)
    d_probs = jnp.einsum(
        "qkgd,skd->kgqs", d_attended, value_heads, preferred_element_type=jnp.float32
    )
    d_scores = (probs * (d_probs - delta[..., None])).astype(jnp.bfloat16)
    d_query = (
        jnp.einsum("kgqs,skd->qkgd", d_scores, key_heads, preferred_element_type=jnp.float32)
        * scale
    )
    key_part = (
        jnp.einsum("kgqs,qkgd->skd", d_scores, grouped, preferred_element_type=jnp.float32) * scale
    )
    value_part = jnp.einsum(
        "kgqs,qkgd->skd", probs.astype(jnp.bfloat16), d_attended, preferred_element_type=jnp.float32
    )
    d_keys = key_part.reshape(width, kv_heads * head)
    d_values = value_part.reshape(width, kv_heads * head)
    d_query, d_keys_all, d_values_all = (d_query, d_keys, d_values)
    d_keys, d_values = (
        lax.psum_scatter(
            d_keys_all.astype(jnp.bfloat16), "ctx", scatter_dimension=0, tiled=True
        ).astype(jnp.float32),
        lax.psum_scatter(
            d_values_all.astype(jnp.bfloat16), "ctx", scatter_dimension=0, tiled=True
        ).astype(jnp.float32),
    )
    d_query = rotate(d_query.reshape(rows, heads, head), state["cosine"], state["sine"], -1.0)
    d_query, query_terms = norm_backward(d_query, state["q_unit"], state["q_factor"], gains[:head])
    d_keys = rotate(d_keys.reshape(rows, kv_heads, head), state["cosine"], state["sine"], -1.0)
    d_keys, key_terms = norm_backward(d_keys, state["k_unit"], state["k_factor"], gains[head:])
    g_heads = jnp.concatenate([jnp.sum(query_terms, (0, 1)), jnp.sum(key_terms, (0, 1))])
    query_grad_low = d_query.astype(jnp.bfloat16).reshape(rows, heads * head)
    key_grad_low = d_keys.astype(jnp.bfloat16).reshape(rows, kv_heads * head)
    value_grad_low = d_values.astype(jnp.bfloat16)
    g_query = left_trans(state["a_low"], query_grad_low)
    g_key = left_trans(state["a_low"], key_grad_low)
    g_value = left_trans(state["a_low"], value_grad_low)
    d_inner = (
        right_trans(query_grad_low, w_query)
        + right_trans(key_grad_low, w_key)
        + right_trans(value_grad_low, w_value)
    )
    d_input, terms = norm_backward(
        d_inner, state["x_unit"], state["x_factor"], attn_gain.astype(jnp.float32)
    )
    g_attn = jnp.sum(terms, 0)
    in_grad = (d_hidden + d_input).astype(jnp.bfloat16)
    return (in_grad, (g_attn, g_heads, g_query, g_key, g_value, g_out, g_ffn, g_gate, g_up, g_down))


def on_device(
    hidden_in,
    out_grad,
    segment_ids,
    doc_positions,
    attn_gain,
    head_gains,
    w_query,
    w_key,
    w_value,
    w_out,
    ffn_gain,
    w_gate,
    w_up,
    w_down,
):
    shards = (attn_gain, head_gains, w_query, w_key, w_value, w_out, ffn_gain, w_gate, w_up, w_down)
    micro = hidden_in.shape[0]
    outputs = []
    for micro_index in range(micro):
        weights = fetch_weights(shards)
        state = forward(
            hidden_in[micro_index, 0],
            segment_ids[micro_index, 0],
            doc_positions[micro_index, 0],
            weights,
            False,
        )
        outputs.append(state["output"].astype(jnp.bfloat16))
    in_grads = []
    totals = None
    for micro_index in range(micro):
        weights = fetch_again(shards)
        state = forward(
            hidden_in[micro_index, 0],
            segment_ids[micro_index, 0],
            doc_positions[micro_index, 0],
            weights,
            True,
        )
        in_grad, grads = backward(
            out_grad[micro_index, 0], segment_ids[micro_index, 0], weights, state
        )
        in_grads.append(in_grad)
        if totals is None:
            totals = grads
        else:
            totals = tuple((left + right for left, right in zip(totals, grads)))
    totals = lax.psum_scatter(totals, ("dp", "ctx"), scatter_dimension=0, tiled=True)
    block_out = jnp.stack(outputs)[:, None]
    input_grads = jnp.stack(in_grads)[:, None]
    return (
        block_out,
        input_grads,
        totals[0],
        totals[1],
        totals[2],
        totals[3],
        totals[4],
        totals[5],
        totals[6],
        totals[7],
        totals[8],
        totals[9],
    )


def solution(mesh):
    placed = (
        P(None, "dp", "ctx", None),
        P(None, "dp", "ctx", None),
        P(None, "dp", "ctx"),
        P(None, "dp", "ctx"),
        P(("dp", "ctx")),
        P(("dp", "ctx")),
        P(("dp", "ctx"), None),
        P(("dp", "ctx"), None),
        P(("dp", "ctx"), None),
        P(("dp", "ctx"), None),
        P(("dp", "ctx")),
        P(("dp", "ctx"), None),
        P(("dp", "ctx"), None),
        P(("dp", "ctx"), None),
    )
    return jax.shard_map(
        on_device,
        mesh=mesh,
        in_specs=placed,
        out_specs=(
            P(None, "dp", "ctx", None),
            P(None, "dp", "ctx", None),
            P(("dp", "ctx")),
            P(("dp", "ctx")),
            P(("dp", "ctx"), None),
            P(("dp", "ctx"), None),
            P(("dp", "ctx"), None),
            P(("dp", "ctx"), None),
            P(("dp", "ctx")),
            P(("dp", "ctx"), None),
            P(("dp", "ctx"), None),
            P(("dp", "ctx"), None),
        ),
        check_vma=False,
    )
```

profile of v0, /device:TPU:1, one launch (start us, length us, event | category | flops | bytes accessed | tf_op | source)
XLA Modules:
  0.0 2026.5 jit_solution(18228906628874597413)
XLA Ops:
  11.3 40.7 %all-reduce.7 = (bf16[128]{0:T(256)(128)(2,1)S(1)}, bf16[1024]{0:T(1024)(128)(2,1)S(1)}, bf16[1024]{0:T(1024)(128)(2,1)S(1)}) all-reduce(bf16[128]{0:T(256)(128)(2,1)S(1)} %dynamic-update-slice.1, bf16[1024]{0:T(1024)(128)(2,1)S(1)} %dynamic-update-slice, ...), channel_id=1, replica_groups=mesh['dp'=8,'ctx'=4] {'dp','ctx'}, use_global_device_ids=true, to_apply=%add.1 | all-reduce | flops 2176 | bytes 8704
  53.5 14.0 all-gather.14.cloned.1.call-done
  75.2 48.1 %all-gather.18.cloned.1.call-done = bf16[1024,512]{1,0:T(8,128)(2,1)} async-done(((bf16[32,512]{1,0:T(8,128)(2,1)}), bf16[1024,512]{1,0:T(8,128)(2,1)}) %all-gather.18.cloned.1.call-update) | async-done | bytes 1048592 | tf_op jit(solution)/shard_map/all_gather | solution.py:58
  131.5 8.0 all-gather
  139.5 6.0 all-gather.1
  146.7 5.2 all-gather.32.cloned.1.call-done
  154.1 27.2 %all-gather.16.cloned.1.call-done = bf16[1024,512]{1,0:T(8,128)(2,1)} async-done(((bf16[256,512]{1,0:T(8,128)(2,1)}), bf16[1024,512]{1,0:T(8,128)(2,1)}) %all-gather.16.cloned.1.call-update) | async-done | bytes 1048592 | tf_op jit(solution)/shard_map/all_gather | solution.py:136
  183.6 57.1 %all-gather.22.cloned.1.call-done = bf16[1024,1024]{1,0:T(8,128)(2,1)} async-done(((bf16[32,1024]{1,0:T(8,128)(2,1)}), bf16[1024,1024]{1,0:T(8,128)(2,1)}) %all-gather.22.cloned.1.call-update) | async-done | bytes 2097168 | tf_op jit(solution)/shard_map/all_gather | solution.py:57
  240.6 3.9 copy.62
  247.1 2.8 multiply_reduce_fusion.11
  252.3 17.6 all-gather.20.cloned.1.call-done
  270.0 3.8 fusion.8
  273.8 4.0 fusion.12
  279.7 4.7 fusion.148
  284.3 45.2 %all-gather.24.cloned.1.call-done = bf16[1024,1024]{1,0:T(8,128)(2,1)} async-done(((bf16[32,1024]{1,0:T(8,128)(2,1)}), bf16[1024,1024]{1,0:T(8,128)(2,1)}) %all-gather.24.cloned.1.call-update) | async-done | bytes 2097168 | tf_op jit(solution)/shard_map/all_gather | solution.py:60
  329.5 3.4 multiply_reduce_fusion.12
  332.9 26.1 %all-gather.34.cloned.1.call-done = bf16[1024,512]{0,1:T(8,128)(2,1)} async-done(((bf16[256,512]{0,1:T(8,128)(2,1)}), bf16[1024,512]{0,1:T(8,128)(2,1)}) %all-gather.34.cloned.1.call-update) | async-done | bytes 1048592 | tf_op jit(solution)/shard_map/all_gather | solution.py:135
  359.0 3.9 fusion.9
  362.9 4.2 fusion.14
  368.9 4.6 fusion.147
  377.1 66.8 %all-gather.26.cloned.1.call-done = bf16[1024,4608]{1,0:T(8,128)(2,1)} async-done(((bf16[32,4608]{1,0:T(8,128)(2,1)}), bf16[1024,4608]{1,0:T(8,128)(2,1)}) %all-gather.26.cloned.1.call-update) | async-done | bytes 9437200 | tf_op jit(solution)/shard_map/all_gather | solution.py:62
  443.9 8.6 fusion.149
  452.5 74.7 %all-gather.28.cloned.1.call-done = bf16[1024,4608]{1,0:T(8,128)(2,1)} async-done(((bf16[32,4608]{1,0:T(8,128)(2,1)}), bf16[1024,4608]{1,0:T(8,128)(2,1)}) %all-gather.28.cloned.1.call-update) | async-done | bytes 9437200 | tf_op jit(solution)/shard_map/all_gather | solution.py:63
  527.2 8.6 fusion.150
  535.9 74.8 %all-gather.30.cloned.1.call-done = bf16[4608,1024]{1,0:T(8,128)(2,1)} async-done(((bf16[144,1024]{1,0:T(8,128)(2,1)}), bf16[4608,1024]{1,0:T(8,128)(2,1)}) %all-gather.30.cloned.1.call-update) | async-done | bytes 9437200 | tf_op jit(solution)/shard_map/all_gather | solution.py:64
  610.7 10.8 multiply_convert_fusion.2
  621.6 6.1 fusion.153
  627.7 6.9 multiply_reduce_fusion.1
  634.7 4.3 fusion.151
  638.9 8.2 fusion.152
  647.1 14.5 multiply_convert_fusion
  661.6 4.4 fusion.155
  666.0 6.1 multiply_reduce_fusion
  679.8 9.6 fusion.3
  689.4 3.2 copy-done.2
  692.6 3.6 fusion.29
  701.8 9.1 fusion.1
  710.9 3.3 copy-done.3
  714.2 3.6 fusion.28
  717.9 8.7 bitcast_convert_fusion.1
  726.8 8.9 bitcast_convert_fusion
  736.9 13.5 reduce-scatter.16.cloned.1.call-done
  755.9 22.4 %reduce-scatter.14.cloned.1.call-done = bf16[256,512]{0,1:T(8,128)(2,1)} async-done(((bf16[1024,512]{0,1:T(8,128)(2,1)}), bf16[256,512]{0,1:T(8,128)(2,1)}) %reduce-scatter.14.cloned.1.call-update) | async-done | bytes 262160 | tf_op jit(solution)/shard_map/reduce_scatter | solution.py:259
  779.9 27.1 %reduce-scatter.18.cloned.1.call-done = bf16[256,512]{0,1:T(8,128)(2,1)} async-done(((bf16[1024,512]{0,1:T(8,128)(2,1)}), bf16[256,512]{0,1:T(8,128)(2,1)}) %reduce-scatter.18.cloned.1.call-update) | async-done | bytes 262160 | tf_op jit(solution)/shard_map/reduce_scatter | solution.py:259
  807.0 2.9 convolution_add_fusion.5
  809.9 5.3 convolution_multiply_fusion.1
  815.8 4.9 convolution_multiply_fusion
  822.8 2.9 convolution_add_fusion.4
  827.6 3.8 convolution_add_fusion.3
  831.5 11.1 fusion.157
  842.6 12.1 convolution_add_fusion.2
  854.8 11.1 fusion.158
  865.9 12.2 convolution_add_fusion.1
  878.4 10.9 fusion.89
  889.3 12.2 convolution_add_fusion
  902.2 7.3 fusion.54
  909.6 6.5 fusion.55
  922.8 39.1 %all-reduce.6 = (f32[1024]{0:T(1024)S(1)}, f32[128]{0:T(128)S(1)}, f32[1024]{0:T(1024)S(1)}) all-reduce(f32[1024]{0:T(1024)S(1)} %add.291, f32[128]{0:T(128)S(1)} %maximum_add_fusion, f32[1024]{0:T(1024)S(1)} %add.297), channel_id=8, replica_groups=mesh['dp'=8,'ctx'=4] {'dp','ctx'}, use_global_device_ids=true, to_apply=%region_28.29.clone | all-reduce | flops 2176 | bytes 17408
  966.8 114.3 %reduce-scatter.24.cloned.1.call-done = f32[32,512]{1,0:T(8,128)} async-done(((f32[1024,512]{1,0:T(8,128)}), f32[32,512]{1,0:T(8,128)}) %reduce-scatter.24.cloned.1.call-update) | async-done | bytes 65552 | tf_op jit(solution)/shard_map/reduce_scatter | solution.py:335
  1081.1 148.6 %reduce-scatter.20.cloned.1.call-done = f32[32,1024]{1,0:T(8,128)} async-done(((f32[1024,1024]{1,0:T(8,128)}), f32[32,1024]{1,0:T(8,128)}) %reduce-scatter.20.cloned.1.call-update) | async-done | bytes 131088 | tf_op jit(solution)/shard_map/reduce_scatter | solution.py:335
  1229.7 148.9 %reduce-scatter.26.cloned.1.call-done = f32[32,1024]{1,0:T(8,128)} async-done(((f32[1024,1024]{1,0:T(8,128)}), f32[32,1024]{1,0:T(8,128)}) %reduce-scatter.26.cloned.1.call-update) | async-done | bytes 131088 | tf_op jit(solution)/shard_map/reduce_scatter | solution.py:335
  1378.6 215.6 %reduce-scatter.28.cloned.1.call-done = f32[32,4608]{1,0:T(8,128)} async-done(((f32[1024,4608]{1,0:T(8,128)}), f32[32,4608]{1,0:T(8,128)}) %reduce-scatter.28.cloned.1.call-update) | async-done | bytes 589840 | tf_op jit(solution)/shard_map/reduce_scatter | solution.py:335
  1594.2 212.6 %reduce-scatter.30.cloned.1.call-done = f32[32,4608]{1,0:T(8,128)} async-done(((f32[1024,4608]{1,0:T(8,128)}), f32[32,4608]{1,0:T(8,128)}) %reduce-scatter.30.cloned.1.call-update) | async-done | bytes 589840 | tf_op jit(solution)/shard_map/reduce_scatter | solution.py:335
  1806.8 212.7 %reduce-scatter.32.cloned.1.call-done = f32[144,1024]{1,0:T(8,128)} async-done(((f32[4608,1024]{1,0:T(8,128)}), f32[144,1024]{1,0:T(8,128)}) %reduce-scatter.32.cloned.1.call-update) | async-done | bytes 589840 | tf_op jit(solution)/shard_map/reduce_scatter | solution.py:335
  (322 shorter events, 77.4 us)
Async XLA Ops:
  7.2 117.5 %copy-start.4 = (bf16[2,1,256,1024]{3,2,1,0:T(8,128)(2,1)S(1)}, bf16[2,1,256,1024]{3,2,1,0:T(8,128)(2,1)}, u32[]{:S(2)}) copy-start(bf16[2,1,256,1024]{3,2,1,0:T(8,128)(2,1)} %param.14) | copy-start | bytes 3145732
  7.2 60.3 %all-gather.14.cloned.1.call-start = ((), (), s32[]{:S(2)}) async-start(), calls=%async_computation.11 | async-start | bytes 1081344 | tf_op jit(solution)/shard_map/all_gather | solution.py:59
  7.9 115.3 %all-gather.18.cloned.1.call-start = ((), (), s32[]{:S(2)}) async-start(), calls=%async_computation.13 | async-start | bytes 1081344 | tf_op jit(solution)/shard_map/all_gather | solution.py:58
  8.7 143.2 %all-gather.32.cloned.1.call-start = ((), (), s32[]{:S(2)}) async-start(), calls=%async_computation.20 | async-start | bytes 1310720 | tf_op jit(solution)/shard_map/all_gather | solution.py:136
  51.9 195.1 %copy-start.64 = (f32[1024]{0:T(1024)}, f32[1024]{0:T(1024)S(1)}, u32[]{:S(2)}) copy-start(f32[1024]{0:T(1024)S(1)} %convert_element_type.280) | copy-start | bytes 12292
  53.4 193.6 %copy-start.75 = (f32[256]{0:T(256)}, f32[256]{0:T(256)S(1)}, u32[]{:S(2)}) copy-start(f32[256]{0:T(256)S(1)} %add_rsqrt_fusion.5) | copy-start | bytes 3076
  70.1 111.2 %all-gather.16.cloned.1.call-start = ((), (), s32[]{:S(2)}) async-start(), calls=%async_computation.12 | async-start | bytes 1310720 | tf_op jit(solution)/shard_map/all_gather | solution.py:136
  70.2 174.4 %copy-start.77 = (f32[256]{0:T(256)}, f32[256]{0:T(256)S(1)}, u32[]{:S(2)}) copy-start(f32[256]{0:T(256)S(1)} %add_rsqrt_fusion.7) | copy-start | bytes 3076
  70.2 61.4 %copy-start.89 = (s32[2,1,256]{2,1,0:T(1,128)S(1)}, s32[2,1,256]{2,1,0:T(1,128)}, u32[]{:S(2)}) copy-start(s32[2,1,256]{2,1,0:T(1,128)} %param.16) | copy-start | bytes 6148
  72.8 167.8 %all-gather.22.cloned.1.call-start = ((), (), s32[]{:S(2)}) async-start(), calls=%async_computation.15 | async-start | bytes 2162688 | tf_op jit(solution)/shard_map/all_gather | solution.py:57
  73.4 196.6 %all-gather.20.cloned.1.call-start = ((), (), s32[]{:S(2)}) async-start(), calls=%async_computation.14 | async-start | bytes 1310720 | tf_op jit(solution)/shard_map/all_gather | solution.py:135
  73.5 80.6 %copy-start.81 = (f32[64]{0:T(128)}, f32[64]{0:T(128)S(1)}, u32[]{:S(2)}) copy-start(f32[64]{0:T(128)S(1)} %get-tuple-element.123) | copy-start | bytes 772
  73.5 176.4 %copy-start.83 = (f32[64]{0:T(128)}, f32[64]{0:T(128)S(1)}, u32[]{:S(2)}) copy-start(f32[64]{0:T(128)S(1)} %get-tuple-element.122) | copy-start | bytes 772
  75.2 176.1 %copy-start.58 = (f32[256,32]{0,1:T(8,128)}, f32[256,32]{0,1:T(8,128)S(1)}, u32[]{:S(2)}) copy-start(f32[256,32]{0,1:T(8,128)S(1)} %get-tuple-element.116) | copy-start | bytes 98308
  75.2 176.1 %copy-start.60 = (f32[256,32]{0,1:T(8,128)}, f32[256,32]{0,1:T(8,128)S(1)}, u32[]{:S(2)}) copy-start(f32[256,32]{0,1:T(8,128)S(1)} %get-tuple-element.107) | copy-start | bytes 98308
  125.3 119.3 %copy-start.73 = (f32[256,8]{0,1:T(8,128)}, f32[256,8]{0,1:T(8,128)S(1)}, u32[]{:S(2)}) copy-start(f32[256,8]{0,1:T(8,128)S(1)} %add_rsqrt_fusion.3) | copy-start | bytes 24580
  127.8 201.7 %all-gather.24.cloned.1.call-start = ((), (), s32[]{:S(2)}) async-start(), calls=%async_computation.16 | async-start | bytes 2162688 | tf_op jit(solution)/shard_map/all_gather | solution.py:60
  128.6 230.4 %all-gather.34.cloned.1.call-start = ((), (), s32[]{:S(2)}) async-start(), calls=%async_computation.21 | async-start | bytes 1310720 | tf_op jit(solution)/shard_map/all_gather | solution.py:135
  129.4 314.5 %all-gather.26.cloned.1.call-start = ((), (), s32[]{:S(2)}) async-start(), calls=%async_computation.17 | async-start | bytes 9732096 | tf_op jit(solution)/shard_map/all_gather | solution.py:62
  130.1 397.1 %all-gather.28.cloned.1.call-start = ((), (), s32[]{:S(2)}) async-start(), calls=%async_computation.18 | async-start | bytes 9732096 | tf_op jit(solution)/shard_map/all_gather | solution.py:63
  130.7 480.0 %all-gather.30.cloned.1.call-start = ((), (), s32[]{:S(2)}) async-start(), calls=%async_computation.19 | async-start | bytes 9732096 | tf_op jit(solution)/shard_map/all_gather | solution.py:64
  131.5 604.3 %reduce-scatter.12.cloned.1.call-start = ((), (), s32[]{:S(2)}) async-start(), calls=%async_computation.22 | async-start | bytes 1310720 | tf_op jit(solution)/shard_map/reduce_scatter | solution.py:256
  146.7 131.1 %copy-start.31 = (pred[256,1024]{0,1:T(8,128)(4,1)}, pred[256,1024]{0,1:T(8,128)(4,1)S(1)}, u32[]{:S(2)}) copy-start(pred[256,1024]{0,1:T(8,128)(4,1)S(1)} %get-tuple-element.111) | copy-start | bytes 786436
  252.3 21.4 %copy-start.41 = (bf16[256,16,32]{0,2,1:T(8,128)(2,1)}, bf16[256,16,32]{0,2,1:T(8,128)(2,1)S(1)}, u32[]{:S(2)}) copy-start(bf16[256,16,32]{0,2,1:T(8,128)(2,1)S(1)} %get-tuple-element.149) | copy-start | bytes 786436
  252.3 106.7 %copy-start.37 = (bf16[256,16,32]{0,2,1:T(8,128)(2,1)}, bf16[256,16,32]{0,2,1:T(8,128)(2,1)S(1)}, u32[]{:S(2)}) copy-start(bf16[256,16,32]{0,2,1:T(8,128)(2,1)S(1)} %get-tuple-element.86) | copy-start | bytes 786436
  252.3 106.7 %copy-start.39 = (bf16[256,16,32]{0,2,1:T(8,128)(2,1)}, bf16[256,16,32]{0,2,1:T(8,128)(2,1)S(1)}, u32[]{:S(2)}) copy-start(bf16[256,16,32]{0,2,1:T(8,128)(2,1)S(1)} %get-tuple-element.87) | copy-start | bytes 786436
  284.3 78.5 %copy-start.53 = (bf16[256,8,2,64]{0,3,2,1:T(8,128)(2,1)}, bf16[256,8,2,64]{0,3,2,1:T(8,128)(2,1)S(1)}, u32[]{:S(2)}) copy-start(bf16[256,8,2,64]{0,3,2,1:T(8,128)(2,1)S(1)} %get-tuple-element.138) | copy-start | bytes 1572868
  376.1 325.7 %copy-start.79 = (f32[8,2,256]{2,1,0:T(2,128)}, f32[8,2,256]{2,1,0:T(2,128)S(1)}, u32[]{:S(2)}) copy-start(f32[8,2,256]{2,1,0:T(2,128)S(1)} %log_add_fusion) | copy-start | bytes 49156
  621.5 13.1 slice-start
  621.6 13.1 slice-start.1
  679.8 12.9 copy-start.42
  679.8 12.8 copy-start.43
  696.2 54.1 %reduce-scatter.16.cloned.1.call-start = ((), (), s32[]{:S(2)}) async-start(), calls=%async_computation.24 | async-start | bytes 1310720 | tf_op jit(solution)/shard_map/reduce_scatter | solution.py:256
  701.8 12.4 copy-start.38
  701.8 12.4 copy-start.40
  717.9 8.9 copy-start.80
  717.9 60.5 %reduce-scatter.14.cloned.1.call-start = ((), (), s32[]{:S(2)}) async-start(), calls=%async_computation.23 | async-start | bytes 1310720 | tf_op jit(solution)/shard_map/reduce_scatter | solution.py:259
  726.6 10.1 copy-start.61
  726.7 10.1 copy-start.63
  726.7 24.7 %copy-start.26 = (f32[256,8,64]{0,2,1:T(8,128)S(1)}, f32[256,8,64]{0,2,1:T(8,128)}, u32[]{:S(2)}) copy-start(f32[256,8,64]{0,2,1:T(8,128)} %copy-done.25) | copy-start | bytes 1572868
  726.7 24.7 %copy-start.74 = (f32[256,8]{0,1:T(8,128)S(1)}, f32[256,8]{0,1:T(8,128)}, u32[]{:S(2)}) copy-start(f32[256,8]{0,1:T(8,128)} %copy-done.73) | copy-start | bytes 24580
  726.7 24.7 %copy-start.82 = (f32[64]{0:T(128)S(1)}, f32[64]{0:T(128)}, u32[]{:S(2)}) copy-start(f32[64]{0:T(128)} %copy-done.81) | copy-start | bytes 772
  726.7 25.4 %copy-start.59 = (f32[256,32]{0,1:T(8,128)S(1)}, f32[256,32]{0,1:T(8,128)}, u32[]{:S(2)}) copy-start(f32[256,32]{0,1:T(8,128)} %copy-done.58) | copy-start | bytes 98308
  726.7 25.4 %copy-start.62 = (f32[256,32]{0,1:T(8,128)S(1)}, f32[256,32]{0,1:T(8,128)}, u32[]{:S(2)}) copy-start(f32[256,32]{0,1:T(8,128)} %get-tuple-element.117) | copy-start | bytes 98308
  726.7 25.4 %copy-start.24 = (f32[256,8,64]{0,2,1:T(8,128)S(1)}, f32[256,8,64]{0,2,1:T(8,128)}, u32[]{:S(2)}) copy-start(f32[256,8,64]{0,2,1:T(8,128)} %copy-done.23) | copy-start | bytes 1572868
  726.7 25.4 %copy-start.72 = (f32[256,8]{0,1:T(8,128)S(1)}, f32[256,8]{0,1:T(8,128)}, u32[]{:S(2)}) copy-start(f32[256,8]{0,1:T(8,128)} %copy-done.71) | copy-start | bytes 24580
  726.8 80.2 %reduce-scatter.18.cloned.1.call-start = ((), (), s32[]{:S(2)}) async-start(), calls=%async_computation.25 | async-start | bytes 1310720 | tf_op jit(solution)/shard_map/reduce_scatter | solution.py:259
  735.7 17.5 copy-start.65
  735.7 17.5 copy-start.78
  735.7 18.1 copy-start.76
  735.7 231.1 %reduce-scatter.22.cloned.1.call-start = ((), (), s32[]{:S(2)}) async-start(), calls=%async_computation.27 | async-start | bytes 2162688 | tf_op jit(solution)/shard_map/reduce_scatter | solution.py:335
  755.7 325.4 %reduce-scatter.24.cloned.1.call-start = ((), (), s32[]{:S(2)}) async-start(), calls=%async_computation.28 | async-start | bytes 2162688 | tf_op jit(solution)/shard_map/reduce_scatter | solution.py:335
  809.9 419.9 %reduce-scatter.20.cloned.1.call-start = ((), (), s32[]{:S(2)}) async-start(), calls=%async_computation.26 | async-start | bytes 4325376 | tf_op jit(solution)/shard_map/reduce_scatter | solution.py:335
  825.7 552.9 %reduce-scatter.26.cloned.1.call-start = ((), (), s32[]{:S(2)}) async-start(), calls=%async_computation.29 | async-start | bytes 4325376 | tf_op jit(solution)/shard_map/reduce_scatter | solution.py:335
  831.4 762.8 %reduce-scatter.28.cloned.1.call-start = ((), (), s32[]{:S(2)}) async-start(), calls=%async_computation.30 | async-start | bytes 19464192 | tf_op jit(solution)/shard_map/reduce_scatter | solution.py:335
  831.4 11.1 copy-start.11
  831.4 11.1 copy-start.47
  854.7 952.1 %reduce-scatter.30.cloned.1.call-start = ((), (), s32[]{:S(2)}) async-start(), calls=%async_computation.31 | async-start | bytes 19464192 | tf_op jit(solution)/shard_map/reduce_scatter | solution.py:335
  854.8 11.1 copy-start.12
  854.8 11.1 copy-start.46
  878.1 1141.3 %reduce-scatter.32.cloned.1.call-start = ((), (), s32[]{:S(2)}) async-start(), calls=%async_computation.32 | async-start | bytes 19464192 | tf_op jit(solution)/shard_map/reduce_scatter | solution.py:335
  878.4 10.9 copy-start.22
  878.4 10.9 copy-start.34
  909.6 8.3 copy-start.30
  (51 other events, 212.2 us)
Sparse Core Ops, SparseCore 0:
  11.0 56.4 all-gather.13
  70.5 52.7 all-gather.17
  125.4 26.4 all-gather.31
  153.9 27.3 all-gather.15
  184.1 56.5 all-gather.21
  242.6 27.2 all-gather.19
  272.9 56.5 all-gather.23
  331.7 27.2 all-gather.33
  361.8 82.0 all-gather.25
  446.6 80.6 all-gather.27
  530.0 80.6 all-gather.29
  696.4 25.1 reduce-scatter.11
  724.5 25.7 reduce-scatter.15
  752.5 25.7 reduce-scatter.13
  781.2 25.7 reduce-scatter.17
  809.7 132.4 reduce-scatter.21
  945.0 136.0 reduce-scatter.23
  1083.8 145.8 reduce-scatter.19
  1232.6 145.9 reduce-scatter.25
  1385.4 208.7 reduce-scatter.27
  1601.2 205.5 reduce-scatter.29
  1813.8 205.6 reduce-scatter.31
where the time goes:
time: 2030 us
  waiting for transfers between devices  1580 us (78%)
  matrix products  275 us (14%)
  blocking collectives  93.8 us (5%)
  local copies, waits for them, and re-layouts  32.7 us (2%)
  other arithmetic  31.1 us (2%)
    reduce_scatter x7, waiting for transfers between devices, on_device(): lax.psum_scatter(totals, ('dp', 'ctx'), scatter_dimension=0, tiled=True)  1050 us
    dot_general x14, matrix products, left_trans(): lax.dot_general(left, right, (((0,), (0,)), ((), ())), preferred_element_...  85.8 us
    unnamed x2, blocking collectives  79.8 us
    all_gather x1, waiting for transfers between devices, fetch_weights(): lax.all_gather(shards[9], ('dp', 'ctx'), axis=0, tiled=True)  74.8 us
    all_gather x1, waiting for transfers between devices, fetch_weights(): lax.all_gather(shards[8], ('dp', 'ctx'), axis=0, tiled=True)  74.7 us
    all_gather x1, waiting for transfers between devices, fetch_weights(): lax.all_gather(shards[7], ('dp', 'ctx'), axis=0, tiled=True)  66.8 us
    dot_general x14, matrix products, matmul(): return jnp.dot(left, right, preferred_element_type=jnp.float32)  60.2 us
    dot_general x14, matrix products, right_trans(): lax.dot_general(left, right, (((1,), (1,)), ((), ())), preferred_element_...  58 us
  transfers between devices with their start and end apart: 22, of which 20 were waited for; matrix products, arithmetic and copies ran while one was open for 12% of the time, Pallas kernels for 0%

commit v1 on v0

--- a/solution.py
+++ b/solution.py
@@ -1,6 +1,10 @@
+import functools
+
 import jax
 import jax.numpy as jnp
 from jax import lax
+from jax.experimental import pallas as pl
+from jax.experimental.pallas import tpu as pltpu
 from jax.sharding import PartitionSpec as P
 
 EPS = 1e-05
@@ -351,6 +355,672 @@
     )
 
 
+CORE, SIDE, HIGH = 1, 2, 4
+
+
+def flip(array, bits):
+    count = lax.axis_size("dp")
+    return lax.ppermute(array, "dp", [(i, i ^ bits) for i in range(count)])
+
+
+def spin(array):
+    count = lax.axis_size("ctx")
+    return lax.ppermute(array, "ctx", [(i, (i + 1) % count) for i in range(count)])
+
+
+def after(array, *others):
+    return lax.optimization_barrier((array,) + others)[0]
+
+
+def choose(bit, zero, one):
+    return jnp.where(bit == 0, zero, one)
+
+
+def pick(array, index, axis=0):
+    return lax.dynamic_index_in_dim(array, index, axis, keepdims=False)
+
+
+def put(buffer, array, *place):
+    index = place + (0,) * (buffer.ndim - len(place))
+    shape = (1,) * (buffer.ndim - array.ndim) + array.shape
+    return lax.dynamic_update_slice(buffer, array.reshape(shape), index)
+
+
+def joined(*arrays):
+    buffer = jnp.zeros((len(arrays),) + arrays[0].shape, arrays[0].dtype)
+    for at, array in enumerate(arrays):
+        buffer = put(buffer, array, at)
+    return buffer
+
+
+def order(bit, own, other):
+    buffer = jnp.zeros((2,) + own.shape, own.dtype)
+    return put(put(buffer, own, bit), other, 1 - bit)
+
+
+def swap_halves(bit, array, axis):
+    low, high = jnp.split(array, 2, axis)
+    return choose(bit, array, jnp.concatenate([high, low], axis))
+
+
+def half_of(bit, array, axis):
+    low, high = jnp.split(array, 2, axis)
+    return choose(bit, low, high)
+
+
+def exchange(array, target, index_of, turn):
+    dp_count, ctx_count = lax.axis_size("dp"), lax.axis_size("ctx")
+    pairs, stay = [], []
+    for dp in range(dp_count):
+        for z in range(ctx_count):
+            to = target(dp, z, turn)
+            if to == (dp, z):
+                stay.append(dp * ctx_count + z)
+            else:
+                pairs.append((dp * ctx_count + z, to[0] * ctx_count + to[1]))
+    piece = pick(array, index_of(turn))
+    got = lax.ppermute(piece, ("dp", "ctx"), pairs)
+    if stay:
+        me = lax.axis_index("dp") * ctx_count + lax.axis_index("ctx")
+        mine = functools.reduce(jnp.logical_or, [me == which for which in stay])
+        got = jnp.where(mine, piece, got)
+    return got
+
+
+def spread(array):
+    ctx = lax.axis_index("ctx")
+
+    def target(dp, z, turn):
+        return dp // 2 * 2 + z // 2, 2 * ((z + turn) % 2) + dp % 2
+
+    got = [exchange(array, target, lambda turn: (ctx + turn) % 2, turn) for turn in range(2)]
+    return order(ctx // 2, got[0], got[1])
+
+
+def unspread(array):
+    ctx = lax.axis_index("ctx")
+
+    def target(dp, z, turn):
+        return dp // 2 * 2 + z % 2, 2 * (dp % 2) + (z // 2 + turn) % 2
+
+    got = [exchange(array, target, lambda turn: (ctx // 2 + turn) % 2, turn) for turn in range(2)]
+    return order(ctx % 2, got[0], got[1])
+
+
+def swap_gather(array, bit_value, bit):
+    return order(bit_value, array, flip(array, bit))
+
+
+def total_low(left, right):
+    return (left.astype(jnp.float32) + right.astype(jnp.float32)).astype(jnp.bfloat16)
+
+
+def team_gather(array, gate=None):
+    side, core = flip(array, SIDE), flip(array, CORE)
+    return joined(array, side, core, flip(side, CORE)).reshape((-1,) + array.shape[1:])
+
+
+def team_reduce(array):
+    got = flip(array[2:].astype(jnp.bfloat16), CORE).astype(jnp.float32)
+    side = flip((array[1] + got[1]).astype(jnp.bfloat16), SIDE)
+    return array[0] + got[0] + side.astype(jnp.float32)
+
+
+def nt(left, right):
+    return lax.dot_general(
+        left, right, (((1,), (1,)), ((), ())), preferred_element_type=jnp.float32
+    )
+
+
+def set_bias(bias_ref, seg_row_ref, seg_col_ref, block):
+    size = bias_ref.shape[0]
+    for first in range(0, size, block):
+        for key in range(0, first + block, block):
+            allowed = seg_col_ref[key : key + block, :] == seg_row_ref[:, first : first + block]
+            if key == first:
+                keys = lax.broadcasted_iota(jnp.int32, (block, block), 0)
+                queries = lax.broadcasted_iota(jnp.int32, (block, block), 1)
+                allowed = jnp.logical_and(allowed, keys <= queries)
+            bias_ref[key : key + block, first : first + block] = jnp.where(allowed, 0.0, -1e30)
+
+
+def turned(values, gain, cosine, sine):
+    half = values.shape[0] // 2
+    factor = lax.rsqrt(jnp.mean(values * values, 0, keepdims=True) + EPS)
+    normed = values * factor * gain
+    first, second = normed[:half], normed[half:]
+    return jnp.concatenate([first * cosine - second * sine, second * cosine + first * sine], 0)
+
+
+def turned_back(incoming, values, gain, cosine, sine):
+    half = values.shape[0] // 2
+    first, second = incoming[:half], incoming[half:]
+    incoming = jnp.concatenate(
+        [first * cosine + second * sine, second * cosine - first * sine], 0
+    )
+    factor = lax.rsqrt(jnp.mean(values * values, 0, keepdims=True) + EPS)
+    unit = values * factor
+    terms = jnp.sum(incoming * unit, 1, keepdims=True)
+    scaled = incoming * gain
+    return factor * (scaled - unit * jnp.mean(scaled * unit, 0, keepdims=True)), terms
+
+
+def forward_kernel(
+    block, q_ref, kv_ref, cos_ref, sin_ref, gain_ref, row_ref, col_ref,
+    o_ref, log_ref, qr_ref, kvr_ref, bias_ref
+):
+    head = kv_ref.shape[0] // 2
+    size = kv_ref.shape[1]
+    scale = head ** (-0.5)
+
+    @pl.when(pl.program_id(0) == 0)
+    def _():
+        set_bias(bias_ref, row_ref, col_ref, block)
+
+    cosine, sine = cos_ref[...], sin_ref[...]
+    keys = turned(kv_ref[:head, :], gain_ref[1], cosine, sine)
+    kvr_ref[:head, :] = keys
+    keys = keys.T.astype(jnp.bfloat16)
+    values = kv_ref[head:, :]
+    kvr_ref[head:, :] = values
+    values = values.astype(jnp.bfloat16)
+    for which in range(q_ref.shape[0] // head):
+        rows = slice(which * head, (which + 1) * head)
+        query = turned(q_ref[rows, :], gain_ref[0], cosine, sine)
+        qr_ref[rows, :] = query
+        query = query.astype(jnp.bfloat16)
+        for first in range(0, size, block):
+            here = slice(first, first + block)
+            total = jnp.zeros((1, block), jnp.float32)
+            summed = jnp.zeros((head, block), jnp.float32)
+            for key in range(0, first + block, block):
+                there = slice(key, key + block)
+                scores = jnp.dot(keys[there], query[:, here], preferred_element_type=jnp.float32)
+                weight = jnp.exp(scores * scale + bias_ref[there, here])
+                total += jnp.sum(weight, 0, keepdims=True)
+                summed += jnp.dot(
+                    values[:, there],
+                    weight.astype(jnp.bfloat16),
+                    preferred_element_type=jnp.float32,
+                )
+            o_ref[rows, here] = summed / total
+            log_ref[0, which : which + 1, here] = jnp.log(total)
+
+
+def backward_kernel(
+    block, q_ref, kv_ref, qr_ref, kvr_ref, do_ref, o_ref, log_ref, cos_ref, sin_ref,
+    gain_ref, row_ref, col_ref, dq_ref, dkv_ref, gains_ref, bias_ref, dkey_ref, dvalue_ref
+):
+    head = kv_ref.shape[0] // 2
+    size = kv_ref.shape[1]
+    scale = head ** (-0.5)
+
+    @pl.when(pl.program_id(0) == 0)
+    def _():
+        set_bias(bias_ref, row_ref, col_ref, block)
+        gains_ref[...] = jnp.zeros_like(gains_ref)
+
+    cosine, sine = cos_ref[...], sin_ref[...]
+    keys_t = kvr_ref[:head, :]
+    keys = keys_t.T.astype(jnp.bfloat16)
+    keys_t = keys_t.astype(jnp.bfloat16)
+    values = kvr_ref[head:, :].T.astype(jnp.bfloat16)
+    dkey_ref[...] = jnp.zeros_like(dkey_ref)
+    dvalue_ref[...] = jnp.zeros_like(dvalue_ref)
+    found = []
+    for which in range(q_ref.shape[0] // head):
+        rows = slice(which * head, (which + 1) * head)
+        query = qr_ref[rows, :].astype(jnp.bfloat16)
+        grad = do_ref[rows, :].astype(jnp.bfloat16)
+        delta = jnp.sum(grad.astype(jnp.float32) * o_ref[rows, :], 0, keepdims=True)
+        pieces = []
+        for first in range(0, size, block):
+            here = slice(first, first + block)
+            dquery = jnp.zeros((head, block), jnp.float32)
+            for key in range(0, first + block, block):
+                there = slice(key, key + block)
+                scores = jnp.dot(keys[there], query[:, here], preferred_element_type=jnp.float32)
+                probs = jnp.exp(
+                    scores * scale + (bias_ref[there, here] - log_ref[0, which : which + 1, here])
+                )
+                dprobs = jnp.dot(values[there], grad[:, here], preferred_element_type=jnp.float32)
+                dscores = (probs * (dprobs - delta[:, here])).astype(jnp.bfloat16)
+                dquery += jnp.dot(keys_t[:, there], dscores, preferred_element_type=jnp.float32)
+                dkey_ref[:, there] += nt(query[:, here], dscores)
+                dvalue_ref[:, there] += nt(grad[:, here], probs.astype(jnp.bfloat16))
+            pieces.append(dquery * scale)
+        dquery, terms = turned_back(
+            jnp.concatenate(pieces, 1), q_ref[rows, :], gain_ref[0], cosine, sine
+        )
+        found.append(dquery)
+        gains_ref[0] += terms
+    dq_ref[...] = jnp.concatenate(found, 0).T
+    dkey, terms = turned_back(dkey_ref[...] * scale, kv_ref[:head, :], gain_ref[1], cosine, sine)
+    dkv_ref[...] = jnp.concatenate([dkey, dvalue_ref[...]], 0).T
+    gains_ref[1] += terms
+
+
+def whole_spec(*shape):
+    return pl.BlockSpec(shape, lambda i: (0,) * len(shape))
+
+
+def attend(raw, cosine, sine, gains, segments, kv_own, head, block):
+    size = raw.shape[1]
+    group = raw.shape[0] // head // kv_own - 2
+    query = pl.BlockSpec((group * head, size), lambda i: (i, 0))
+    kv_at = group * kv_own // 2
+    return pl.pallas_call(
+        functools.partial(forward_kernel, block),
+        grid=(kv_own,),
+        in_specs=[
+            query,
+            pl.BlockSpec((2 * head, size), lambda i: (kv_at + i, 0)),
+            whole_spec(head // 2, size),
+            whole_spec(head // 2, size),
+            whole_spec(2, head, 1),
+            whole_spec(1, size),
+            whole_spec(size, 1),
+        ],
+        out_specs=[
+            query,
+            pl.BlockSpec((1, group, size), lambda i: (i, 0, 0)),
+            query,
+            pl.BlockSpec((2 * head, size), lambda i: (i, 0)),
+        ],
+        out_shape=[
+            jax.ShapeDtypeStruct((kv_own * group * head, size), jnp.float32),
+            jax.ShapeDtypeStruct((kv_own, group, size), jnp.float32),
+            jax.ShapeDtypeStruct((kv_own * group * head, size), jnp.float32),
+            jax.ShapeDtypeStruct((kv_own * 2 * head, size), jnp.float32),
+        ],
+        scratch_shapes=[pltpu.VMEM((size, size), jnp.float32)],
+        compiler_params=pltpu.CompilerParams(vmem_limit_bytes=40 * 2**20),
+        cost_estimate=pl.CostEstimate(
+            flops=16 * kv_own * group * size * size * head,
+            bytes_accessed=12 * raw.size,
+            transcendentals=kv_own * group * size * size,
+        ),
+    )(raw, raw, cosine, sine, gains, segments[None, :], segments[:, None])
+
+
+def attend_back(
+    raw, turned_q, turned_kv, grad, attended, logs, cosine, sine, gains, segments,
+    kv_own, head, block, begin, count
+):
+    size = raw.shape[1]
+    group = raw.shape[0] // head // kv_own - 2
+    query = pl.BlockSpec((group * head, size), lambda i: (begin + i, 0))
+    kv_at = group * kv_own // 2 + begin
+    return pl.pallas_call(
+        functools.partial(backward_kernel, block),
+        grid=(count,),
+        in_specs=[
+            query,
+            pl.BlockSpec((2 * head, size), lambda i: (kv_at + i, 0)),
+            query,
+            pl.BlockSpec((2 * head, size), lambda i: (begin + i, 0)),
+            query,
+            query,
+            pl.BlockSpec((1, group, size), lambda i: (begin + i, 0, 0)),
+            whole_spec(head // 2, size),
+            whole_spec(head // 2, size),
+            whole_spec(2, head, 1),
+            whole_spec(1, size),
+            whole_spec(size, 1),
+        ],
+        out_specs=[
+            pl.BlockSpec((size, group * head), lambda i: (0, i)),
+            pl.BlockSpec((size, 2 * head), lambda i: (0, i)),
+            whole_spec(2, head, 1),
+        ],
+        out_shape=[
+            jax.ShapeDtypeStruct((size, count * group * head), jnp.float32),
+            jax.ShapeDtypeStruct((size, count * 2 * head), jnp.float32),
+            jax.ShapeDtypeStruct((2, head, 1), jnp.float32),
+        ],
+        scratch_shapes=[
+            pltpu.VMEM((size, size), jnp.float32),
+            pltpu.VMEM((head, size), jnp.float32),
+            pltpu.VMEM((head, size), jnp.float32),
+        ],
+        compiler_params=pltpu.CompilerParams(vmem_limit_bytes=40 * 2**20),
+        cost_estimate=pl.CostEstimate(
+            flops=40 * count * group * size * size * head,
+            bytes_accessed=4 * raw.size * count,
+            transcendentals=count * group * size * size,
+        ),
+    )(
+        raw, raw, turned_q, turned_kv, grad, attended, logs, cosine, sine, gains,
+        segments[None, :], segments[:, None]
+    )
+
+
+def on_device_fast(
+    hidden_in,
+    out_grad,
+    segment_ids,
+    doc_positions,
+    attn_gain,
+    head_gains,
+    w_query,
+    w_key,
+    w_value,
+    w_out,
+    ffn_gain,
+    w_gate,
+    w_up,
+    w_down,
+):
+    low, full = jnp.bfloat16, jnp.float32
+    dp, ctx = lax.axis_index("dp"), lax.axis_index("ctx")
+    ctx_count = lax.axis_size("ctx")
+    core, side, high = dp % 2, dp // 2 % 2, dp // 4
+    width = hidden_in.shape[-1]
+    rows = w_query.shape[0]
+    head = head_gains.shape[0] * lax.axis_size("dp") * ctx_count // 2
+    group = w_query.shape[1] // w_key.shape[1]
+    kv_own = w_key.shape[1] // head // 2
+    units = w_down.shape[0] * ctx_count
+
+    x_half = spread(hidden_in[:, 0]).reshape(-1, width)
+    marks = spread(jnp.stack([segment_ids[:, 0], doc_positions[:, 0]], 1))
+    marks = swap_gather(marks, core, CORE).reshape(-1, 2, marks.shape[-1])
+    segments, places = marks[:, 0].reshape(-1), marks[:, 1].reshape(-1)
+    x_all = swap_gather(x_half, core, CORE).reshape(-1, width)
+
+    def of_member(which):
+        return jnp.concatenate(
+            [
+                w[:, (top * 4 + which) * units : (top * 4 + which + 1) * units]
+                for w in (w_gate, w_up)
+                for top in range(w_gate.shape[1] // units // 4)
+            ],
+            1,
+        )
+
+    def related(zero, one, two, three):
+        near, far = choose(side, zero, two), choose(side, two, zero)
+        near_far, far_far = choose(side, one, three), choose(side, three, one)
+        return (
+            choose(core, near, near_far),
+            choose(core, far, far_far),
+            choose(core, near_far, near),
+            choose(core, far_far, far),
+        )
+
+    members = related(*[of_member(which) for which in range(4)])
+    block_ffn = jnp.zeros((2, 2) + members[0].shape, low)
+    block_ffn = put(block_ffn, members[0], side, core)
+    block_ffn = put(block_ffn, flip(members[1], SIDE), 1 - side, core)
+    block_ffn = put(block_ffn, flip(members[2], CORE), side, 1 - core)
+    block_ffn = put(block_ffn, flip(members[3], SIDE | CORE), 1 - side, 1 - core)
+    block_ffn = block_ffn.reshape(4, rows, -1)
+
+    head_few = head_gains.shape[0]
+    gains = jnp.stack([attn_gain, ffn_gain, jnp.pad(head_gains, (0, rows - head_few))])
+    gains = jnp.pad(gains, ((0, rows - 3), (0, 128 - rows)))
+    key_value = jnp.stack([w_key.reshape(rows, -1, 2, head), w_value.reshape(rows, -1, 2, head)], 3)
+    parities = [
+        jnp.concatenate(
+            [
+                w_query.reshape(rows, -1, 2, group * head)[:, :, which].reshape(rows, -1),
+                key_value[:, :, which].reshape(rows, -1),
+                gains,
+            ],
+            1,
+        )
+        for which in range(2)
+    ]
+    inner = parities[0].shape[1]
+    got = flip(choose(core, parities[1], parities[0]), CORE)
+    block = joined(
+        choose(core, parities[0], got),
+        choose(core, got, parities[1]),
+        jnp.pad(w_out, ((0, 0), (0, inner - width))),
+    )
+    buffer = jnp.zeros((2, 2, 3, ctx_count, rows, inner), low)
+    for step in range(ctx_count):
+        following = spin(block) if step < ctx_count - 1 else None
+        from_side, from_high = flip(block, SIDE), flip(block, HIGH)
+        from_both = flip(from_side, HIGH) if step % 2 == 0 else flip(from_high, SIDE)
+        place = (ctx - step) % ctx_count
+        for up, across, piece in (
+            (high, side, block),
+            (high, 1 - side, from_side),
+            (1 - high, side, from_high),
+            (1 - high, 1 - side, from_both),
+        ):
+            buffer = put(buffer, piece[:, None], up, across, 0, place)
+        last_attn = block
+        block = following
+    w_in = buffer[:, :, :2].reshape(-1, inner)
+    w_mine = buffer[:, :, 2].reshape(-1, inner)[:, :width]
+    w_theirs = flip(w_mine, CORE)
+
+    features = inner - 128
+    gains_all = w_in[:, features:].reshape(-1, rows, 128)[:, :3, :rows].astype(full)
+    attn_gain_all, ffn_gain_all = gains_all[:, 0].reshape(-1), gains_all[:, 1].reshape(-1)
+    head_gains_all = gains_all[:, 2, :head_few].reshape(2, head, 1)
+    w_in = w_in[:, :features]
+
+    ffn_blocks, ffn_far = [after(block_ffn, x_half, last_attn)], []
+
+    def ffn_step(*ready):
+        block = ffn_blocks[-1]
+        if ready:
+            block = after(block, *ready)
+            ffn_blocks[-1] = block
+        if len(ffn_blocks) < ctx_count:
+            ffn_blocks.append(spin(block))
+        ffn_far.append(flip(block, HIGH))
+
+    x = x_all.astype(full)
+    normed, _, _ = norm_forward(x, attn_gain_all)
+    a_low = normed.astype(low)
+    ffn_step()
+    raw = lax.dot_general(w_in, a_low, (((0,), (1,)), ((), ())), preferred_element_type=full)
+    ffn_step(a_low)
+    freq = THETA ** (-(jnp.arange(head // 2, dtype=full) * 2.0 / head))
+    turn = freq[:, None] * places.astype(full)[None, :]
+    cosine, sine = jnp.cos(turn), jnp.sin(turn)
+    attended, logs, turned_q, turned_kv = attend(
+        raw, cosine, sine, head_gains_all, segments, kv_own, head, 256
+    )
+    ffn_step(attended)
+    attended_low = attended.astype(low)
+    o_theirs = flip(half_of(1 - core, attended_low, 1), CORE)
+    hidden = (
+        x_half.astype(full)
+        + left_trans(half_of(core, attended_low, 1), w_mine)
+        + left_trans(o_theirs, w_theirs)
+    )
+    normed_two, h_unit, h_factor = norm_forward(hidden, ffn_gain_all)
+    b_own = swap_halves(high, normed_two.astype(low), 1)
+    b_side, b_core = flip(b_own, SIDE), flip(b_own, CORE)
+    ffn_step(b_own)
+    w_ffn = jnp.zeros((2, 4, ctx_count) + block_ffn.shape[1:], low)
+    for step in range(ctx_count):
+        place = (ctx - step) % ctx_count
+        w_ffn = put(w_ffn, ffn_blocks[step][:, None], 0, 0, place)
+        w_ffn = put(w_ffn, ffn_far[step][:, None], 1, 0, place)
+    w_ffn = w_ffn.reshape(width, -1)
+    df = spread(after(out_grad[:, 0], b_own)).reshape(-1, width)
+    down_blocks, down_far = [after(w_down, ffn_blocks[-1])], []
+
+    def down_step(*ready):
+        block = down_blocks[-1]
+        if ready:
+            block = after(block, *ready)
+            down_blocks[-1] = block
+        if len(down_blocks) < ctx_count:
+            down_blocks.append(spin(block))
+        down_far.append(flip(block, HIGH))
+
+    down_step()
+    b_both = flip(b_side, CORE)
+    team_b = joined(b_own, b_side, b_core, b_both).reshape(-1, width)
+    down_step(b_both)
+    down_step(b_both)
+    pre = matmul(team_b, w_ffn)
+    down_step(pre)
+    w_down_all = jnp.zeros((2, ctx_count) + w_down.shape, low)
+    for step in range(ctx_count):
+        place = (ctx - step) % ctx_count
+        w_down_all = put(w_down_all, down_blocks[step], high, place)
+        w_down_all = put(w_down_all, down_far[step], 1 - high, place)
+    w_down_all = w_down_all.reshape(-1, width)
+    team_df = team_gather(df)
+
+    mid = pre.shape[1] // 2
+    gate, upper = pre[:, :mid], pre[:, mid:]
+    sigma = jax.nn.sigmoid(gate)
+    act = (gate * sigma * upper).astype(low)
+    d_act = right_trans(team_df, w_down_all)
+    d_upper = (d_act * gate * sigma).astype(low)
+    d_gate = (d_act * upper * sigma * (1.0 + gate * (1.0 - sigma))).astype(low)
+    d_pre = jnp.concatenate([d_gate, d_upper], 1)
+    partial_db = right_trans(d_pre, w_ffn)
+    db = team_reduce(partial_db.reshape(4, -1, width))
+    db = swap_halves(high, db, 1)
+
+    def behind(step):
+        return (ctx - 1 - step) % ctx_count
+
+    g_ffn = left_trans(after(team_b, partial_db), d_pre).astype(low)
+    g_ffn = g_ffn.reshape(2, 4, ctx_count, rows, -1)
+    ffn_got = [flip(pick(g_ffn[1], behind(step), 1), HIGH) for step in range(ctx_count)]
+    g_down = left_trans(after(act, g_ffn), team_df).astype(low)
+    g_down = g_down.reshape(2, ctx_count, -1, width)
+    g_down_near, g_down_far = pick(g_down, high), pick(g_down, 1 - high)
+    down_got = [flip(pick(g_down_far, behind(step)), HIGH) for step in range(ctx_count)]
+    partial_out = matmul(after(act, g_down), w_down_all)
+
+    def ffn_term(step):
+        return total_low(pick(g_ffn[0], behind(step), 1), ffn_got[step])
+
+    def down_term(step):
+        return total_low(pick(g_down_near, behind(step)), down_got[step])
+
+    ffn_ring = spin(after(ffn_term(0), partial_out))
+    down_ring = spin(after(down_term(0), partial_out))
+    d_hidden, ffn_terms = norm_backward(db, h_unit, h_factor, ffn_gain_all)
+    d_hidden = df.astype(full) + d_hidden
+    dz = d_hidden.astype(low)
+    dz_all = swap_gather(dz, core, CORE).reshape(-1, width)
+    ffn_ring = spin(total_low(after(ffn_ring, dz), ffn_term(1)))
+    down_ring = spin(total_low(after(down_ring, dz), down_term(1)))
+    d_attended = right_trans(w_mine, dz_all)
+    g_out = matmul(attended_low, dz_all).astype(low).reshape(2, 2, ctx_count, -1, width)
+    back = functools.partial(
+        attend_back, raw, turned_q, turned_kv, d_attended, attended, logs, cosine, sine,
+        head_gains_all, segments, kv_own, head, 256
+    )
+    dq_one, dkv_one, g_heads_one = back(0, kv_own // 2)
+    ffn_ring = spin(total_low(after(ffn_ring, dq_one), ffn_term(2)))
+    down_ring = spin(total_low(after(down_ring, dq_one), down_term(2)))
+    block_out = hidden + team_reduce(partial_out.reshape(4, -1, width))
+    block_out = unspread(after(block_out, dq_one).astype(low).reshape(2, -1, width))
+
+    def squares(array, step):
+        part = pick(array, behind(step), 2)
+        mine, other = pick(part, high), pick(part, 1 - high)
+        if step % 2 == 0:
+            got = flip(other, HIGH)
+            mine_near, mine_far = pick(mine, side), pick(mine, 1 - side)
+            got_near, got_far = pick(got, side), pick(got, 1 - side)
+            from_side = flip(total_low(mine_far, got_far), SIDE)
+            return total_low(total_low(mine_near, got_near), from_side)
+        near, far = pick(part, side, 1), pick(part, 1 - side, 1)
+        got = flip(far, SIDE)
+        from_high = flip(total_low(pick(near, 1 - high), pick(got, 1 - high)), HIGH)
+        return total_low(total_low(pick(near, high), pick(got, high)), from_high)
+
+    out_terms = [squares(after(g_out, dq_one), step) for step in range(ctx_count)]
+    out_ring = spin(out_terms[0])
+    dq_two, dkv_two, g_heads_two = back(kv_own // 2, kv_own - kv_own // 2)
+    d_raw = jnp.concatenate([dq_one, dq_two, dkv_one, dkv_two], 1).astype(low)
+    g_heads = g_heads_one + g_heads_two
+    g_in = left_trans(a_low, d_raw).astype(low)
+    d_theirs = right_trans(half_of(1 - core, d_raw, 0), w_in)
+    d_from = flip(d_theirs.astype(low), CORE)
+    d_inner = right_trans(half_of(core, d_raw, 0), w_in) + d_from.astype(full)
+    _, x_unit, x_factor = norm_forward(x_half.astype(full), attn_gain_all)
+    d_input, attn_terms = norm_backward(d_inner, x_unit, x_factor, attn_gain_all)
+    in_grad = unspread((d_hidden + d_input).astype(low).reshape(2, -1, width))
+    out_ring = spin(total_low(after(out_ring, dq_two), out_terms[1]))
+    ffn_total = total_low(after(ffn_ring, dq_two), ffn_term(3)).reshape(2, 2, rows, -1)
+    g_down = total_low(after(down_ring, dq_two), down_term(3))
+
+    own_heads = jnp.pad(g_heads.reshape(-1, head_few), ((0, 0), (0, rows - head_few)))
+    g_gains = jnp.stack(
+        [
+            jnp.sum(attn_terms, 0).reshape(-1, rows),
+            jnp.sum(ffn_terms, 0).reshape(-1, rows),
+            own_heads,
+        ],
+        1,
+    )
+    g_gains = jnp.pad(g_gains, ((0, 0), (0, rows - 3), (0, 128 - rows))).reshape(-1, 128)
+    g_in = jnp.concatenate([g_in, g_gains.astype(low)], 1)
+    g_in = jnp.moveaxis(g_in.reshape(2, 2, 2, ctx_count, rows, inner), 3, 2)
+    in_terms = [squares(g_in, step) for step in range(ctx_count)]
+    in_ring = spin(in_terms[0])
+    out_ring = spin(total_low(out_ring, out_terms[2]))
+    in_ring = spin(total_low(in_ring, in_terms[1]))
+    g_out = total_low(out_ring, out_terms[3])
+    in_ring = spin(total_low(in_ring, in_terms[2]))
+
+    ffn_total = after(ffn_total, in_terms[3])
+    found = related(
+        pick(pick(ffn_total, side), core),
+        flip(pick(pick(ffn_total, side), 1 - core), CORE),
+        flip(pick(pick(ffn_total, 1 - side), core), SIDE),
+        flip(pick(pick(ffn_total, 1 - side), 1 - core), SIDE | CORE),
+    )
+    found = (found[0], found[2], found[1], found[3])
+    blocks = w_gate.shape[1] // units // 4
+
+    def to_columns(first):
+        return jnp.concatenate(
+            [
+                found[which][:, (first + top) * units : (first + top + 1) * units].astype(full)
+                for top in range(blocks)
+                for which in range(4)
+            ],
+            1,
+        )
+
+    g_gate, g_up = to_columns(0), to_columns(blocks)
+
+    g_in = total_low(in_ring, in_terms[3])
+    own = pick(g_in, core).astype(full)
+    got = flip(pick(g_in, 1 - core), CORE).astype(full)
+    even, odd = choose(core, own, got), choose(core, got, own)
+    first = group * head * kv_own
+
+    def mixed(start, stop, step, size):
+        return jnp.concatenate(
+            [part[:, at : at + size] for at in range(start, stop, step) for part in (even, odd)], 1
+        )
+
+    g_gains = (own + got)[:, features:]
+
+    return (
+        block_out[:, None],
+        in_grad[:, None],
+        g_gains[0, :rows],
+        g_gains[2, :head_few],
+        mixed(0, first, group * head, group * head),
+        mixed(first, features, 2 * head, head),
+        mixed(first + head, features, 2 * head, head),
+        g_out.astype(full),
+        g_gains[1, :rows],
+        g_gate,
+        g_up,
+        g_down.astype(full),
+    )
+
+
 def solution(mesh):
     placed = (
         P(None, "dp", "ctx", None),
@@ -368,8 +1038,9 @@
         P(("dp", "ctx"), None),
         P(("dp", "ctx"), None),
     )
+    fits = mesh.shape["dp"] == 8 and mesh.shape["ctx"] == 4
     return jax.shard_map(
-        on_device,
+        on_device_fast if fits else on_device,
         mesh=mesh,
         in_specs=placed,
         out_specs=(

time: 2030 us -> 582 us (0.29)
  waiting for transfers between devices: 1580 us -> 193 us
  matrix products: 275 us -> 96.6 us
  starting transfers between devices: 1.27 us -> 120 us
  blocking collectives: 93.8 us -> 0 us
  local copies, waits for them, and re-layouts: 32.7 us -> 77.7 us
  Pallas kernels: 0 us -> 35.3 us
    reduce_scatter x11 -> x0, waiting for transfers between devices: 1120 us -> none  [the longest x7 1050 us: on_device(): lax.psum_scatter(totals, ('dp', 'ctx'), scatter_dimension=0, tiled=True)]
    all_gather x11 -> x0, waiting for transfers between devices: 457 us -> none  [the longest x1 74.8 us: fetch_weights(): lax.all_gather(shards[9], ('dp', 'ctx'), axis=0, tiled=True)]
    ppermute x0 -> x99, waiting for transfers between devices: none -> 193 us  [the longest x68 112 us: flip(): return lax.ppermute(array, 'dp', [(i, i ^ bits) for i in range(count)])]
    ppermute x0 -> x99, starting transfers between devices: none -> 120 us  [the longest x68 55.5 us: flip(): return lax.ppermute(array, 'dp', [(i, i ^ bits) for i in range(count)])]
    unnamed x2 -> x0, blocking collectives: 79.8 us -> none
    dot_general x12 -> x1, matrix products: 70.5 us -> 2.38 us  [on_device_fast(): lax.dot_general(w_in, a_low, (((0,), (1,)), ((), ())), preferred_element_...]
    dot_general x14 -> x5, matrix products: 85.8 us -> 29.5 us  [left_trans(): lax.dot_general(left, right, (((0,), (0,)), ((), ())), preferred_element_...]
    dot_general x14 -> x3, matrix products: 60.2 us -> 22.5 us  [matmul(): return jnp.dot(left, right, preferred_element_type=jnp.float32)]
  transfers between devices with their start and end apart: 22 -> 99, of which waited for: 20 -> 30; matrix products, arithmetic and copies ran while one was open for 12% -> 27% of each run, Pallas kernels for 0% -> 6%
where the time goes in v1:
time: 582 us; the launch traced here: 575 us
  waiting for transfers between devices  193 us (33%)
  starting transfers between devices  120 us (21%)
  matrix products  96.6 us (17%)
  local copies, waits for them, and re-layouts  77.7 us (13%)
  other arithmetic  49.3 us (8%)
  Pallas kernels  35.3 us (6%)
    ppermute x68, waiting for transfers between devices, flip(): return lax.ppermute(array, 'dp', [(i, i ^ bits) for i in range(count)])  112 us
    ppermute x68, starting transfers between devices, flip(): return lax.ppermute(array, 'dp', [(i, i ^ bits) for i in range(count)])  55.5 us
    ppermute x21, waiting for transfers between devices, spin(): lax.ppermute(array, 'ctx', [(i, (i + 1) % count) for i in range(count)])  51.4 us
    ppermute x10, starting transfers between devices, exchange(): got = lax.ppermute(piece, ('dp', 'ctx'), pairs)  42.9 us
    dot_general x5, matrix products, right_trans(): lax.dot_general(left, right, (((1,), (1,)), ((), ())), preferred_element_...  42.2 us
    dynamic_update_slice x56, local copies, waits for them, and re-layouts, put(): return lax.dynamic_update_slice(buffer, array.reshape(shape), index)  29.9 us
    dot_general x5, matrix products, left_trans(): lax.dot_general(left, right, (((0,), (0,)), ((), ())), preferred_element_...  29.5 us
    ppermute x10, waiting for transfers between devices, exchange(): got = lax.ppermute(piece, ('dp', 'ctx'), pairs)  29.2 us
  transfers between devices with their start and end apart: 99, of which 30 were waited for; matrix products, arithmetic and copies ran while one was open for 27% of the time, Pallas kernels for 6%

profile of v1, /device:TPU:1, one launch (start us, length us, event | category | flops | bytes accessed | tf_op | source)
XLA Modules:
  0.0 575.2 jit_solution(9849598101881061806)
XLA Ops:
  5.5 2.1 collective-permute-start.27
  8.7 3.7 collective-permute-start
  13.1 3.5 collective-permute-start.19
  22.3 3.1 collective-permute-done.19
  25.4 3.7 collective-permute-start.20
  32.9 3.5 collective-permute-start.1
  45.1 7.9 %collective-permute-done.6 = bf16[3,32,1152]{2,1,0:T(8,128)(2,1)S(1)} collective-permute-done((bf16[3,32,1152]{2,1,0:T(8,128)(2,1)S(1)}, bf16[3,32,1152]{2,1,0:T(8,128)(2,1)S(1)}, u32[]{:S(2)}, u32[]{:S(2)}) %collective-permute-start.6) | collective-permute-done | bytes 221216 | tf_op jit(solution)/shard_map/ppermute | solution.py:368
  56.5 4.4 collective-permute-done.10
  63.8 2.3 collective-permute-done.8
  69.4 3.3 collective-permute-start.18
  79.2 17.6 %collective-permute-done.13 = bf16[3,32,1152]{2,1,0:T(8,128)(2,1)S(1)} collective-permute-done((bf16[3,32,1152]{2,1,0:T(8,128)(2,1)S(1)}, bf16[3,32,1152]{2,1,0:T(8,128)(2,1)S(1)}, u32[]{:S(2)}, u32[]{:S(2)}) %collective-permute-start.13) | collective-permute-done | bytes 221216 | tf_op jit(solution)/shard_map/ppermute | solution.py:363
  97.1 5.5 collective-permute-done.16
  103.0 4.5 collective-permute-done.17
  110.5 3.2 collective-permute-start.23
  115.7 2.3 bitcast_dynamic-update-slice_fusion.8
  118.1 2.2 multiply_reduce_fusion
  122.0 2.4 fusion.28.q_ref.kv_ref
  125.3 9.7 %shard_map.229 = (f32[512,1024]{1,0:T(8,128)S(1)}, f32[4,2,1024]{2,1,0:T(2,128)S(1)}, f32[512,1024]{1,0:T(8,128)S(1)}, f32[512,1024]{1,0:T(8,128)S(1)}) custom-call(f32[1024,1024]{1,0:T(8,128)S(1)} %fusion.28.q_ref.kv_ref, f32[1024,1024]{1,0:T(8,128)S(1)} %fusion.28.q_ref.kv_ref, f32[32,1024]{1,0:T(8,128)S(1)} %get-tuple-element.216.cos_ref, ...), custom_call_target="tpu_custom_call" | custom-call | flops 8589934592 | bytes 12582912 | tf_op jit(solution)/shard_map/pallas_call | solution.py:612
  138.8 2.7 collective-permute-done.33
  148.6 3.1 collective-permute-start.37
  152.2 5.4 collective-permute-done.35
  158.9 22.2 %collective-permute-done.37 = bf16[256,1024]{1,0:T(8,128)(2,1)S(1)} collective-permute-done((bf16[256,1024]{1,0:T(8,128)(2,1)S(1)}, bf16[256,1024]{1,0:T(8,128)(2,1)S(1)}, u32[]{:S(2)}, u32[]{:S(2)}) %collective-permute-start.37) | collective-permute-done | bytes 524320 | tf_op jit(solution)/shard_map/ppermute | solution.py:422
  182.4 2.5 dynamic_update_slice.238
  189.7 21.2 %collective-permute-done.39 = bf16[512,1024]{1,0:T(8,128)(2,1)S(1)} collective-permute-done((bf16[512,1024]{1,0:T(8,128)(2,1)S(1)}, bf16[512,1024]{1,0:T(8,128)(2,1)S(1)}, u32[]{:S(2)}, u32[]{:S(2)}) %collective-permute-start.39) | collective-permute-done | bytes 1048608 | tf_op jit(solution)/shard_map/ppermute | solution.py:363
  213.0 5.6 collective-permute-start.45
  218.7 13.1 %fusion.112 = f32[2048,2304]{1,0:T(8,128)} fusion(bf16[2048,1024]{1,0:T(8,128)(2,1)S(1)} %bitcast.576, bf16[1024,2304]{1,0:T(8,128)(2,1)S(1)} %bitcast.571), kind=kOutput, calls=%fused_computation.343 | convolution fusion | flops 9663676416 | bytes 27787264 | tf_op jit(solution)/shard_map/dot_general | solution.py:15
  236.7 5.9 %collective-permute-done.47 = bf16[144,1024]{1,0:T(8,128)(2,1)S(1)} collective-permute-done((bf16[144,1024]{1,0:T(8,128)(2,1)S(1)}, bf16[144,1024]{1,0:T(8,128)(2,1)S(1)}, u32[]{:S(2)}, u32[]{:S(2)}) %collective-permute-start.47) | collective-permute-done | bytes 294944 | tf_op jit(solution)/shard_map/ppermute | solution.py:368
  245.4 4.6 collective-permute-done.48
  250.7 18.5 %multiply_convert_fusion.1 = (bf16[2048,1152]{1,0:T(8,128)(2,1)}, bf16[2048,1152]{1,0:T(8,128)(2,1)}, bf16[2048,1152]{1,0:T(8,128)(2,1)}) fusion(f32[2048,2304]{1,0:T(8,128)} %fusion.112, bf16[2048,1024]{1,0:T(8,128)(2,1)} %bitcast.104, bf16[1152,1024]{1,0:T(8,128)(2,1)} %bitcast.114), kind=kOutput, calls=%fused_computation.2 | convolution fusion | flops 4869586944 | bytes 39583744 | tf_op jit(solution)/shard_map/dot_general | solution.py:25
  269.2 16.0 %fusion.1 = f32[2048,1024]{1,0:T(8,128)} fusion(bf16[1024,2304]{1,0:T(8,128)(2,1)} %bitcast.572, bf16[2048,1152]{1,0:T(8,128)(2,1)} %get-tuple-element.90, bf16[2048,1152]{1,0:T(8,128)(2,1)} %get-tuple-element.89), kind=kOutput, calls=%fused_computation.6 | convolution fusion | flops 9682550784 | bytes 22544384 | tf_op jit(solution)/shard_map/dot_general | solution.py:25
  285.2 3.9 slice.536
  289.1 8.4 %convolution_convert_fusion = bf16[1152,1024]{1,0:T(8,128)(2,1)S(1)} fusion(bf16[2048,1152]{1,0:T(8,128)(2,1)} %get-tuple-element.51, bf16[2048,1024]{1,0:T(8,128)(2,1)} %bitcast.104), kind=kOutput, calls=%fused_computation.14 | convolution fusion | flops 4833017856 | bytes 11272192 | tf_op jit(solution)/shard_map/dot_general | solution.py:19
  299.6 2.6 collective-permute-start.51
  302.4 14.4 %fusion.2 = bf16[1024,2304]{1,0:T(8,128)(2,1)S(1)} fusion(bf16[2048,1024]{1,0:T(8,128)(2,1)S(1)} %bitcast.577, bf16[2048,1152]{1,0:T(8,128)(2,1)} %get-tuple-element.90, bf16[2048,1152]{1,0:T(8,128)(2,1)} %get-tuple-element.89), kind=kOutput, calls=%fused_computation.7 | convolution fusion | flops 9684910080 | bytes 18350080 | tf_op jit(solution)/shard_map/dot_general | solution.py:19
  316.8 8.2 %fusion.113 = f32[2048,1024]{1,0:T(8,128)S(1)} fusion(bf16[2048,1152]{1,0:T(8,128)(2,1)} %get-tuple-element.51, bf16[1152,1024]{1,0:T(8,128)(2,1)} %bitcast.114), kind=kOutput, calls=%fused_computation.344 | convolution fusion | flops 4831838208 | bytes 15466496 | tf_op jit(solution)/shard_map/dot_general | solution.py:15
  332.9 2.2 convert_element_type.685
  335.7 9.7 %collective-permute-done.82 = bf16[4,32,2304]{2,1,0:T(8,128)(2,1)S(1)} collective-permute-done((bf16[4,32,2304]{2,1,0:T(8,128)(2,1)S(1)}, bf16[4,32,2304]{2,1,0:T(8,128)(2,1)S(1)}, u32[]{:S(2)}, u32[]{:S(2)}) %collective-permute-start.82) | collective-permute-done | bytes 589856 | tf_op jit(solution)/shard_map/ppermute | solution.py:363
  348.4 19.9 %collective-permute-done.52 = bf16[512,1024]{1,0:T(8,128)(2,1)S(1)} collective-permute-done((bf16[512,1024]{1,0:T(8,128)(2,1)S(1)}, bf16[512,1024]{1,0:T(8,128)(2,1)S(1)}, u32[]{:S(2)}, u32[]{:S(2)}) %collective-permute-start.52) | collective-permute-done | bytes 1048608 | tf_op jit(solution)/shard_map/ppermute | solution.py:363
  372.1 18.4 %collective-permute-done.50 = bf16[512,1024]{1,0:T(8,128)(2,1)} collective-permute-done((bf16[512,1024]{1,0:T(8,128)(2,1)S(1)}, bf16[512,1024]{1,0:T(8,128)(2,1)}, u32[]{:S(2)}, u32[]{:S(2)}) %collective-permute-start.50) | collective-permute-done | bytes 1048608 | tf_op jit(solution)/shard_map/ppermute | solution.py:363
  390.5 3.5 collective-permute-start.53
  394.0 3.1 fusion.23
  407.1 12.8 %shard_map.230 = (f32[1024,256]{1,0:T(8,128)S(1)}, f32[1024,256]{1,0:T(8,128)S(1)}, f32[2,64,1]{2,1,0:T(8,128)S(1)}) custom-call(f32[1024,1024]{1,0:T(8,128)} %copy-done, f32[1024,1024]{1,0:T(8,128)} %copy-done, f32[512,1024]{1,0:T(8,128)S(1)} %copy-done.2, f32[512,1024]{1,0:T(8,128)S(1)} %copy-done.4, f32[512,1024]{1,0:T(8,128)S(1)} %fusion.92.do_ref, ...), custom_call_target="tpu_custom_call" | custom-call | flops 10737418240 | bytes 8388608 | tf_op jit(solution)/shard_map/pallas_call | solution.py:654
  419.9 12.8 %shard_map.231 = (f32[1024,256]{1,0:T(8,128)S(1)}, f32[1024,256]{1,0:T(8,128)S(1)}, f32[2,64,1]{2,1,0:T(8,128)S(1)}) custom-call(f32[1024,1024]{1,0:T(8,128)} %copy-done, f32[1024,1024]{1,0:T(8,128)} %copy-done, f32[512,1024]{1,0:T(8,128)S(1)} %copy-done.2, f32[512,1024]{1,0:T(8,128)S(1)} %copy-done.4, f32[512,1024]{1,0:T(8,128)S(1)} %fusion.92.do_ref, ...), custom_call_target="tpu_custom_call" | custom-call | flops 10737418240 | bytes 8388608 | tf_op jit(solution)/shard_map/pallas_call | solution.py:654
  438.5 3.7 convolution_convert_fusion.1
  443.2 2.1 add_convert_fusion.1
  445.3 2.3 fusion.32
  450.0 2.8 collective-permute-start.56
  453.5 3.5 collective-permute-start.73
  464.7 5.9 %collective-permute-start.54 = (bf16[256,1024]{1,0:T(8,128)(2,1)}, bf16[256,1024]{1,0:T(8,128)(2,1)S(1)}, u32[]{:S(2)}, u32[]{:S(2)}) collective-permute-start(bf16[256,1024]{1,0:T(8,128)(2,1)} %get-tuple-element.125), channel_id=1, source_target_pairs={{1,4},{2,1},{3,5},{4,2},{5,6},{6,3},{9,12},{10,9},{11,13},{12,10},... | collective-permute-start | bytes 1572872 | tf_op jit(solution)/shard_map/ppermute | solution.py:422
  471.8 2.1 fusion.56
  473.9 4.5 collective-permute-done.79
  478.3 2.3 collective-permute-start.87
  480.7 5.4 collective-permute-start.55
  489.8 4.2 fusion.13
  494.3 3.2 pad_maximum_fusion.5
  497.5 4.5 copy.89
  505.8 2.8 collective-permute-done.55
  515.2 2.7 fusion.12
  518.0 13.0 %collective-permute-start.57 = (bf16[256,1024]{1,0:T(8,128)(2,1)S(1)}, bf16[256,1024]{1,0:T(8,128)(2,1)S(1)}, u32[]{:S(2)}, u32[]{:S(2)}) collective-permute-start(bf16[256,1024]{1,0:T(8,128)(2,1)S(1)} %get-tuple-element.123), channel_id=1, source_target_pairs={{1,4},{2,1},{3,5},{4,2},{5,6},{6,3},{9,12},{10,9},{11,13},{12,10},... | collective-permute-start | bytes 1572872 | tf_op jit(solution)/shard_map/ppermute | solution.py:422
  535.1 6.7 %collective-permute-done.61 = bf16[2,32,1152]{2,1,0:T(8,128)(2,1)S(1)} collective-permute-done((bf16[2,32,1152]{2,1,0:T(8,128)(2,1)S(1)}, bf16[2,32,1152]{2,1,0:T(8,128)(2,1)S(1)}, u32[]{:S(2)}, u32[]{:S(2)}) %collective-permute-start.61) | collective-permute-done | bytes 147488 | tf_op jit(solution)/shard_map/ppermute | solution.py:368
  543.0 2.3 collective-permute-start.64
  545.7 9.0 %collective-permute-done.64 = bf16[2,32,1152]{2,1,0:T(8,128)(2,1)S(1)} collective-permute-done((bf16[2,32,1152]{2,1,0:T(8,128)(2,1)S(1)}, bf16[2,32,1152]{2,1,0:T(8,128)(2,1)S(1)}, u32[]{:S(2)}, u32[]{:S(2)}) %collective-permute-start.64) | collective-permute-done | bytes 147488 | tf_op jit(solution)/shard_map/ppermute | solution.py:368
  557.7 4.7 collective-permute-done.67
  568.7 3.8 collective-permute-done.91
  (514 shorter events, 154.8 us)
Async XLA Ops:
  5.5 32.3 %collective-permute-start.27 = (bf16[32,2304]{1,0:T(8,128)(2,1)}, bf16[32,2304]{1,0:T(8,128)(2,1)}, u32[]{:S(2)}, u32[]{:S(2)}) collective-permute-start(bf16[32,2304]{1,0:T(8,128)(2,1)} %get-tuple-element.141), channel_id=1, source_target_pairs={{0,8},{4,12},{8,0},{12,4},{16,24},{20,28},{24,16},{28,20},{1,9},{5... | collective-permute-start | bytes 442376 | tf_op jit(solution)/shard_map/ppermute | solution.py:363
  7.6 31.9 %collective-permute-start.28 = (bf16[32,2304]{1,0:T(8,128)(2,1)}, bf16[32,2304]{1,0:T(8,128)(2,1)}, u32[]{:S(2)}, u32[]{:S(2)}) collective-permute-start(bf16[32,2304]{1,0:T(8,128)(2,1)} %get-tuple-element.140), channel_id=1, source_target_pairs={{0,4},{4,0},{8,12},{12,8},{16,20},{20,16},{24,28},{28,24},{1,5},{5... | collective-permute-start | bytes 442376 | tf_op jit(solution)/shard_map/ppermute | solution.py:363
  8.5 33.7 %collective-permute-start.29 = (bf16[32,2304]{1,0:T(8,128)(2,1)}, bf16[32,2304]{1,0:T(8,128)(2,1)}, u32[]{:S(2)}, u32[]{:S(2)}) collective-permute-start(bf16[32,2304]{1,0:T(8,128)(2,1)} %get-tuple-element.139), channel_id=1, source_target_pairs={{0,12},{4,8},{8,4},{12,0},{16,28},{20,24},{24,20},{28,16},{1,13},{... | collective-permute-start | bytes 442376 | tf_op jit(solution)/shard_map/ppermute | solution.py:363
  8.7 58.7 %collective-permute-start = (bf16[256,1024]{1,0:T(8,128)(2,1)S(1)}, bf16[256,1024]{1,0:T(8,128)(2,1)S(1)}, u32[]{:S(2)}, u32[]{:S(2)}) collective-permute-start(bf16[256,1024]{1,0:T(8,128)(2,1)S(1)} %get-tuple-element.131), channel_id=1, source_target_pairs={{1,2},{2,4},{3,6},{4,1},{5,3},{6,5},{9,10},{10,12},{11,14},{12,9},... | collective-permute-start | bytes 1572872 | tf_op jit(solution)/shard_map/ppermute | solution.py:422
  13.1 12.3 %collective-permute-start.19 = (s32[2,256]{1,0:T(2,128)S(1)}, s32[2,256]{1,0:T(2,128)S(1)}, u32[]{:S(2)}, u32[]{:S(2)}) collective-permute-start(s32[2,256]{1,0:T(2,128)S(1)} %get-tuple-element.218), channel_id=1, source_target_pairs={{1,2},{2,4},{3,6},{4,1},{5,3},{6,5},{9,10},{10,12},{11,14},{12,9},... | collective-permute-start | bytes 6152 | tf_op jit(solution)/shard_map/ppermute | solution.py:422
  32.9 36.1 %collective-permute-start.1 = (bf16[256,1024]{1,0:T(8,128)(2,1)S(1)}, bf16[256,1024]{1,0:T(8,128)(2,1)S(1)}, u32[]{:S(2)}, u32[]{:S(2)}) collective-permute-start(bf16[256,1024]{1,0:T(8,128)(2,1)S(1)} %get-tuple-element.130), channel_id=1, source_target_pairs={{0,2},{1,0},{2,6},{3,4},{4,3},{5,1},{6,7},{7,5},{8,10},{9,8},{10,1... | collective-permute-start | bytes 1572872 | tf_op jit(solution)/shard_map/ppermute | solution.py:422
  37.8 15.2 %collective-permute-start.6 = (bf16[3,32,1152]{2,1,0:T(8,128)(2,1)S(1)}, bf16[3,32,1152]{2,1,0:T(8,128)(2,1)S(1)}, u32[]{:S(2)}, u32[]{:S(2)}) collective-permute-start(bf16[3,32,1152]{2,1,0:T(8,128)(2,1)S(1)} %bitcast_dynamic-update-slice_fusion.53), channel_id=1, source_target_pairs={{0,1},{1,2},{2,3},{3,0},{4,5},{5,6},{6,7},{7,4},{8,9},{9,10},{10,1... | collective-permute-start | bytes 663560 | tf_op jit(solution)/shard_map/ppermute | solution.py:368
  39.5 14.4 %collective-permute-start.3 = (bf16[3,32,1152]{2,1,0:T(8,128)(2,1)S(1)}, bf16[3,32,1152]{2,1,0:T(8,128)(2,1)S(1)}, u32[]{:S(2)}, u32[]{:S(2)}) collective-permute-start(bf16[3,32,1152]{2,1,0:T(8,128)(2,1)S(1)} %bitcast_dynamic-update-slice_fusion.53), channel_id=1, source_target_pairs={{0,8},{4,12},{8,0},{12,4},{16,24},{20,28},{24,16},{28,20},{1,9},{5... | collective-permute-start | bytes 663560 | tf_op jit(solution)/shard_map/ppermute | solution.py:363
  42.3 12.9 %collective-permute-start.4 = (bf16[3,32,1152]{2,1,0:T(8,128)(2,1)S(1)}, bf16[3,32,1152]{2,1,0:T(8,128)(2,1)S(1)}, u32[]{:S(2)}, u32[]{:S(2)}) collective-permute-start(bf16[3,32,1152]{2,1,0:T(8,128)(2,1)S(1)} %bitcast_dynamic-update-slice_fusion.53), channel_id=1, source_target_pairs={{0,16},{4,20},{8,24},{12,28},{16,0},{20,4},{24,8},{28,12},{1,17},{... | collective-permute-start | bytes 663560 | tf_op jit(solution)/shard_map/ppermute | solution.py:363
  62.1 11.5 %collective-permute-start.14 = (bf16[3,32,1152]{2,1,0:T(8,128)(2,1)S(1)}, bf16[3,32,1152]{2,1,0:T(8,128)(2,1)S(1)}, u32[]{:S(2)}, u32[]{:S(2)}) collective-permute-start(bf16[3,32,1152]{2,1,0:T(8,128)(2,1)S(1)} %collective-permute-done.10), channel_id=1, source_target_pairs={{0,1},{1,2},{2,3},{3,0},{4,5},{5,6},{6,7},{7,4},{8,9},{9,10},{10,1... | collective-permute-start | bytes 663560 | tf_op jit(solution)/shard_map/ppermute | solution.py:368
  62.5 15.0 %collective-permute-start.11 = (bf16[3,32,1152]{2,1,0:T(8,128)(2,1)S(1)}, bf16[3,32,1152]{2,1,0:T(8,128)(2,1)S(1)}, u32[]{:S(2)}, u32[]{:S(2)}) collective-permute-start(bf16[3,32,1152]{2,1,0:T(8,128)(2,1)S(1)} %collective-permute-done.10), channel_id=1, source_target_pairs={{0,8},{4,12},{8,0},{12,4},{16,24},{20,28},{24,16},{28,20},{1,9},{5... | collective-permute-start | bytes 663560 | tf_op jit(solution)/shard_map/ppermute | solution.py:363
  67.4 11.5 %collective-permute-start.12 = (bf16[3,32,1152]{2,1,0:T(8,128)(2,1)S(1)}, bf16[3,32,1152]{2,1,0:T(8,128)(2,1)S(1)}, u32[]{:S(2)}, u32[]{:S(2)}) collective-permute-start(bf16[3,32,1152]{2,1,0:T(8,128)(2,1)S(1)} %collective-permute-done.10), channel_id=1, source_target_pairs={{0,16},{4,20},{8,24},{12,28},{16,0},{20,4},{24,8},{28,12},{1,17},{... | collective-permute-start | bytes 663560 | tf_op jit(solution)/shard_map/ppermute | solution.py:363
  69.4 46.4 %collective-permute-start.18 = (bf16[512,1024]{1,0:T(8,128)(2,1)S(1)}, bf16[512,1024]{1,0:T(8,128)(2,1)}, u32[]{:S(2)}, u32[]{:S(2)}) collective-permute-start(bf16[512,1024]{1,0:T(8,128)(2,1)S(1)} %bitcast.547), channel_id=1, source_target_pairs={{0,4},{4,0},{8,12},{12,8},{16,20},{20,16},{24,28},{28,24},{1,5},{5... | collective-permute-start | bytes 3145736 | tf_op jit(solution)/shard_map/ppermute | solution.py:363
  75.0 49.3 %collective-permute-start.31 = (bf16[4,32,2304]{2,1,0:T(8,128)(2,1)}, bf16[4,32,2304]{2,1,0:T(8,128)(2,1)}, u32[]{:S(2)}, u32[]{:S(2)}) collective-permute-start(bf16[4,32,2304]{2,1,0:T(8,128)(2,1)} %bitcast.77), channel_id=1, source_target_pairs={{0,1},{1,2},{2,3},{3,0},{4,5},{5,6},{6,7},{7,4},{8,9},{9,10},{10,1... | collective-permute-start | bytes 1769480 | tf_op jit(solution)/shard_map/ppermute | solution.py:368
  77.2 36.6 %collective-permute-start.30 = (bf16[4,32,2304]{2,1,0:T(8,128)(2,1)}, bf16[4,32,2304]{2,1,0:T(8,128)(2,1)}, u32[]{:S(2)}, u32[]{:S(2)}) collective-permute-start(bf16[4,32,2304]{2,1,0:T(8,128)(2,1)} %bitcast.77), channel_id=1, source_target_pairs={{0,16},{4,20},{8,24},{12,28},{16,0},{20,4},{24,8},{28,12},{1,17},{... | collective-permute-start | bytes 1769480 | tf_op jit(solution)/shard_map/ppermute | solution.py:363
  77.5 19.3 %collective-permute-start.13 = (bf16[3,32,1152]{2,1,0:T(8,128)(2,1)S(1)}, bf16[3,32,1152]{2,1,0:T(8,128)(2,1)S(1)}, u32[]{:S(2)}, u32[]{:S(2)}) collective-permute-start(bf16[3,32,1152]{2,1,0:T(8,128)(2,1)S(1)} %collective-permute-done.11), channel_id=1, source_target_pairs={{0,16},{4,20},{8,24},{12,28},{16,0},{20,4},{24,8},{28,12},{1,17},{... | collective-permute-start | bytes 663560 | tf_op jit(solution)/shard_map/ppermute | solution.py:363
  78.9 24.0 %collective-permute-start.15 = (bf16[3,32,1152]{2,1,0:T(8,128)(2,1)S(1)}, bf16[3,32,1152]{2,1,0:T(8,128)(2,1)S(1)}, u32[]{:S(2)}, u32[]{:S(2)}) collective-permute-start(bf16[3,32,1152]{2,1,0:T(8,128)(2,1)S(1)} %collective-permute-done.14), channel_id=1, source_target_pairs={{0,8},{4,12},{8,0},{12,4},{16,24},{20,28},{24,16},{28,20},{1,9},{5... | collective-permute-start | bytes 663560 | tf_op jit(solution)/shard_map/ppermute | solution.py:363
  110.5 32.6 %collective-permute-start.23 = (bf16[512,1024]{1,0:T(8,128)(2,1)}, bf16[512,1024]{1,0:T(8,128)(2,1)}, u32[]{:S(2)}, u32[]{:S(2)}) collective-permute-start(bf16[512,1024]{1,0:T(8,128)(2,1)} %slice.385), channel_id=1, source_target_pairs={{0,4},{4,0},{8,12},{12,8},{16,20},{20,16},{24,28},{28,24},{1,5},{5... | collective-permute-start | bytes 3145736 | tf_op jit(solution)/shard_map/ppermute | solution.py:363
  124.4 17.1 %collective-permute-start.33 = (bf16[4,32,2304]{2,1,0:T(8,128)(2,1)}, bf16[4,32,2304]{2,1,0:T(8,128)(2,1)}, u32[]{:S(2)}, u32[]{:S(2)}) collective-permute-start(bf16[4,32,2304]{2,1,0:T(8,128)(2,1)} %collective-permute-done.31), channel_id=1, source_target_pairs={{0,1},{1,2},{2,3},{3,0},{4,5},{5,6},{6,7},{7,4},{8,9},{9,10},{10,1... | collective-permute-start | bytes 1769480 | tf_op jit(solution)/shard_map/ppermute | solution.py:368
  125.1 16.6 %collective-permute-start.32 = (bf16[4,32,2304]{2,1,0:T(8,128)(2,1)}, bf16[4,32,2304]{2,1,0:T(8,128)(2,1)S(1)}, u32[]{:S(2)}, u32[]{:S(2)}) collective-permute-start(bf16[4,32,2304]{2,1,0:T(8,128)(2,1)} %collective-permute-done.31), channel_id=1, source_target_pairs={{0,16},{4,20},{8,24},{12,28},{16,0},{20,4},{24,8},{28,12},{1,17},{... | collective-permute-start | bytes 1769480 | tf_op jit(solution)/shard_map/ppermute | solution.py:363
  141.5 16.1 %collective-permute-start.35 = (bf16[4,32,2304]{2,1,0:T(8,128)(2,1)}, bf16[4,32,2304]{2,1,0:T(8,128)(2,1)S(1)}, u32[]{:S(2)}, u32[]{:S(2)}) collective-permute-start(bf16[4,32,2304]{2,1,0:T(8,128)(2,1)} %collective-permute-done.33), channel_id=1, source_target_pairs={{0,1},{1,2},{2,3},{3,0},{4,5},{5,6},{6,7},{7,4},{8,9},{9,10},{10,1... | collective-permute-start | bytes 1769480 | tf_op jit(solution)/shard_map/ppermute | solution.py:368
  141.5 17.1 %collective-permute-start.34 = (bf16[4,32,2304]{2,1,0:T(8,128)(2,1)}, bf16[4,32,2304]{2,1,0:T(8,128)(2,1)S(1)}, u32[]{:S(2)}, u32[]{:S(2)}) collective-permute-start(bf16[4,32,2304]{2,1,0:T(8,128)(2,1)} %collective-permute-done.33), channel_id=1, source_target_pairs={{0,16},{4,20},{8,24},{12,28},{16,0},{20,4},{24,8},{28,12},{1,17},{... | collective-permute-start | bytes 1769480 | tf_op jit(solution)/shard_map/ppermute | solution.py:363
  146.8 42.1 %collective-permute-start.24 = (bf16[512,1024]{1,0:T(8,128)(2,1)S(1)}, bf16[512,1024]{1,0:T(8,128)(2,1)S(1)}, u32[]{:S(2)}, u32[]{:S(2)}) collective-permute-start(bf16[512,1024]{1,0:T(8,128)(2,1)S(1)} %maximum_select_fusion.1), channel_id=1, source_target_pairs={{0,8},{4,12},{8,0},{12,4},{16,24},{20,28},{24,16},{28,20},{1,9},{5... | collective-permute-start | bytes 3145736 | tf_op jit(solution)/shard_map/ppermute | solution.py:363
  147.1 41.9 %collective-permute-start.25 = (bf16[512,1024]{1,0:T(8,128)(2,1)S(1)}, bf16[512,1024]{1,0:T(8,128)(2,1)S(1)}, u32[]{:S(2)}, u32[]{:S(2)}) collective-permute-start(bf16[512,1024]{1,0:T(8,128)(2,1)S(1)} %maximum_select_fusion.1), channel_id=1, source_target_pairs={{0,4},{4,0},{8,12},{12,8},{16,20},{20,16},{24,28},{28,24},{1,5},{5... | collective-permute-start | bytes 3145736 | tf_op jit(solution)/shard_map/ppermute | solution.py:363
  148.6 32.5 %collective-permute-start.37 = (bf16[256,1024]{1,0:T(8,128)(2,1)S(1)}, bf16[256,1024]{1,0:T(8,128)(2,1)S(1)}, u32[]{:S(2)}, u32[]{:S(2)}) collective-permute-start(bf16[256,1024]{1,0:T(8,128)(2,1)S(1)} %get-tuple-element.127), channel_id=1, source_target_pairs={{1,2},{2,4},{3,6},{4,1},{5,3},{6,5},{9,10},{10,12},{11,14},{12,9},... | collective-permute-start | bytes 1572872 | tf_op jit(solution)/shard_map/ppermute | solution.py:422
  157.6 24.6 %collective-permute-start.38 = (bf16[256,1024]{1,0:T(8,128)(2,1)S(1)}, bf16[256,1024]{1,0:T(8,128)(2,1)S(1)}, u32[]{:S(2)}, u32[]{:S(2)}) collective-permute-start(bf16[256,1024]{1,0:T(8,128)(2,1)S(1)} %get-tuple-element.126), channel_id=1, source_target_pairs={{0,2},{1,0},{2,6},{3,4},{4,3},{5,1},{6,7},{7,5},{8,10},{9,8},{10,1... | collective-permute-start | bytes 1572872 | tf_op jit(solution)/shard_map/ppermute | solution.py:422
  158.6 31.1 %collective-permute-start.36 = (bf16[4,32,2304]{2,1,0:T(8,128)(2,1)S(1)}, bf16[4,32,2304]{2,1,0:T(8,128)(2,1)S(1)}, u32[]{:S(2)}, u32[]{:S(2)}) collective-permute-start(bf16[4,32,2304]{2,1,0:T(8,128)(2,1)S(1)} %collective-permute-done.35), channel_id=1, source_target_pairs={{0,16},{4,20},{8,24},{12,28},{16,0},{20,4},{24,8},{28,12},{1,17},{... | collective-permute-start | bytes 1769480 | tf_op jit(solution)/shard_map/ppermute | solution.py:363
  181.0 32.0 %collective-permute-start.43 = (bf16[144,1024]{1,0:T(8,128)(2,1)S(1)}, bf16[144,1024]{1,0:T(8,128)(2,1)S(1)}, u32[]{:S(2)}, u32[]{:S(2)}) collective-permute-start(bf16[144,1024]{1,0:T(8,128)(2,1)S(1)} %copy-done.42), channel_id=1, source_target_pairs={{0,1},{1,2},{2,3},{3,0},{4,5},{5,6},{6,7},{7,4},{8,9},{9,10},{10,1... | collective-permute-start | bytes 884744 | tf_op jit(solution)/shard_map/ppermute | solution.py:368
  187.9 23.0 %collective-permute-start.39 = (bf16[512,1024]{1,0:T(8,128)(2,1)S(1)}, bf16[512,1024]{1,0:T(8,128)(2,1)S(1)}, u32[]{:S(2)}, u32[]{:S(2)}) collective-permute-start(bf16[512,1024]{1,0:T(8,128)(2,1)S(1)} %bitcast.550), channel_id=1, source_target_pairs={{0,8},{4,12},{8,0},{12,4},{16,24},{20,28},{24,16},{28,20},{1,9},{5... | collective-permute-start | bytes 3145736 | tf_op jit(solution)/shard_map/ppermute | solution.py:363
  188.9 23.0 %collective-permute-start.40 = (bf16[512,1024]{1,0:T(8,128)(2,1)S(1)}, bf16[512,1024]{1,0:T(8,128)(2,1)S(1)}, u32[]{:S(2)}, u32[]{:S(2)}) collective-permute-start(bf16[512,1024]{1,0:T(8,128)(2,1)S(1)} %bitcast.551), channel_id=1, source_target_pairs={{0,4},{4,0},{8,12},{12,8},{16,20},{20,16},{24,28},{28,24},{1,5},{5... | collective-permute-start | bytes 3145736 | tf_op jit(solution)/shard_map/ppermute | solution.py:363
  189.0 24.0 %collective-permute-start.26 = (bf16[512,1024]{1,0:T(8,128)(2,1)S(1)}, bf16[512,1024]{1,0:T(8,128)(2,1)S(1)}, u32[]{:S(2)}, u32[]{:S(2)}) collective-permute-start(bf16[512,1024]{1,0:T(8,128)(2,1)S(1)} %collective-permute-done.24), channel_id=1, source_target_pairs={{0,4},{4,0},{8,12},{12,8},{16,20},{20,16},{24,28},{28,24},{1,5},{5... | collective-permute-start | bytes 3145736 | tf_op jit(solution)/shard_map/ppermute | solution.py:363
  210.9 24.8 %collective-permute-start.41 = (bf16[512,1024]{1,0:T(8,128)(2,1)S(1)}, bf16[512,1024]{1,0:T(8,128)(2,1)S(1)}, u32[]{:S(2)}, u32[]{:S(2)}) collective-permute-start(bf16[512,1024]{1,0:T(8,128)(2,1)S(1)} %collective-permute-done.39), channel_id=1, source_target_pairs={{0,4},{4,0},{8,12},{12,8},{16,20},{20,16},{24,28},{28,24},{1,5},{5... | collective-permute-start | bytes 3145736 | tf_op jit(solution)/shard_map/ppermute | solution.py:363
  213.0 19.6 %collective-permute-start.45 = (bf16[144,1024]{1,0:T(8,128)(2,1)S(1)}, bf16[144,1024]{1,0:T(8,128)(2,1)S(1)}, u32[]{:S(2)}, u32[]{:S(2)}) collective-permute-start(bf16[144,1024]{1,0:T(8,128)(2,1)S(1)} %collective-permute-done.43), channel_id=1, source_target_pairs={{0,1},{1,2},{2,3},{3,0},{4,5},{5,6},{6,7},{7,4},{8,9},{9,10},{10,1... | collective-permute-start | bytes 884744 | tf_op jit(solution)/shard_map/ppermute | solution.py:368
  218.6 15.5 %collective-permute-start.44 = (bf16[144,1024]{1,0:T(8,128)(2,1)S(1)}, bf16[144,1024]{1,0:T(8,128)(2,1)S(1)}, u32[]{:S(2)}, u32[]{:S(2)}) collective-permute-start(bf16[144,1024]{1,0:T(8,128)(2,1)S(1)} %collective-permute-done.43), channel_id=1, source_target_pairs={{0,16},{4,20},{8,24},{12,28},{16,0},{20,4},{24,8},{28,12},{1,17},{... | collective-permute-start | bytes 884744 | tf_op jit(solution)/shard_map/ppermute | solution.py:363
  298.6 33.3 %collective-permute-start.92 = (bf16[144,1024]{1,0:T(8,128)(2,1)S(1)}, bf16[144,1024]{1,0:T(8,128)(2,1)S(1)}, u32[]{:S(2)}, u32[]{:S(2)}) collective-permute-start(bf16[144,1024]{1,0:T(8,128)(2,1)S(1)} %get-tuple-element.97), channel_id=1, source_target_pairs={{0,16},{4,20},{8,24},{12,28},{16,0},{20,4},{24,8},{28,12},{1,17},{... | collective-permute-start | bytes 884744 | tf_op jit(solution)/shard_map/ppermute | solution.py:363
  299.6 33.4 %collective-permute-start.51 = (bf16[2,512,1024]{2,1,0:T(8,128)(2,1)}, bf16[2,512,1024]{2,1,0:T(8,128)(2,1)}, u32[]{:S(2)}, u32[]{:S(2)}) collective-permute-start(bf16[2,512,1024]{2,1,0:T(8,128)(2,1)} %bitcast.118), channel_id=1, source_target_pairs={{0,4},{4,0},{8,12},{12,8},{16,20},{20,16},{24,28},{28,24},{1,5},{5... | collective-permute-start | bytes 6291464 | tf_op jit(solution)/shard_map/ppermute | solution.py:363
  302.2 96.5 %collective-permute-start.94 = (bf16[144,1024]{1,0:T(8,128)(2,1)}, bf16[144,1024]{1,0:T(8,128)(2,1)}, u32[]{:S(2)}, u32[]{:S(2)}) collective-permute-start(bf16[144,1024]{1,0:T(8,128)(2,1)} %get-tuple-element.96), channel_id=1, source_target_pairs={{0,16},{4,20},{8,24},{12,28},{16,0},{20,4},{24,8},{28,12},{1,17},{... | collective-permute-start | bytes 884744 | tf_op jit(solution)/shard_map/ppermute | solution.py:363
  328.8 17.0 %collective-permute-start.49 = (bf16[2,512,1024]{2,1,0:T(8,128)(2,1)}, bf16[2,512,1024]{2,1,0:T(8,128)(2,1)}, u32[]{:S(2)}, u32[]{:S(2)}) collective-permute-start(bf16[2,512,1024]{2,1,0:T(8,128)(2,1)} %bitcast.115), channel_id=1, source_target_pairs={{0,4},{4,0},{8,12},{12,8},{16,20},{20,16},{24,28},{28,24},{1,5},{5... | collective-permute-start | bytes 6291464 | tf_op jit(solution)/shard_map/ppermute | solution.py:363
  330.7 14.7 %collective-permute-start.82 = (bf16[4,32,2304]{2,1,0:T(8,128)(2,1)S(1)}, bf16[4,32,2304]{2,1,0:T(8,128)(2,1)S(1)}, u32[]{:S(2)}, u32[]{:S(2)}) collective-permute-start(bf16[4,32,2304]{2,1,0:T(8,128)(2,1)S(1)} %get-tuple-element.101), channel_id=1, source_target_pairs={{0,16},{4,20},{8,24},{12,28},{16,0},{20,4},{24,8},{28,12},{1,17},{... | collective-permute-start | bytes 1769480 | tf_op jit(solution)/shard_map/ppermute | solution.py:363
  331.9 69.4 %collective-permute-start.84 = (bf16[4,32,2304]{2,1,0:T(8,128)(2,1)}, bf16[4,32,2304]{2,1,0:T(8,128)(2,1)}, u32[]{:S(2)}, u32[]{:S(2)}) collective-permute-start(bf16[4,32,2304]{2,1,0:T(8,128)(2,1)} %get-tuple-element.100), channel_id=1, source_target_pairs={{0,16},{4,20},{8,24},{12,28},{16,0},{20,4},{24,8},{28,12},{1,17},{... | collective-permute-start | bytes 1769480 | tf_op jit(solution)/shard_map/ppermute | solution.py:363
  332.9 64.2 %collective-permute-start.93 = (bf16[144,1024]{1,0:T(8,128)(2,1)}, bf16[144,1024]{1,0:T(8,128)(2,1)}, u32[]{:S(2)}, u32[]{:S(2)}) collective-permute-start(bf16[144,1024]{1,0:T(8,128)(2,1)} %fusion.50), channel_id=1, source_target_pairs={{0,1},{1,2},{2,3},{3,0},{4,5},{5,6},{6,7},{7,4},{8,9},{9,10},{10,1... | collective-permute-start | bytes 884744 | tf_op jit(solution)/shard_map/ppermute | solution.py:368
  345.3 23.0 %collective-permute-start.52 = (bf16[512,1024]{1,0:T(8,128)(2,1)S(1)}, bf16[512,1024]{1,0:T(8,128)(2,1)S(1)}, u32[]{:S(2)}, u32[]{:S(2)}) collective-permute-start(bf16[512,1024]{1,0:T(8,128)(2,1)S(1)} %fusion.16), channel_id=1, source_target_pairs={{0,8},{4,12},{8,0},{12,4},{16,24},{20,28},{24,16},{28,20},{1,9},{5... | collective-permute-start | bytes 3145736 | tf_op jit(solution)/shard_map/ppermute | solution.py:363
  345.8 52.6 %collective-permute-start.83 = (bf16[4,32,2304]{2,1,0:T(8,128)(2,1)S(1)}, bf16[4,32,2304]{2,1,0:T(8,128)(2,1)}, u32[]{:S(2)}, u32[]{:S(2)}) collective-permute-start(bf16[4,32,2304]{2,1,0:T(8,128)(2,1)S(1)} %fusion.38), channel_id=1, source_target_pairs={{0,1},{1,2},{2,3},{3,0},{4,5},{5,6},{6,7},{7,4},{8,9},{9,10},{10,1... | collective-permute-start | bytes 1769480 | tf_op jit(solution)/shard_map/ppermute | solution.py:368
  368.3 22.1 %collective-permute-start.50 = (bf16[512,1024]{1,0:T(8,128)(2,1)S(1)}, bf16[512,1024]{1,0:T(8,128)(2,1)}, u32[]{:S(2)}, u32[]{:S(2)}) collective-permute-start(bf16[512,1024]{1,0:T(8,128)(2,1)S(1)} %fusion.20), channel_id=1, source_target_pairs={{0,8},{4,12},{8,0},{12,4},{16,24},{20,28},{24,16},{28,20},{1,9},{5... | collective-permute-start | bytes 3145736 | tf_op jit(solution)/shard_map/ppermute | solution.py:363
  390.5 12.6 %collective-permute-start.53 = (bf16[512,1024]{1,0:T(8,128)(2,1)}, bf16[512,1024]{1,0:T(8,128)(2,1)}, u32[]{:S(2)}, u32[]{:S(2)}) collective-permute-start(bf16[512,1024]{1,0:T(8,128)(2,1)} %get-tuple-element.222), channel_id=1, source_target_pairs={{0,4},{4,0},{8,12},{12,8},{16,20},{20,16},{24,28},{28,24},{1,5},{5... | collective-permute-start | bytes 3145736 | tf_op jit(solution)/shard_map/ppermute | solution.py:363
  397.1 35.7 %collective-permute-start.96 = (bf16[144,1024]{1,0:T(8,128)(2,1)S(1)}, bf16[144,1024]{1,0:T(8,128)(2,1)}, u32[]{:S(2)}, u32[]{:S(2)}) collective-permute-start(bf16[144,1024]{1,0:T(8,128)(2,1)S(1)} %get-tuple-element.95), channel_id=1, source_target_pairs={{0,16},{4,20},{8,24},{12,28},{16,0},{20,4},{24,8},{28,12},{1,17},{... | collective-permute-start | bytes 884744 | tf_op jit(solution)/shard_map/ppermute | solution.py:363
  398.3 72.5 %collective-permute-start.98 = (bf16[144,1024]{1,0:T(8,128)(2,1)}, bf16[144,1024]{1,0:T(8,128)(2,1)}, u32[]{:S(2)}, u32[]{:S(2)}) collective-permute-start(bf16[144,1024]{1,0:T(8,128)(2,1)} %get-tuple-element.94), channel_id=1, source_target_pairs={{0,16},{4,20},{8,24},{12,28},{16,0},{20,4},{24,8},{28,12},{1,17},{... | collective-permute-start | bytes 884744 | tf_op jit(solution)/shard_map/ppermute | solution.py:363
  398.6 43.6 %collective-permute-start.86 = (bf16[4,32,2304]{2,1,0:T(8,128)(2,1)}, bf16[4,32,2304]{2,1,0:T(8,128)(2,1)S(1)}, u32[]{:S(2)}, u32[]{:S(2)}) collective-permute-start(bf16[4,32,2304]{2,1,0:T(8,128)(2,1)} %get-tuple-element.99), channel_id=1, source_target_pairs={{0,16},{4,20},{8,24},{12,28},{16,0},{20,4},{24,8},{28,12},{1,17},{... | collective-permute-start | bytes 1769480 | tf_op jit(solution)/shard_map/ppermute | solution.py:363
  401.2 31.6 %collective-permute-start.95 = (bf16[144,1024]{1,0:T(8,128)(2,1)S(1)}, bf16[144,1024]{1,0:T(8,128)(2,1)S(1)}, u32[]{:S(2)}, u32[]{:S(2)}) collective-permute-start(bf16[144,1024]{1,0:T(8,128)(2,1)S(1)} %add_convert_fusion.5), channel_id=1, source_target_pairs={{0,1},{1,2},{2,3},{3,0},{4,5},{5,6},{6,7},{7,4},{8,9},{9,10},{10,1... | collective-permute-start | bytes 884744 | tf_op jit(solution)/shard_map/ppermute | solution.py:368
  403.0 33.4 %collective-permute-start.85 = (bf16[4,32,2304]{2,1,0:T(8,128)(2,1)S(1)}, bf16[4,32,2304]{2,1,0:T(8,128)(2,1)S(1)}, u32[]{:S(2)}, u32[]{:S(2)}) collective-permute-start(bf16[4,32,2304]{2,1,0:T(8,128)(2,1)S(1)} %add_convert_fusion.2), channel_id=1, source_target_pairs={{0,1},{1,2},{2,3},{3,0},{4,5},{5,6},{6,7},{7,4},{8,9},{9,10},{10,1... | collective-permute-start | bytes 1769480 | tf_op jit(solution)/shard_map/ppermute | solution.py:368
  434.8 27.0 %collective-permute-start.97 = (bf16[144,1024]{1,0:T(8,128)(2,1)}, bf16[144,1024]{1,0:T(8,128)(2,1)}, u32[]{:S(2)}, u32[]{:S(2)}) collective-permute-start(bf16[144,1024]{1,0:T(8,128)(2,1)} %add_convert_fusion.4), channel_id=1, source_target_pairs={{0,1},{1,2},{2,3},{3,0},{4,5},{5,6},{6,7},{7,4},{8,9},{9,10},{10,1... | collective-permute-start | bytes 884744 | tf_op jit(solution)/shard_map/ppermute | solution.py:368
  437.6 12.3 %collective-permute-start.74 = (bf16[2,32,1024]{2,1,0:T(8,128)(2,1)S(1)}, bf16[2,32,1024]{2,1,0:T(8,128)(2,1)S(1)}, u32[]{:S(2)}, u32[]{:S(2)}) collective-permute-start(bf16[2,32,1024]{2,1,0:T(8,128)(2,1)S(1)} %get-tuple-element.120), channel_id=1, source_target_pairs={{0,8},{4,12},{8,0},{12,4},{16,24},{20,28},{24,16},{28,20},{1,9},{5... | collective-permute-start | bytes 393224 | tf_op jit(solution)/shard_map/ppermute | solution.py:363
  450.0 39.8 %collective-permute-start.56 = (bf16[512,1024]{1,0:T(8,128)(2,1)}, bf16[512,1024]{1,0:T(8,128)(2,1)}, u32[]{:S(2)}, u32[]{:S(2)}) collective-permute-start(bf16[512,1024]{1,0:T(8,128)(2,1)} %fusion.32), channel_id=1, source_target_pairs={{0,4},{4,0},{8,12},{12,8},{16,20},{20,16},{24,28},{28,24},{1,5},{5... | collective-permute-start | bytes 3145736 | tf_op jit(solution)/shard_map/ppermute | solution.py:363
  464.2 68.0 %collective-permute-start.88 = (bf16[4,32,2304]{2,1,0:T(8,128)(2,1)}, bf16[4,32,2304]{2,1,0:T(8,128)(2,1)}, u32[]{:S(2)}, u32[]{:S(2)}) collective-permute-start(bf16[4,32,2304]{2,1,0:T(8,128)(2,1)} %get-tuple-element.98), channel_id=1, source_target_pairs={{0,16},{4,20},{8,24},{12,28},{16,0},{20,4},{24,8},{28,12},{1,17},{... | collective-permute-start | bytes 1769480 | tf_op jit(solution)/shard_map/ppermute | solution.py:363
  464.7 23.0 %collective-permute-start.54 = (bf16[256,1024]{1,0:T(8,128)(2,1)}, bf16[256,1024]{1,0:T(8,128)(2,1)S(1)}, u32[]{:S(2)}, u32[]{:S(2)}) collective-permute-start(bf16[256,1024]{1,0:T(8,128)(2,1)} %get-tuple-element.125), channel_id=1, source_target_pairs={{1,4},{2,1},{3,5},{4,2},{5,6},{6,3},{9,12},{10,9},{11,13},{12,10},... | collective-permute-start | bytes 1572872 | tf_op jit(solution)/shard_map/ppermute | solution.py:422
  478.3 32.0 %collective-permute-start.87 = (bf16[4,32,2304]{2,1,0:T(8,128)(2,1)}, bf16[4,32,2304]{2,1,0:T(8,128)(2,1)}, u32[]{:S(2)}, u32[]{:S(2)}) collective-permute-start(bf16[4,32,2304]{2,1,0:T(8,128)(2,1)} %add_convert_fusion.1), channel_id=1, source_target_pairs={{0,1},{1,2},{2,3},{3,0},{4,5},{5,6},{6,7},{7,4},{8,9},{9,10},{10,1... | collective-permute-start | bytes 1769480 | tf_op jit(solution)/shard_map/ppermute | solution.py:368
  480.7 27.9 %collective-permute-start.55 = (bf16[256,1024]{1,0:T(8,128)(2,1)}, bf16[256,1024]{1,0:T(8,128)(2,1)}, u32[]{:S(2)}, u32[]{:S(2)}) collective-permute-start(bf16[256,1024]{1,0:T(8,128)(2,1)} %get-tuple-element.124), channel_id=1, source_target_pairs={{0,1},{1,5},{2,0},{3,4},{4,3},{5,7},{6,2},{7,6},{8,9},{9,13},{10,8... | collective-permute-start | bytes 1572872 | tf_op jit(solution)/shard_map/ppermute | solution.py:422
  510.4 23.8 %collective-permute-start.65 = (bf16[2,2,32,1152]{3,2,1,0:T(8,128)(2,1)S(1)}, bf16[2,2,32,1152]{3,2,1,0:T(8,128)(2,1)S(1)}, u32[]{:S(2)}, u32[]{:S(2)}) collective-permute-start(bf16[2,2,32,1152]{3,2,1,0:T(8,128)(2,1)S(1)} %get-tuple-element.107), channel_id=1, source_target_pairs={{0,16},{4,20},{8,24},{12,28},{16,0},{20,4},{24,8},{28,12},{1,17},{... | collective-permute-start | bytes 884744 | tf_op jit(solution)/shard_map/ppermute | solution.py:363
  511.4 22.9 %collective-permute-start.68 = (bf16[2,2,32,1152]{3,2,1,0:T(8,128)(2,1)S(1)}, bf16[2,2,32,1152]{3,2,1,0:T(8,128)(2,1)S(1)}, u32[]{:S(2)}, u32[]{:S(2)}) collective-permute-start(bf16[2,2,32,1152]{3,2,1,0:T(8,128)(2,1)S(1)} %get-tuple-element.105), channel_id=1, source_target_pairs={{0,8},{4,12},{8,0},{12,4},{16,24},{20,28},{24,16},{28,20},{1,9},{5... | collective-permute-start | bytes 884744 | tf_op jit(solution)/shard_map/ppermute | solution.py:363
  513.8 17.2 %collective-permute-start.60 = (bf16[2,32,1152]{2,1,0:T(8,128)(2,1)S(1)}, bf16[2,32,1152]{2,1,0:T(8,128)(2,1)S(1)}, u32[]{:S(2)}, u32[]{:S(2)}) collective-permute-start(bf16[2,32,1152]{2,1,0:T(8,128)(2,1)S(1)} %get-tuple-element.110), channel_id=1, source_target_pairs={{0,8},{4,12},{8,0},{12,4},{16,24},{20,28},{24,16},{28,20},{1,9},{5... | collective-permute-start | bytes 442376 | tf_op jit(solution)/shard_map/ppermute | solution.py:363
  518.0 27.3 %collective-permute-start.57 = (bf16[256,1024]{1,0:T(8,128)(2,1)S(1)}, bf16[256,1024]{1,0:T(8,128)(2,1)S(1)}, u32[]{:S(2)}, u32[]{:S(2)}) collective-permute-start(bf16[256,1024]{1,0:T(8,128)(2,1)S(1)} %get-tuple-element.123), channel_id=1, source_target_pairs={{1,4},{2,1},{3,5},{4,2},{5,6},{6,3},{9,12},{10,9},{11,13},{12,10},... | collective-permute-start | bytes 1572872 | tf_op jit(solution)/shard_map/ppermute | solution.py:422
  534.2 23.4 %collective-permute-start.58 = (bf16[256,1024]{1,0:T(8,128)(2,1)S(1)}, bf16[256,1024]{1,0:T(8,128)(2,1)S(1)}, u32[]{:S(2)}, u32[]{:S(2)}) collective-permute-start(bf16[256,1024]{1,0:T(8,128)(2,1)S(1)} %get-tuple-element.122), channel_id=1, source_target_pairs={{0,1},{1,5},{2,0},{3,4},{4,3},{5,7},{6,2},{7,6},{8,9},{9,13},{10,8... | collective-permute-start | bytes 1572872 | tf_op jit(solution)/shard_map/ppermute | solution.py:422
  543.0 11.7 %collective-permute-start.64 = (bf16[2,32,1152]{2,1,0:T(8,128)(2,1)S(1)}, bf16[2,32,1152]{2,1,0:T(8,128)(2,1)S(1)}, u32[]{:S(2)}, u32[]{:S(2)}) collective-permute-start(bf16[2,32,1152]{2,1,0:T(8,128)(2,1)S(1)} %get-tuple-element.104), channel_id=1, source_target_pairs={{0,1},{1,2},{2,3},{3,0},{4,5},{5,6},{6,7},{7,4},{8,9},{9,10},{10,1... | collective-permute-start | bytes 442376 | tf_op jit(solution)/shard_map/ppermute | solution.py:368
  545.6 12.1 %collective-permute-start.69 = (bf16[2,32,1152]{2,1,0:T(8,128)(2,1)S(1)}, bf16[2,32,1152]{2,1,0:T(8,128)(2,1)S(1)}, u32[]{:S(2)}, u32[]{:S(2)}) collective-permute-start(bf16[2,32,1152]{2,1,0:T(8,128)(2,1)S(1)} %get-tuple-element.102), channel_id=1, source_target_pairs={{0,16},{4,20},{8,24},{12,28},{16,0},{20,4},{24,8},{28,12},{1,17},{... | collective-permute-start | bytes 442376 | tf_op jit(solution)/shard_map/ppermute | solution.py:363
  (106 other events, 1419.8 us)

commit v2 on v1

--- a/solution.py
+++ b/solution.py
@@ -368,8 +368,8 @@
     return lax.ppermute(array, "ctx", [(i, (i + 1) % count) for i in range(count)])
 
 
-def after(array, *others):
-    return lax.optimization_barrier((array,) + others)[0]
+def hold(*arrays):
+    return lax.optimization_barrier(arrays)
 
 
 def choose(bit, zero, one):
@@ -384,6 +384,189 @@
     index = place + (0,) * (buffer.ndim - len(place))
     shape = (1,) * (buffer.ndim - array.ndim) + array.shape
     return lax.dynamic_update_slice(buffer, array.reshape(shape), index)
+
+
+def place_kernel(splits, count, slots_ref, *refs):
+    pieces, outs = refs[:count], refs[count:]
+    at = 0
+    for piece in pieces:
+        for part in range(len(splits)):
+            outs[splits[part]][slots_ref[at]] = piece[part]
+            at += 1
+
+
+def placed(pieces, splits, slots, counts):
+    shape = pieces[0].shape
+    return pl.pallas_call(
+        functools.partial(place_kernel, splits, len(pieces)),
+        in_specs=[pl.BlockSpec(memory_space=pltpu.SMEM)]
+        + [pl.BlockSpec(memory_space=pltpu.VMEM)] * len(pieces),
+        out_specs=[pl.BlockSpec(memory_space=pltpu.VMEM)] * len(counts),
+        out_shape=[
+            jax.ShapeDtypeStruct((count,) + shape[1:], pieces[0].dtype) for count in counts
+        ],
+        compiler_params=pltpu.CompilerParams(vmem_limit_bytes=40 * 2**20),
+    )(jnp.stack(slots).astype(jnp.int32), *pieces)
+
+
+def block_kernel(slots_ref, own_ref, core_ref, side_ref, down_ref, out_ref):
+    rows = own_ref.shape[1]
+    for member, ref, first in ((0, own_ref, 0), (1, core_ref, 1), (2, side_ref, 0), (3, side_ref, 2)):
+        for part in range(2):
+            start = pl.multiple_of((part * 4 + slots_ref[member]) * rows, rows)
+            out_ref[pl.ds(start, rows), :] = ref[first + part]
+    out_ref[8 * rows :, : down_ref.shape[1]] = down_ref[...]
+    out_ref[8 * rows :, down_ref.shape[1] :] = jnp.zeros_like(
+        out_ref[8 * rows :, down_ref.shape[1] :]
+    )
+
+
+def unit_block(slots, own, from_core, from_side, down):
+    rows, columns = own.shape[1:]
+    shape = (8 * rows + down.shape[0], columns)
+    return pl.pallas_call(
+        block_kernel,
+        in_specs=[pl.BlockSpec(memory_space=pltpu.SMEM)]
+        + [pl.BlockSpec(memory_space=pltpu.VMEM)] * 4,
+        out_specs=pl.BlockSpec(memory_space=pltpu.VMEM),
+        out_shape=jax.ShapeDtypeStruct(shape, own.dtype),
+    )(jnp.stack(slots).astype(jnp.int32), own, from_core, from_side, down)
+
+
+def unit_kernel(chunk, ctx_count, tiles, rows, slots_ref, *refs):
+    pieces, refs = refs[: 2 * ctx_count], refs[2 * ctx_count :]
+    b_refs, df_refs = refs[:2], refs[2:4]
+    act_ref, pre_ref, all_b_ref, all_df_ref = refs[-12:-8]
+    db_refs, out_refs, (w_ref, down_ref, b_ref, df_ref) = refs[-8:-6], refs[-6:-4], refs[-4:]
+    mid = pieces[0].shape[1]
+    width = down_ref.shape[1]
+    down_rows = pieces[0].shape[0] - 8 * rows
+    tile = pl.program_id(0)
+
+    @pl.when(tile == 0)
+    def _():
+        high = slots_ref[ctx_count]
+        for step in range(ctx_count):
+            place = slots_ref[step]
+            for far in range(2):
+                piece = pieces[2 * step + far]
+                for member in range(4):
+                    first = ((far * 4 + member) * ctx_count + place) * rows
+                    to = pl.ds(pl.multiple_of(first, rows), rows)
+                    w_ref[to, :mid] = piece[member * rows : (member + 1) * rows, :]
+                    w_ref[to, mid:] = piece[(4 + member) * rows : (5 + member) * rows, :]
+                half = high if far == 0 else 1 - high
+                first = (half * ctx_count + place) * down_rows
+                to = pl.ds(pl.multiple_of(first, 16), down_rows)
+                down_ref[to, :] = piece[8 * rows :, :width]
+
+    for which in range(2):
+
+        @pl.when(tile // tiles == which)
+        def _(which=which):
+            b_ref[...] = b_refs[which][...]
+            df_ref[...] = df_refs[which][...]
+
+    b, df = b_ref[...], df_ref[...]
+    all_b_ref[...] = b
+    all_df_ref[...] = df
+    db, out = 0.0, 0.0
+    for first in range(0, mid, chunk):
+        here, there = slice(first, first + chunk), slice(mid + first, mid + first + chunk)
+        gate = jnp.dot(b, w_ref[:, here], preferred_element_type=jnp.float32)
+        upper = jnp.dot(b, w_ref[:, there], preferred_element_type=jnp.float32)
+        d_act = nt(df, down_ref[here, :])
+        sigma = 1.0 / (1.0 + jnp.exp(-gate))
+        silu = gate * sigma
+        act = (silu * upper).astype(jnp.bfloat16)
+        d_upper = (d_act * silu).astype(jnp.bfloat16)
+        d_gate = (d_act * upper * sigma * (1.0 + gate * (1.0 - sigma))).astype(jnp.bfloat16)
+        act_ref[:, here] = act
+        pre_ref[:, here] = d_gate
+        pre_ref[:, there] = d_upper
+        db += nt(d_gate, w_ref[:, here]) + nt(d_upper, w_ref[:, there])
+        out += jnp.dot(act, down_ref[here, :], preferred_element_type=jnp.float32)
+    for which in range(2):
+
+        @pl.when(tile // tiles == which)
+        def _(which=which):
+            db_refs[which][...] = db.astype(jnp.bfloat16)
+            out_refs[which][...] = out.astype(jnp.bfloat16)
+
+
+def feed_forward(slots, pieces, rows, b_parts, df_parts, size, begin, left):
+    tokens, width = b_parts[0].shape
+    mid = pieces[0].shape[1]
+    down_rows = pieces[0].shape[0] - 8 * rows
+    tiles = tokens // size
+    once = lambda array: pl.BlockSpec(
+        array.shape, lambda t: (0,) * array.ndim, pipeline_mode=pl.Buffered(1)
+    )
+
+    def part(which):
+        return pl.BlockSpec((size, width), lambda t: (jnp.clip(t - which * tiles, 0, tiles - 1), 0))
+
+    def tiled(count, first):
+        return pl.BlockSpec((size, count), lambda t: (first + t, 0))
+
+    first = begin * tiles
+    first_left = 1 + len(pieces) + 4
+    full = lambda count: jax.ShapeDtypeStruct((4 * tokens, count), jnp.bfloat16)
+    half = jax.ShapeDtypeStruct((tokens, width), jnp.bfloat16)
+    return pl.pallas_call(
+        functools.partial(unit_kernel, mid // 3, len(pieces) // 2, tiles, rows),
+        grid=(2 * tiles,),
+        in_specs=[pl.BlockSpec(memory_space=pltpu.SMEM)]
+        + [once(array) for array in pieces]
+        + [part(which) for which in range(2)] * 2
+        + [pl.BlockSpec(memory_space=pl.ANY)] * len(left),
+        out_specs=[tiled(mid, first), tiled(2 * mid, first), tiled(width, first), tiled(width, first)]
+        + [part(which) for which in range(2)] * 2,
+        out_shape=[full(mid), full(2 * mid), full(width), full(width)] + [half] * 4,
+        input_output_aliases={first_left + at: at for at in range(len(left))},
+        scratch_shapes=[
+            pltpu.VMEM((width, 2 * mid), jnp.bfloat16),
+            pltpu.VMEM((len(pieces) * down_rows, width), jnp.bfloat16),
+            pltpu.VMEM((size, width), jnp.bfloat16),
+            pltpu.VMEM((size, width), jnp.bfloat16),
+        ],
+        compiler_params=pltpu.CompilerParams(vmem_limit_bytes=52 * 2**20),
+        cost_estimate=pl.CostEstimate(flops=10 * tokens * mid * width, bytes_accessed=0, transcendentals=0),
+    )(jnp.stack(slots).astype(jnp.int32), *pieces, *b_parts, *df_parts, *left)
+
+
+def spread_kernel(ctx_count, rows, slots_ref, ffn_ref, down_ref, *outs):
+    mid = ffn_ref.shape[1] // 2
+    width = down_ref.shape[1]
+    down_rows = down_ref.shape[0] // (2 * ctx_count)
+    high = slots_ref[ctx_count]
+    for far in range(2):
+        half = high if far == 0 else 1 - high
+        for step in range(ctx_count):
+            place = slots_ref[step]
+            out = outs[far * ctx_count + step]
+            for member in range(4):
+                first = ((far * 4 + member) * ctx_count + place) * rows
+                here = pl.ds(pl.multiple_of(first, rows), rows)
+                out[member * rows : (member + 1) * rows, :] = ffn_ref[here, :mid]
+                out[(4 + member) * rows : (5 + member) * rows, :] = ffn_ref[here, mid:]
+            first = (half * ctx_count + place) * down_rows
+            here = pl.ds(pl.multiple_of(first, 16), down_rows)
+            out[8 * rows :, :width] = down_ref[here, :]
+            out[8 * rows :, width:] = jnp.zeros_like(out[8 * rows :, width:])
+
+
+def spread_units(slots, ffn, down, rows, ctx_count):
+    shape = (8 * rows + down.shape[0] // (2 * ctx_count), ffn.shape[1] // 2)
+    return pl.pallas_call(
+        functools.partial(spread_kernel, ctx_count, rows),
+        in_specs=[pl.BlockSpec(memory_space=pltpu.SMEM)]
+        + [pl.BlockSpec(memory_space=pltpu.VMEM)] * 2,
+        out_specs=[pl.BlockSpec(memory_space=pltpu.VMEM)] * (2 * ctx_count),
+        out_shape=[jax.ShapeDtypeStruct(shape, ffn.dtype)] * (2 * ctx_count),
+        compiler_params=pltpu.CompilerParams(vmem_limit_bytes=40 * 2**20),
+        cost_estimate=pl.CostEstimate(flops=3 * 10**9, bytes_accessed=0, transcendentals=0),
+    )(jnp.stack(slots).astype(jnp.int32), ffn, down)
 
 
 def joined(*arrays):
@@ -408,23 +591,31 @@
     return choose(bit, low, high)
 
 
-def exchange(array, target, index_of, turn):
+def exchange(array, target, index_of):
     dp_count, ctx_count = lax.axis_size("dp"), lax.axis_size("ctx")
-    pairs, stay = [], []
-    for dp in range(dp_count):
-        for z in range(ctx_count):
-            to = target(dp, z, turn)
-            if to == (dp, z):
-                stay.append(dp * ctx_count + z)
-            else:
-                pairs.append((dp * ctx_count + z, to[0] * ctx_count + to[1]))
-    piece = pick(array, index_of(turn))
-    got = lax.ppermute(piece, ("dp", "ctx"), pairs)
-    if stay:
-        me = lax.axis_index("dp") * ctx_count + lax.axis_index("ctx")
-        mine = functools.reduce(jnp.logical_or, [me == which for which in stay])
-        got = jnp.where(mine, piece, got)
-    return got
+    me = lax.axis_index("dp") * ctx_count + lax.axis_index("ctx")
+    came, kept = [], []
+    for turn in range(2):
+        pairs, stay = [], []
+        for dp in range(dp_count):
+            for z in range(ctx_count):
+                to = target(dp, z, turn)
+                if to == (dp, z):
+                    stay.append(dp * ctx_count + z)
+                else:
+                    pairs.append((dp * ctx_count + z, to[0] * ctx_count + to[1]))
+        piece = pick(array, index_of(turn))
+        came.append(lax.ppermute(piece, ("dp", "ctx"), pairs))
+        mine = functools.reduce(jnp.logical_or, [me == which for which in stay]) if stay else None
+        kept.append((piece, mine))
+    return came, kept
+
+
+def settled(came, kept):
+    return [
+        got if mine is None else jnp.where(mine, piece, got)
+        for got, (piece, mine) in zip(came, kept)
+    ]
 
 
 def spread(array):
@@ -433,8 +624,7 @@
     def target(dp, z, turn):
         return dp // 2 * 2 + z // 2, 2 * ((z + turn) % 2) + dp % 2
 
-    got = [exchange(array, target, lambda turn: (ctx + turn) % 2, turn) for turn in range(2)]
-    return order(ctx // 2, got[0], got[1])
+    return exchange(array, target, lambda turn: (ctx + turn) % 2)
 
 
 def unspread(array):
@@ -443,8 +633,7 @@
     def target(dp, z, turn):
         return dp // 2 * 2 + z % 2, 2 * (dp % 2) + (z // 2 + turn) % 2
 
-    got = [exchange(array, target, lambda turn: (ctx // 2 + turn) % 2, turn) for turn in range(2)]
-    return order(ctx % 2, got[0], got[1])
+    return exchange(array, target, lambda turn: (ctx // 2 + turn) % 2)
 
 
 def swap_gather(array, bit_value, bit):
@@ -453,17 +642,6 @@
 
 def total_low(left, right):
     return (left.astype(jnp.float32) + right.astype(jnp.float32)).astype(jnp.bfloat16)
-
-
-def team_gather(array, gate=None):
-    side, core = flip(array, SIDE), flip(array, CORE)
-    return joined(array, side, core, flip(side, CORE)).reshape((-1,) + array.shape[1:])
-
-
-def team_reduce(array):
-    got = flip(array[2:].astype(jnp.bfloat16), CORE).astype(jnp.float32)
-    side = flip((array[1] + got[1]).astype(jnp.bfloat16), SIDE)
-    return array[0] + got[0] + side.astype(jnp.float32)
 
 
 def nt(left, right):
@@ -519,16 +697,14 @@
 
     cosine, sine = cos_ref[...], sin_ref[...]
     keys = turned(kv_ref[:head, :], gain_ref[1], cosine, sine)
-    kvr_ref[:head, :] = keys
+    kvr_ref[:head, :] = keys.astype(jnp.bfloat16)
     keys = keys.T.astype(jnp.bfloat16)
-    values = kv_ref[head:, :]
+    values = kv_ref[head:, :].astype(jnp.bfloat16)
     kvr_ref[head:, :] = values
-    values = values.astype(jnp.bfloat16)
     for which in range(q_ref.shape[0] // head):
         rows = slice(which * head, (which + 1) * head)
-        query = turned(q_ref[rows, :], gain_ref[0], cosine, sine)
+        query = turned(q_ref[rows, :], gain_ref[0], cosine, sine).astype(jnp.bfloat16)
         qr_ref[rows, :] = query
-        query = query.astype(jnp.bfloat16)
         for first in range(0, size, block):
             here = slice(first, first + block)
             total = jnp.zeros((1, block), jnp.float32)
@@ -562,16 +738,15 @@
 
     cosine, sine = cos_ref[...], sin_ref[...]
     keys_t = kvr_ref[:head, :]
-    keys = keys_t.T.astype(jnp.bfloat16)
-    keys_t = keys_t.astype(jnp.bfloat16)
-    values = kvr_ref[head:, :].T.astype(jnp.bfloat16)
+    keys = keys_t.astype(jnp.float32).T.astype(jnp.bfloat16)
+    values = kvr_ref[head:, :].astype(jnp.float32).T.astype(jnp.bfloat16)
     dkey_ref[...] = jnp.zeros_like(dkey_ref)
     dvalue_ref[...] = jnp.zeros_like(dvalue_ref)
     found = []
     for which in range(q_ref.shape[0] // head):
         rows = slice(which * head, (which + 1) * head)
-        query = qr_ref[rows, :].astype(jnp.bfloat16)
-        grad = do_ref[rows, :].astype(jnp.bfloat16)
+        query = qr_ref[rows, :]
+        grad = do_ref[rows, :]
         delta = jnp.sum(grad.astype(jnp.float32) * o_ref[rows, :], 0, keepdims=True)
         pieces = []
         for first in range(0, size, block):
@@ -594,9 +769,9 @@
         )
         found.append(dquery)
         gains_ref[0] += terms
-    dq_ref[...] = jnp.concatenate(found, 0).T
+    dq_ref[...] = jnp.concatenate(found, 0).T.astype(jnp.bfloat16)
     dkey, terms = turned_back(dkey_ref[...] * scale, kv_ref[:head, :], gain_ref[1], cosine, sine)
-    dkv_ref[...] = jnp.concatenate([dkey, dvalue_ref[...]], 0).T
+    dkv_ref[...] = jnp.concatenate([dkey, dvalue_ref[...]], 0).T.astype(jnp.bfloat16)
     gains_ref[1] += terms
 
 
@@ -630,16 +805,12 @@
         out_shape=[
             jax.ShapeDtypeStruct((kv_own * group * head, size), jnp.float32),
             jax.ShapeDtypeStruct((kv_own, group, size), jnp.float32),
-            jax.ShapeDtypeStruct((kv_own * group * head, size), jnp.float32),
-            jax.ShapeDtypeStruct((kv_own * 2 * head, size), jnp.float32),
+            jax.ShapeDtypeStruct((kv_own * group * head, size), jnp.bfloat16),
+            jax.ShapeDtypeStruct((kv_own * 2 * head, size), jnp.bfloat16),
         ],
         scratch_shapes=[pltpu.VMEM((size, size), jnp.float32)],
         compiler_params=pltpu.CompilerParams(vmem_limit_bytes=40 * 2**20),
-        cost_estimate=pl.CostEstimate(
-            flops=16 * kv_own * group * size * size * head,
-            bytes_accessed=12 * raw.size,
-            transcendentals=kv_own * group * size * size,
-        ),
+        cost_estimate=pl.CostEstimate(flops=10**6, bytes_accessed=0, transcendentals=0),
     )(raw, raw, cosine, sine, gains, segments[None, :], segments[:, None])
 
 
@@ -674,8 +845,8 @@
             whole_spec(2, head, 1),
         ],
         out_shape=[
-            jax.ShapeDtypeStruct((size, count * group * head), jnp.float32),
-            jax.ShapeDtypeStruct((size, count * 2 * head), jnp.float32),
+            jax.ShapeDtypeStruct((size, count * group * head), jnp.bfloat16),
+            jax.ShapeDtypeStruct((size, count * 2 * head), jnp.bfloat16),
             jax.ShapeDtypeStruct((2, head, 1), jnp.float32),
         ],
         scratch_shapes=[
@@ -684,11 +855,7 @@
             pltpu.VMEM((head, size), jnp.float32),
         ],
         compiler_params=pltpu.CompilerParams(vmem_limit_bytes=40 * 2**20),
-        cost_estimate=pl.CostEstimate(
-            flops=40 * count * group * size * size * head,
-            bytes_accessed=4 * raw.size * count,
-            transcendentals=count * group * size * size,
-        ),
+        cost_estimate=pl.CostEstimate(flops=10**6, bytes_accessed=0, transcendentals=0),
     )(
         raw, raw, turned_q, turned_kv, grad, attended, logs, cosine, sine, gains,
         segments[None, :], segments[:, None]
@@ -722,39 +889,12 @@
     kv_own = w_key.shape[1] // head // 2
     units = w_down.shape[0] * ctx_count
 
-    x_half = spread(hidden_in[:, 0]).reshape(-1, width)
-    marks = spread(jnp.stack([segment_ids[:, 0], doc_positions[:, 0]], 1))
-    marks = swap_gather(marks, core, CORE).reshape(-1, 2, marks.shape[-1])
-    segments, places = marks[:, 0].reshape(-1), marks[:, 1].reshape(-1)
-    x_all = swap_gather(x_half, core, CORE).reshape(-1, width)
-
-    def of_member(which):
-        return jnp.concatenate(
-            [
-                w[:, (top * 4 + which) * units : (top * 4 + which + 1) * units]
-                for w in (w_gate, w_up)
-                for top in range(w_gate.shape[1] // units // 4)
-            ],
-            1,
-        )
-
-    def related(zero, one, two, three):
-        near, far = choose(side, zero, two), choose(side, two, zero)
-        near_far, far_far = choose(side, one, three), choose(side, three, one)
-        return (
-            choose(core, near, near_far),
-            choose(core, far, far_far),
-            choose(core, near_far, near),
-            choose(core, far_far, far),
-        )
-
-    members = related(*[of_member(which) for which in range(4)])
-    block_ffn = jnp.zeros((2, 2) + members[0].shape, low)
-    block_ffn = put(block_ffn, members[0], side, core)
-    block_ffn = put(block_ffn, flip(members[1], SIDE), 1 - side, core)
-    block_ffn = put(block_ffn, flip(members[2], CORE), side, 1 - core)
-    block_ffn = put(block_ffn, flip(members[3], SIDE | CORE), 1 - side, 1 - core)
-    block_ffn = block_ffn.reshape(4, rows, -1)
+    tokens = hidden_in.shape[2]
+    marks = jnp.stack(
+        [segment_ids[:, 0], doc_positions[:, 0] // 256, doc_positions[:, 0] % 256], 1
+    ).reshape(2, 1, -1)
+    marks = jnp.pad(marks, ((0, 0), (0, 15), (0, width - 3 * tokens))).astype(low)
+    both_came, both_kept = spread(jnp.concatenate([hidden_in[:, 0], marks, out_grad[:, 0]], 1))
 
     head_few = head_gains.shape[0]
     gains = jnp.stack([attn_gain, ffn_gain, jnp.pad(head_gains, (0, rows - head_few))])
@@ -772,62 +912,113 @@
         for which in range(2)
     ]
     inner = parities[0].shape[1]
-    got = flip(choose(core, parities[1], parities[0]), CORE)
+
+    tops = w_gate.shape[1] // units // 4
+
+    def of_member(which):
+        return [
+            jnp.concatenate(
+                [w[:, (top * 4 + which) * units : (top * 4 + which + 1) * units] for top in range(tops)],
+                1,
+            )
+            for w in (w_gate, w_up)
+        ]
+
+    def related(zero, one, two, three):
+        near, far = choose(side, zero, two), choose(side, two, zero)
+        near_far, far_far = choose(side, one, three), choose(side, three, one)
+        return (
+            choose(core, near, near_far),
+            choose(core, far, far_far),
+            choose(core, near_far, near),
+            choose(core, far_far, far),
+        )
+
+    members = [of_member(which) for which in range(4)]
+    gate_of = related(*[member[0] for member in members])
+    up_of = related(*[member[1] for member in members])
+    from_core = flip(
+        joined(choose(core, parities[1], parities[0]), gate_of[2], up_of[2], gate_of[3], up_of[3]),
+        CORE,
+    )
     block = joined(
-        choose(core, parities[0], got),
-        choose(core, got, parities[1]),
+        choose(core, parities[0], from_core[0]),
+        choose(core, from_core[0], parities[1]),
         jnp.pad(w_out, ((0, 0), (0, inner - width))),
     )
-    buffer = jnp.zeros((2, 2, 3, ctx_count, rows, inner), low)
+    from_side = flip(joined(gate_of[1], up_of[1], from_core[3], from_core[4]), SIDE)
+    blocks = [block]
+    for step in range(ctx_count - 1):
+        blocks.append(spin(blocks[-1]))
+
+    def across(pair):
+        return [pair, flip(pair, SIDE), flip(pair, HIGH), flip(pair, SIDE | HIGH)]
+
+    early = across(jnp.concatenate(blocks[:2], 0))
+    blocks[3], *rest = hold(blocks[3], *both_came, *early)
+    both_came, early = rest[:2], rest[2:]
+    late = across(jnp.concatenate(blocks[2:], 0))
+    block_ffn = unit_block(
+        [side * 2 + core, side * 2 + 1 - core, 2 - side * 2 + core, 2 - side * 2 + 1 - core],
+        joined(gate_of[0], up_of[0]), from_core, from_side, w_down,
+    )
+    ffn_blocks = [block_ffn, spin(block_ffn)]
+    got = settled(both_came, both_kept)
+    taken = tokens + 16
+    x_half = order(ctx // 2, got[0][:taken], got[1][:taken])
+    x_other = flip(x_half, CORE)
+    x_half, *late = hold(x_half, *late)
+    ffn_far = [flip(block_ffn, HIGH)]
+    df = order(ctx // 2, got[0][taken:], got[1][taken:]).reshape(-1, width)
+    df_side, df_core = flip(df, SIDE), flip(df, CORE)
+    pieces = [
+        pair[3 * part : 3 * part + 3] for pairs in (early, late) for part in range(2) for pair in pairs
+    ]
+
+    slots = []
     for step in range(ctx_count):
-        following = spin(block) if step < ctx_count - 1 else None
-        from_side, from_high = flip(block, SIDE), flip(block, HIGH)
-        from_both = flip(from_side, HIGH) if step % 2 == 0 else flip(from_high, SIDE)
         place = (ctx - step) % ctx_count
-        for up, across, piece in (
-            (high, side, block),
-            (high, 1 - side, from_side),
-            (1 - high, side, from_high),
-            (1 - high, 1 - side, from_both),
-        ):
-            buffer = put(buffer, piece[:, None], up, across, 0, place)
-        last_attn = block
-        block = following
-    w_in = buffer[:, :, :2].reshape(-1, inner)
-    w_mine = buffer[:, :, 2].reshape(-1, inner)[:, :width]
+        for far in range(4):
+            up = 1 - high if far >= 2 else high
+            across_to = 1 - side if far % 2 == 1 else side
+            chip = up * 2 + across_to
+            slots += [(chip * 2 + c) * ctx_count + place for c in range(2)]
+            slots += [chip * ctx_count + place]
+    w_in, w_mine = placed(pieces, (0, 0, 1), slots, (8 * ctx_count, 4 * ctx_count))
+    w_in, w_mine = w_in.reshape(-1, inner), w_mine.reshape(-1, inner)[:, :width]
+    w_in, w_mine, x_other, ffn_blocks[1], ffn_far[0] = hold(
+        w_in, w_mine, x_other, ffn_blocks[1], ffn_far[0]
+    )
+    ffn_blocks.append(spin(ffn_blocks[1]))
+    ffn_far.append(flip(ffn_blocks[1], HIGH))
     w_theirs = flip(w_mine, CORE)
-
     features = inner - 128
     gains_all = w_in[:, features:].reshape(-1, rows, 128)[:, :3, :rows].astype(full)
+    w_in = w_in[:, :features]
     attn_gain_all, ffn_gain_all = gains_all[:, 0].reshape(-1), gains_all[:, 1].reshape(-1)
     head_gains_all = gains_all[:, 2, :head_few].reshape(2, head, 1)
-    w_in = w_in[:, :features]
-
-    ffn_blocks, ffn_far = [after(block_ffn, x_half, last_attn)], []
-
-    def ffn_step(*ready):
-        block = ffn_blocks[-1]
-        if ready:
-            block = after(block, *ready)
-            ffn_blocks[-1] = block
-        if len(ffn_blocks) < ctx_count:
-            ffn_blocks.append(spin(block))
-        ffn_far.append(flip(block, HIGH))
-
-    x = x_all.astype(full)
-    normed, _, _ = norm_forward(x, attn_gain_all)
+
+    x_all = order(core, x_half, x_other)
+    marks = x_all[:, :, tokens, : 3 * tokens].reshape(-1, 3, tokens)
+    x_all, x_half = x_all[:, :, :tokens].reshape(-1, width), x_half[:, :tokens].reshape(-1, width)
+    segments = marks[:, 0].reshape(-1).astype(jnp.int32)
+    places = (256.0 * marks[:, 1].astype(full) + marks[:, 2].astype(full)).reshape(-1)
+    normed, _, _ = norm_forward(x_all.astype(full), attn_gain_all)
     a_low = normed.astype(low)
-    ffn_step()
     raw = lax.dot_general(w_in, a_low, (((0,), (1,)), ((), ())), preferred_element_type=full)
-    ffn_step(a_low)
     freq = THETA ** (-(jnp.arange(head // 2, dtype=full) * 2.0 / head))
-    turn = freq[:, None] * places.astype(full)[None, :]
+    turn = freq[:, None] * places[None, :]
     cosine, sine = jnp.cos(turn), jnp.sin(turn)
     attended, logs, turned_q, turned_kv = attend(
         raw, cosine, sine, head_gains_all, segments, kv_own, head, 256
     )
-    ffn_step(attended)
     attended_low = attended.astype(low)
+    attended_low, ffn_blocks[2], ffn_far[1], df_side, df_core, w_theirs = hold(
+        attended_low, ffn_blocks[2], ffn_far[1], df_side, df_core, w_theirs
+    )
+    df_both = flip(df_side, CORE)
+    ffn_blocks.append(spin(ffn_blocks[2]))
+    ffn_far.append(flip(ffn_blocks[2], HIGH))
     o_theirs = flip(half_of(1 - core, attended_low, 1), CORE)
     hidden = (
         x_half.astype(full)
@@ -836,141 +1027,155 @@
     )
     normed_two, h_unit, h_factor = norm_forward(hidden, ffn_gain_all)
     b_own = swap_halves(high, normed_two.astype(low), 1)
+    b_own, ffn_blocks[3], ffn_far[2], df_both = hold(b_own, ffn_blocks[3], ffn_far[2], df_both)
+    ffn_far.append(flip(ffn_blocks[3], HIGH))
     b_side, b_core = flip(b_own, SIDE), flip(b_own, CORE)
-    ffn_step(b_own)
-    w_ffn = jnp.zeros((2, 4, ctx_count) + block_ffn.shape[1:], low)
-    for step in range(ctx_count):
-        place = (ctx - step) % ctx_count
-        w_ffn = put(w_ffn, ffn_blocks[step][:, None], 0, 0, place)
-        w_ffn = put(w_ffn, ffn_far[step][:, None], 1, 0, place)
-    w_ffn = w_ffn.reshape(width, -1)
-    df = spread(after(out_grad[:, 0], b_own)).reshape(-1, width)
-    down_blocks, down_far = [after(w_down, ffn_blocks[-1])], []
-
-    def down_step(*ready):
-        block = down_blocks[-1]
-        if ready:
-            block = after(block, *ready)
-            down_blocks[-1] = block
-        if len(down_blocks) < ctx_count:
-            down_blocks.append(spin(block))
-        down_far.append(flip(block, HIGH))
-
-    down_step()
+    b_side, b_core, ffn_far[3] = hold(b_side, b_core, ffn_far[3])
     b_both = flip(b_side, CORE)
-    team_b = joined(b_own, b_side, b_core, b_both).reshape(-1, width)
-    down_step(b_both)
-    down_step(b_both)
-    pre = matmul(team_b, w_ffn)
-    down_step(pre)
-    w_down_all = jnp.zeros((2, ctx_count) + w_down.shape, low)
-    for step in range(ctx_count):
-        place = (ctx - step) % ctx_count
-        w_down_all = put(w_down_all, down_blocks[step], high, place)
-        w_down_all = put(w_down_all, down_far[step], 1 - high, place)
-    w_down_all = w_down_all.reshape(-1, width)
-    team_df = team_gather(df)
-
-    mid = pre.shape[1] // 2
-    gate, upper = pre[:, :mid], pre[:, mid:]
-    sigma = jax.nn.sigmoid(gate)
-    act = (gate * sigma * upper).astype(low)
-    d_act = right_trans(team_df, w_down_all)
-    d_upper = (d_act * gate * sigma).astype(low)
-    d_gate = (d_act * upper * sigma * (1.0 + gate * (1.0 - sigma))).astype(low)
-    d_pre = jnp.concatenate([d_gate, d_upper], 1)
-    partial_db = right_trans(d_pre, w_ffn)
-    db = team_reduce(partial_db.reshape(4, -1, width))
-    db = swap_halves(high, db, 1)
+
+    units_of = functools.partial(
+        feed_forward,
+        [(ctx - step) % ctx_count for step in range(ctx_count)] + [high],
+        [block for pair in zip(ffn_blocks, ffn_far) for block in pair],
+        rows,
+    )
+    *left, db_side, db_both, out_side, out_both = units_of(
+        [b_side, b_both], [df_side, df_both], 256, 2, []
+    )
+    got_both, got_out_both = flip(db_both, CORE), flip(out_both, CORE)
+    db_far = total_low(db_side, got_both)
+    db_far, b_own, b_core, got_out_both = hold(db_far, b_own, b_core, got_out_both)
+    got_side = flip(db_far, SIDE)
+    act, d_pre, team_b, team_df, db_own, db_core, out_own, out_core = units_of(
+        [b_own, b_core], [df, df_core], 256, 0, left
+    )
+    block_side = total_low(out_side, got_out_both)
+    db_core, d_pre, act, got_side, block_side = hold(db_core, d_pre, act, got_side, block_side)
+    got_core, got_out_core, got_block = flip(db_core, CORE), flip(out_core, CORE), flip(block_side, SIDE)
 
     def behind(step):
         return (ctx - 1 - step) % ctx_count
 
-    g_ffn = left_trans(after(team_b, partial_db), d_pre).astype(low)
-    g_ffn = g_ffn.reshape(2, 4, ctx_count, rows, -1)
-    ffn_got = [flip(pick(g_ffn[1], behind(step), 1), HIGH) for step in range(ctx_count)]
-    g_down = left_trans(after(act, g_ffn), team_df).astype(low)
-    g_down = g_down.reshape(2, ctx_count, -1, width)
-    g_down_near, g_down_far = pick(g_down, high), pick(g_down, 1 - high)
-    down_got = [flip(pick(g_down_far, behind(step)), HIGH) for step in range(ctx_count)]
-    partial_out = matmul(after(act, g_down), w_down_all)
-
-    def ffn_term(step):
-        return total_low(pick(g_ffn[0], behind(step), 1), ffn_got[step])
-
-    def down_term(step):
-        return total_low(pick(g_down_near, behind(step)), down_got[step])
-
-    ffn_ring = spin(after(ffn_term(0), partial_out))
-    down_ring = spin(after(down_term(0), partial_out))
+    g_down = left_trans(act, team_df).astype(low)
+    g_down, team_b = hold(g_down, team_b)
+    g_ffn = left_trans(team_b, d_pre).astype(low)
+    terms = spread_units(
+        [behind(step) for step in range(ctx_count)] + [high], g_ffn, g_down, rows, ctx_count
+    )
+    *terms, got_core, got_out_core, got_block = hold(*terms, got_core, got_out_core, got_block)
+    near_terms = terms[:ctx_count]
+    far_got = [flip(term, HIGH) for term in terms[ctx_count:]]
+    block_out = hidden + out_own.astype(full) + got_out_core.astype(full) + got_block.astype(full)
+    block_came, block_kept = unspread(block_out.astype(low).reshape(2, -1, width))
+
+    db = db_own.astype(full) + got_core.astype(full) + got_side.astype(full)
+    db = swap_halves(high, db, 1)
     d_hidden, ffn_terms = norm_backward(db, h_unit, h_factor, ffn_gain_all)
     d_hidden = df.astype(full) + d_hidden
     dz = d_hidden.astype(low)
-    dz_all = swap_gather(dz, core, CORE).reshape(-1, width)
-    ffn_ring = spin(total_low(after(ffn_ring, dz), ffn_term(1)))
-    down_ring = spin(total_low(after(down_ring, dz), down_term(1)))
-    d_attended = right_trans(w_mine, dz_all)
+    dz_other = flip(dz, CORE)
+    dz_all = order(core, dz, dz_other).reshape(-1, width)
+    d_attended = right_trans(w_mine, dz_all).astype(low)
     g_out = matmul(attended_low, dz_all).astype(low).reshape(2, 2, ctx_count, -1, width)
+
+    def side_square(array):
+        near = jnp.where(side == 0, array[:, 0], array[:, 1])
+        far = jnp.where(side == 0, array[:, 1], array[:, 0])
+        near = joined(pick(near, high), pick(near, 1 - high))
+        return near, flip(joined(pick(far, high), pick(far, 1 - high)), SIDE)
+
+    def high_square(near, got):
+        sums = near.astype(full) + got.astype(full)
+        return sums[0], flip(sums[1].astype(low), HIGH)
+
+    def total(terms):
+        return functools.reduce(lambda a, b: a + b, [term.astype(full) for term in terms])
+
     back = functools.partial(
-        attend_back, raw, turned_q, turned_kv, d_attended, attended, logs, cosine, sine,
-        head_gains_all, segments, kv_own, head, 256
-    )
-    dq_one, dkv_one, g_heads_one = back(0, kv_own // 2)
-    ffn_ring = spin(total_low(after(ffn_ring, dq_one), ffn_term(2)))
-    down_ring = spin(total_low(after(down_ring, dq_one), down_term(2)))
-    block_out = hidden + team_reduce(partial_out.reshape(4, -1, width))
-    block_out = unspread(after(block_out, dq_one).astype(low).reshape(2, -1, width))
-
-    def squares(array, step):
-        part = pick(array, behind(step), 2)
-        mine, other = pick(part, high), pick(part, 1 - high)
-        if step % 2 == 0:
-            got = flip(other, HIGH)
-            mine_near, mine_far = pick(mine, side), pick(mine, 1 - side)
-            got_near, got_far = pick(got, side), pick(got, 1 - side)
-            from_side = flip(total_low(mine_far, got_far), SIDE)
-            return total_low(total_low(mine_near, got_near), from_side)
-        near, far = pick(part, side, 1), pick(part, 1 - side, 1)
-        got = flip(far, SIDE)
-        from_high = flip(total_low(pick(near, 1 - high), pick(got, 1 - high)), HIGH)
-        return total_low(total_low(pick(near, high), pick(got, high)), from_high)
-
-    out_terms = [squares(after(g_out, dq_one), step) for step in range(ctx_count)]
-    out_ring = spin(out_terms[0])
-    dq_two, dkv_two, g_heads_two = back(kv_own // 2, kv_own - kv_own // 2)
-    d_raw = jnp.concatenate([dq_one, dq_two, dkv_one, dkv_two], 1).astype(low)
-    g_heads = g_heads_one + g_heads_two
+        attend_back, raw, turned_q, turned_kv, attended=attended, logs=logs, cosine=cosine,
+        sine=sine, gains=head_gains_all, segments=segments, kv_own=kv_own, head=head, block=256
+    )
+    g_out = jnp.stack([pick(g_out, behind(step), 2) for step in range(ctx_count)], 2)
+    g_out, d_attended, far_got[0], *block_came = hold(g_out, d_attended, far_got[0], *block_came)
+    unit_total = total_low(near_terms[0], far_got[0])
+    d_attended, unit_total = hold(d_attended, unit_total)
+    unit_ring = spin(unit_total)
+    out_near, out_got = side_square(g_out)
+    dq, dkv, g_heads = back(grad=d_attended, begin=0, count=kv_own)
+    dq, out_got, unit_ring, far_got[1] = hold(dq, out_got, unit_ring, far_got[1])
+    out_near, out_got = high_square(out_near, out_got)
+    unit_total = total_low(unit_ring, total_low(near_terms[1], far_got[1]))
+    unit_ring = spin(unit_total)
+    d_raw = jnp.concatenate([dq, dkv], 1)
+    d_theirs = right_trans(half_of(1 - core, d_raw, 0), w_in).astype(low)
+    d_theirs, d_raw = hold(d_theirs, d_raw)
+    d_from = flip(d_theirs, CORE)
     g_in = left_trans(a_low, d_raw).astype(low)
-    d_theirs = right_trans(half_of(1 - core, d_raw, 0), w_in)
-    d_from = flip(d_theirs.astype(low), CORE)
-    d_inner = right_trans(half_of(core, d_raw, 0), w_in) + d_from.astype(full)
+    g_in = g_in.reshape(2, 2, 2, ctx_count, rows, features)
+    g_in = jnp.stack([pick(g_in, behind(step), 3) for step in range(ctx_count)], 2)
+    g_in, d_raw = hold(g_in, d_raw)
+    early_near, early_got = side_square(g_in[:, :, :2])
+    late_near, late_got = side_square(g_in[:, :, 2:])
+    d_inner = right_trans(half_of(core, d_raw, 0), w_in)
+    d_inner, d_from, out_got = hold(d_inner, d_from, out_got)
+    d_inner = d_inner + d_from.astype(full)
     _, x_unit, x_factor = norm_forward(x_half.astype(full), attn_gain_all)
     d_input, attn_terms = norm_backward(d_inner, x_unit, x_factor, attn_gain_all)
-    in_grad = unspread((d_hidden + d_input).astype(low).reshape(2, -1, width))
-    out_ring = spin(total_low(after(out_ring, dq_two), out_terms[1]))
-    ffn_total = total_low(after(ffn_ring, dq_two), ffn_term(3)).reshape(2, 2, rows, -1)
-    g_down = total_low(after(down_ring, dq_two), down_term(3))
-
-    own_heads = jnp.pad(g_heads.reshape(-1, head_few), ((0, 0), (0, rows - head_few)))
-    g_gains = jnp.stack(
-        [
-            jnp.sum(attn_terms, 0).reshape(-1, rows),
-            jnp.sum(ffn_terms, 0).reshape(-1, rows),
-            own_heads,
-        ],
-        1,
-    )
-    g_gains = jnp.pad(g_gains, ((0, 0), (0, rows - 3), (0, 128 - rows))).reshape(-1, 128)
-    g_in = jnp.concatenate([g_in, g_gains.astype(low)], 1)
-    g_in = jnp.moveaxis(g_in.reshape(2, 2, 2, ctx_count, rows, inner), 3, 2)
-    in_terms = [squares(g_in, step) for step in range(ctx_count)]
-    in_ring = spin(in_terms[0])
-    out_ring = spin(total_low(out_ring, out_terms[2]))
-    in_ring = spin(total_low(in_ring, in_terms[1]))
-    g_out = total_low(out_ring, out_terms[3])
-    in_ring = spin(total_low(in_ring, in_terms[2]))
-
-    ffn_total = after(ffn_total, in_terms[3])
+    in_grad = (d_hidden + d_input).astype(low)
+    out_total = out_near + out_got.astype(full)
+    g_gains = jnp.concatenate([jnp.sum(attn_terms, 0), jnp.sum(ffn_terms, 0), g_heads.reshape(-1)])
+    g_gains = g_gains.reshape(-1, 128)
+    g_gains = jnp.pad(g_gains, ((0, 24 - g_gains.shape[0]), (0, 0)))
+    in_grad, early_got, g_gains = hold(in_grad, early_got, g_gains)
+    early_near, early_got = high_square(early_near, early_got)
+    g_gains = g_gains + flip(g_gains, CORE)
+    in_came, in_kept = unspread(in_grad.reshape(2, -1, width))
+    early_got, late_got, g_gains, unit_ring, far_got[2] = hold(
+        early_got, late_got, g_gains, unit_ring, far_got[2]
+    )
+    unit_total = total_low(unit_ring, total_low(near_terms[2], far_got[2]))
+    unit_ring = spin(unit_total)
+    late_near, late_got = high_square(late_near, late_got)
+    g_gains = g_gains + flip(g_gains, SIDE)
+    g_gains = (g_gains + flip(g_gains, HIGH)).reshape(-1)
+
+    def own_of(place):
+        which = dp * ctx_count + place
+        row = [
+            lax.dynamic_slice(g_gains, (start + which * count,), (count,))
+            for start, count in ((0, rows), (width, rows), (2 * width, head_few))
+        ]
+        row = jnp.concatenate(row)[None]
+        return jnp.pad(row, ((0, 15), (0, width - row.shape[1])))
+
+    def terms_of(near, got, first):
+        terms = near + got.astype(full)
+        return [
+            jnp.concatenate(
+                [
+                    terms[at].reshape(2 * rows, width),
+                    out_total[first + at],
+                    own_of(behind(first + at)),
+                ],
+                0,
+            )
+            for at in range(2)
+        ]
+
+    in_terms = terms_of(early_near, early_got, 0)
+    in_ring = spin(in_terms[0].astype(low))
+    in_ring, late_got = hold(in_ring, late_got)
+    in_terms += terms_of(late_near, late_got, 2)
+    in_ring = spin((in_ring.astype(full) + in_terms[1]).astype(low))
+    in_ring, unit_ring = hold(in_ring, unit_ring)
+    in_ring = spin((in_ring.astype(full) + in_terms[2]).astype(low))
+    in_ring, far_got[3], *in_came = hold(in_ring, far_got[3], *in_came)
+    unit_total = total_low(unit_ring, total_low(near_terms[3], far_got[3]))
+    ffn_total = jnp.concatenate(
+        [unit_total[: 4 * rows], unit_total[4 * rows : 8 * rows]], 1
+    ).reshape(2, 2, rows, -1)
+    g_down = unit_total[8 * rows :, :width]
+
     found = related(
         pick(pick(ffn_total, side), core),
         flip(pick(pick(ffn_total, side), 1 - core), CORE),
@@ -978,21 +1183,24 @@
         flip(pick(pick(ffn_total, 1 - side), 1 - core), SIDE | CORE),
     )
     found = (found[0], found[2], found[1], found[3])
-    blocks = w_gate.shape[1] // units // 4
 
     def to_columns(first):
         return jnp.concatenate(
             [
                 found[which][:, (first + top) * units : (first + top + 1) * units].astype(full)
-                for top in range(blocks)
+                for top in range(tops)
                 for which in range(4)
             ],
             1,
         )
 
-    g_gate, g_up = to_columns(0), to_columns(blocks)
-
-    g_in = total_low(in_ring, in_terms[3])
+    g_gate, g_up = to_columns(0), to_columns(tops)
+
+    in_sum = in_ring.astype(full) + in_terms[3]
+    g_in, g_out = in_sum[: 2 * rows].astype(low).reshape(2, rows, width), in_sum[2 * rows : 3 * rows]
+    g_gains = in_sum[3 * rows]
+    in_grad = order(ctx % 2, *settled(in_came, in_kept))
+    block_out = order(ctx % 2, *settled(block_came, block_kept))
     own = pick(g_in, core).astype(full)
     got = flip(pick(g_in, 1 - core), CORE).astype(full)
     even, odd = choose(core, own, got), choose(core, got, own)
@@ -1003,18 +1211,16 @@
             [part[:, at : at + size] for at in range(start, stop, step) for part in (even, odd)], 1
         )
 
-    g_gains = (own + got)[:, features:]
-
     return (
         block_out[:, None],
         in_grad[:, None],
-        g_gains[0, :rows],
-        g_gains[2, :head_few],
+        g_gains[:rows],
+        g_gains[2 * rows : 2 * rows + head_few],
         mixed(0, first, group * head, group * head),
         mixed(first, features, 2 * head, head),
         mixed(first + head, features, 2 * head, head),
-        g_out.astype(full),
-        g_gains[1, :rows],
+        g_out,
+        g_gains[rows : 2 * rows],
         g_gate,
         g_up,
         g_down.astype(full),

time: 582 us -> 509 us (0.87)
  matrix products: 96.6 us -> 34 us
  Pallas kernels: 35.3 us -> 96.5 us
  local copies, waits for them, and re-layouts: 77.7 us -> 41.2 us
  starting transfers between devices: 120 us -> 89.6 us
    pallas_call x0 -> x5, Pallas kernels: none -> 64 us  [the longest x2 58.7 us: feed_forward(): pl.pallas_call(functools.partial(unit_kernel, mid // 3, len(pieces) // 2,...]
    dot_general x5 -> x3, matrix products: 42.2 us -> 3.91 us  [right_trans(): lax.dot_general(left, right, (((1,), (1,)), ((), ())), preferred_element_...]
    ppermute x21 -> x12, waiting for transfers between devices: 51.4 us -> 77.1 us  [spin(): lax.ppermute(array, 'ctx', [(i, (i + 1) % count) for i in range(count)])]
    dynamic_update_slice x56 -> x14, local copies, waits for them, and re-layouts: 29.9 us -> 5.7 us  [put(): return lax.dynamic_update_slice(buffer, array.reshape(shape), index)]
    ppermute x10 -> x6, starting transfers between devices: 42.9 us -> 19.9 us  [exchange(): came.append(lax.ppermute(piece, ('dp', 'ctx'), pairs))]
    dot_general x3 -> x1, matrix products: 22.5 us -> 1.26 us  [matmul(): return jnp.dot(left, right, preferred_element_type=jnp.float32)]
    ppermute x10 -> x6, waiting for transfers between devices: 29.2 us -> 9.47 us  [exchange(): came.append(lax.ppermute(piece, ('dp', 'ctx'), pairs))]
    ppermute x68 -> x46, starting transfers between devices: 55.5 us -> 40.9 us  [flip(): return lax.ppermute(array, 'dp', [(i, i ^ bits) for i in range(count)])]
  transfers between devices with their start and end apart: 99 -> 64, of which waited for: 30 -> 24; matrix products, arithmetic and copies ran while one was open for 27% -> 17% of each run, Pallas kernels for 6% -> 13%
where the time goes in v2:
time: 509 us; the launch traced here: 502 us
  waiting for transfers between devices  189 us (37%)
  Pallas kernels  96.5 us (19%)
  starting transfers between devices  89.6 us (18%)
  other arithmetic  48.2 us (9%)
  local copies, waits for them, and re-layouts  41.2 us (8%)
  matrix products  34 us (7%)
    ppermute x46, waiting for transfers between devices, flip(): return lax.ppermute(array, 'dp', [(i, i ^ bits) for i in range(count)])  103 us
    ppermute x12, waiting for transfers between devices, spin(): lax.ppermute(array, 'ctx', [(i, (i + 1) % count) for i in range(count)])  77.1 us
    pallas_call x2, Pallas kernels, feed_forward(): pl.pallas_call(functools.partial(unit_kernel, mid // 3, len(pieces) // 2,...  58.7 us
    ppermute x46, starting transfers between devices, flip(): return lax.ppermute(array, 'dp', [(i, i ^ bits) for i in range(count)])  40.9 us
    ppermute x12, starting transfers between devices, spin(): lax.ppermute(array, 'ctx', [(i, (i + 1) % count) for i in range(count)])  28.8 us
    dot_general x5, matrix products, left_trans(): lax.dot_general(left, right, (((0,), (0,)), ((), ())), preferred_element_...  26.4 us
    pallas_call x1, Pallas kernels, attend_back(): pl.pallas_call(functools.partial(backward_kernel, block), grid=(count,),...  22.8 us
    ppermute x6, starting transfers between devices, exchange(): came.append(lax.ppermute(piece, ('dp', 'ctx'), pairs))  19.9 us
  transfers between devices with their start and end apart: 64, of which 24 were waited for; matrix products, arithmetic and copies ran while one was open for 17% of the time, Pallas kernels for 13%

profile of v2, /device:TPU:1, one launch (start us, length us, event | category | flops | bytes accessed | tf_op | source)
XLA Modules:
  0.0 502.1 jit_solution(8713079132026263931)
XLA Ops:
  11.2 2.8 collective-permute-start.1
  15.2 3.4 collective-permute-start.4
  18.6 2.3 collective-permute-start.5
  24.6 5.7 %collective-permute-done.13.side_ref = bf16[4,32,1152]{2,1,0:T(8,128)(2,1)S(1)} collective-permute-done((bf16[4,32,1152]{2,1,0:T(8,128)(2,1)}, bf16[4,32,1152]{2,1,0:T(8,128)(2,1)S(1)}, u32[]{:S(2)}, u32[]{:S(2)}) %collective-permute-start.13) | collective-permute-done | bytes 294944 | tf_op jit(solution)/shard_map/ppermute | solution.py:363
  31.6 27.3 %collective-permute-done.2 = bf16[3,32,1152]{2,1,0:T(8,128)(2,1)S(1)} collective-permute-done((bf16[3,32,1152]{2,1,0:T(8,128)(2,1)}, bf16[3,32,1152]{2,1,0:T(8,128)(2,1)S(1)}, u32[]{:S(2)}, u32[]{:S(2)}) %collective-permute-start.2) | collective-permute-done | bytes 221216 | tf_op jit(solution)/shard_map/ppermute | solution.py:368
  59.6 2.2 collective-permute-start.8
  61.8 1.6 pad_maximum_fusion.7.own_ref
  63.4 2.2 shard_map.230.refs_0_
  65.6 12.4 %collective-permute-start.3 = (bf16[3,32,1152]{2,1,0:T(8,128)(2,1)}, bf16[3,32,1152]{2,1,0:T(8,128)(2,1)S(1)}, u32[]{:S(2)}, u32[]{:S(2)}) collective-permute-start(bf16[3,32,1152]{2,1,0:T(8,128)(2,1)} %copy-done.71), channel_id=1, source_target_pairs={{0,1},{1,2},{2,3},{3,0},{4,5},{5,6},{6,7},{7,4},{8,9},{9,10},{10,1... | collective-permute-start | bytes 663560 | tf_op jit(solution)/shard_map/ppermute | solution.py:368
  79.0 2.1 collective-permute-start.14
  90.3 30.2 %collective-permute-done.10 = bf16[6,32,1152]{2,1,0:T(8,128)(2,1)S(1)} collective-permute-done((bf16[6,32,1152]{2,1,0:T(8,128)(2,1)S(1)}, bf16[6,32,1152]{2,1,0:T(8,128)(2,1)S(1)}, u32[]{:S(2)}, u32[]{:S(2)}) %collective-permute-start.10) | collective-permute-done | bytes 442400 | tf_op jit(solution)/shard_map/ppermute | solution.py:363
  120.8 2.9 collective-permute-start.19
  127.7 2.5 slice_convert_fusion
  130.8 3.9 collective-permute-start.16
  138.2 2.7 fusion.3
  141.1 2.4 fusion.21.q_ref.kv_ref
  143.6 9.7 %shard_map.231 = (f32[512,1024]{1,0:T(8,128)S(1)}, f32[4,2,1024]{2,1,0:T(2,128)S(1)}, bf16[512,1024]{1,0:T(8,128)(2,1)S(1)}, bf16[512,1024]{1,0:T(8,128)(2,1)S(1)}) custom-call(f32[1024,1024]{1,0:T(8,128)S(1)} %fusion.21.q_ref.kv_ref, f32[1024,1024]{1,0:T(8,128)S(1)} %fusion.21.q_ref.kv_ref, f32[32,1024]{1,0:T(8,128)S(1)} %get-tuple-element.407.cos_ref, ...), custom_call_target="tpu_custom_call" | custom-call | flops 1000000 | tf_op jit(solution)/shard_map/pallas_call | solution.py:787
  154.9 1.6 collective-permute-done.17.refs_3_
  157.3 1.6 collective-permute-start.21
  158.9 2.1 collective-permute-start.22
  162.9 2.3 fusion.37
  165.2 2.1 multiply_reduce_fusion.3
  169.0 14.0 %collective-permute-done.22.refs_6_ = bf16[400,1152]{1,0:T(8,128)(2,1)S(1)} collective-permute-done((bf16[400,1152]{1,0:T(8,128)(2,1)}, bf16[400,1152]{1,0:T(8,128)(2,1)S(1)}, u32[]{:S(2)}, u32[]{:S(2)}) %collective-permute-start.22) | collective-permute-done | bytes 921632 | tf_op jit(solution)/shard_map/ppermute | solution.py:368
  183.3 1.4 collective-permute-start.26
  185.9 20.9 %collective-permute-done.27.refs_7_ = bf16[400,1152]{1,0:T(8,128)(2,1)S(1)} collective-permute-done((bf16[400,1152]{1,0:T(8,128)(2,1)S(1)}, bf16[400,1152]{1,0:T(8,128)(2,1)S(1)}, u32[]{:S(2)}, u32[]{:S(2)}) %collective-permute-start.27) | collective-permute-done | bytes 921632 | tf_op jit(solution)/shard_map/ppermute | solution.py:363
  206.9 1.9 collective-permute-start.28
  208.9 2.5 collective-permute-done.28.refs_9_
  212.6 29.5 %shard_map.232 = (bf16[2048,1152]{1,0:T(8,128)(2,1)}, bf16[2048,2304]{1,0:T(8,128)(2,1)}, bf16[2048,1024]{1,0:T(8,128)(2,1)}, bf16[2048,1024]{1,0:T(8,128)(2,1)}...) custom-call(s32[5]{0:T(128)S(1)} %stack.304.slots_ref, ...), custom_call_target="tpu_custom_call" | custom-call | flops 6039797760 | tf_op jit(solution)/shard_map/pallas_call | solution.py:516
  242.6 2.5 collective-permute-done.29
  245.1 2.6 add_convert_fusion.2
  249.2 29.2 %shard_map.233 = (bf16[2048,1152]{1,0:T(8,128)(2,1)}, bf16[2048,2304]{1,0:T(8,128)(2,1)}, bf16[2048,1024]{1,0:T(8,128)(2,1)}, bf16[2048,1024]{1,0:T(8,128)(2,1)}...) custom-call(s32[5]{0:T(128)S(1)} %stack.304.slots_ref, ...), custom_call_target="tpu_custom_call", output_to_operand_aliasing={{0}: (13, {}), {1}: (14, {}), {2}: (15, {}), {3}: (16, {})} | custom-call | flops 6039797760 | tf_op jit(solution)/shard_map/pallas_call | solution.py:516
  279.1 1.8 add_convert_fusion.1
  280.9 8.6 %convolution_convert_fusion.1.down_ref = bf16[1152,1024]{1,0:T(8,128)(2,1)S(1)} fusion(bf16[2048,1152]{1,0:T(8,128)(2,1)} %get-tuple-element.180, bf16[2048,1024]{1,0:T(8,128)(2,1)} %get-tuple-element.181), kind=kOutput, calls=%fused_computation.9 | convolution fusion | flops 4833017856 | bytes 11272192 | tf_op jit(solution)/shard_map/dot_general | solution.py:19
  291.0 11.0 %convolution_convert_fusion.ffn_ref = bf16[1024,2304]{1,0:T(8,128)(2,1)S(1)} fusion(bf16[2048,1024]{1,0:T(8,128)(2,1)S(1)} %copy-done.48, bf16[2048,2304]{1,0:T(8,128)(2,1)S(1)} %bitcast.325), kind=kOutput, calls=%fused_computation.2 | convolution fusion | flops 9666035712 | bytes 18350080 | tf_op jit(solution)/shard_map/dot_general | solution.py:19
  301.9 2.3 shard_map.234
  304.3 9.7 %collective-permute-done.34 = bf16[512,1024]{1,0:T(8,128)(2,1)S(1)} collective-permute-done((bf16[512,1024]{1,0:T(8,128)(2,1)S(1)}, bf16[512,1024]{1,0:T(8,128)(2,1)S(1)}, u32[]{:S(2)}, u32[]{:S(2)}) %collective-permute-start.34) | collective-permute-done | bytes 1048608 | tf_op jit(solution)/shard_map/ppermute | solution.py:363
  314.0 1.8 convert_add_fusion.1
  316.1 1.4 copy-done.37
  318.8 4.5 fusion.68
  324.5 1.6 fusion.15
  327.4 2.1 collective-permute-start.37
  329.6 2.7 collective-permute-start.38
  334.0 1.4 bitcast_dynamic-update-slice_fusion.3
  340.6 9.5 %collective-permute-done.38 = bf16[256,1024]{1,0:T(8,128)(2,1)S(1)} collective-permute-done((bf16[256,1024]{1,0:T(8,128)(2,1)S(1)}, bf16[256,1024]{1,0:T(8,128)(2,1)S(1)}, u32[]{:S(2)}, u32[]{:S(2)}) %collective-permute-start.38) | collective-permute-done | bytes 524320 | tf_op jit(solution)/shard_map/ppermute | solution.py:608
  350.9 4.0 collective-permute-done.36
  361.1 22.8 %shard_map.235 = (bf16[1024,512]{1,0:T(8,128)(2,1)S(1)}, bf16[1024,512]{1,0:T(8,128)(2,1)S(1)}, f32[2,64,1]{2,1,0:T(8,128)S(1)}) custom-call(f32[1024,1024]{1,0:T(8,128)S(1)} %copy-done.1, f32[1024,1024]{1,0:T(8,128)S(1)} %copy-done.1, bf16[512,1024]{1,0:T(8,128)(2,1)S(1)} %copy-done.12, bf16[512,1024]{1,0:T(8,128)(2,1)S(1)} %copy-done.14, ...), custom_call_target="tpu_custom_call" | custom-call | flops 1000000 | tf_op jit(solution)/shard_map/pallas_call | solution.py:825
  390.1 1.9 add_convert_fusion.7
  397.0 2.4 convolution_convert_fusion.2
  399.9 2.3 collective-permute-start.42
  407.9 2.5 fusion.13
  410.4 5.6 %collective-permute-done.44 = bf16[2,2,2,32,1024]{4,3,2,1,0:T(8,128)(2,1)S(1)} collective-permute-done((bf16[2,2,2,32,1024]{4,3,2,1,0:T(8,128)(2,1)S(1)}, bf16[2,2,2,32,1024]{4,3,2,1,0:T(8,128)(2,1)S(1)}, u32[]{:S(2)}, u32[]{:S(2)}) %collective-permute-start.44) | collective-permute-done | bytes 524320 | tf_op jit(solution)/shard_map/ppermute | solution.py:363
  419.4 6.3 %collective-permute-start.58 = (bf16[256,1024]{1,0:T(8,128)(2,1)S(1)}, bf16[256,1024]{1,0:T(8,128)(2,1)S(1)}, u32[]{:S(2)}, u32[]{:S(2)}) collective-permute-start(bf16[256,1024]{1,0:T(8,128)(2,1)S(1)} %get-tuple-element.278), channel_id=1, source_target_pairs={{1,4},{2,1},{3,5},{4,2},{5,6},{6,3},{9,12},{10,9},{11,13},{12,10},... | collective-permute-start | bytes 1572872 | tf_op jit(solution)/shard_map/ppermute | solution.py:608
  425.7 1.6 collective-permute-done.46
  427.3 1.5 add_convert_fusion.5
  428.9 1.4 collective-permute-start.55
  430.8 2.3 collective-permute-done.50
  434.7 10.8 %collective-permute-done.51 = f32[24,128]{1,0:T(8,128)S(1)} collective-permute-done((f32[24,128]{1,0:T(8,128)S(1)}, f32[24,128]{1,0:T(8,128)S(1)}, u32[]{:S(2)}, u32[]{:S(2)}) %collective-permute-start.51) | collective-permute-done | bytes 12320 | tf_op jit(solution)/shard_map/ppermute | solution.py:363
  445.8 1.4 collective-permute-start.52
  447.6 9.8 %collective-permute-done.52 = bf16[112,1024]{1,0:T(8,128)(2,1)S(1)} collective-permute-done((bf16[112,1024]{1,0:T(8,128)(2,1)S(1)}, bf16[112,1024]{1,0:T(8,128)(2,1)S(1)}, u32[]{:S(2)}, u32[]{:S(2)}) %collective-permute-start.52) | collective-permute-done | bytes 229408 | tf_op jit(solution)/shard_map/ppermute | solution.py:368
  457.3 2.9 collective-permute-start.59
  460.3 1.7 collective-permute-start.54
  462.2 16.3 %collective-permute-done.54 = bf16[112,1024]{1,0:T(8,128)(2,1)S(1)} collective-permute-done((bf16[112,1024]{1,0:T(8,128)(2,1)S(1)}, bf16[112,1024]{1,0:T(8,128)(2,1)S(1)}, u32[]{:S(2)}, u32[]{:S(2)}) %collective-permute-start.54) | collective-permute-done | bytes 229408 | tf_op jit(solution)/shard_map/ppermute | solution.py:368
  479.1 7.9 %collective-permute-done.56 = bf16[112,1024]{1,0:T(8,128)(2,1)S(1)} collective-permute-done((bf16[112,1024]{1,0:T(8,128)(2,1)S(1)}, bf16[112,1024]{1,0:T(8,128)(2,1)S(1)}, u32[]{:S(2)}, u32[]{:S(2)}) %collective-permute-start.56) | collective-permute-done | bytes 229408 | tf_op jit(solution)/shard_map/ppermute | solution.py:368
  495.7 3.4 collective-permute-done.63
  (459 shorter events, 101.2 us)
Async XLA Ops:
  7.8 2.1 collective-permute-start
  11.2 11.1 %collective-permute-start.1 = (bf16[3,32,1152]{2,1,0:T(8,128)(2,1)S(1)}, bf16[3,32,1152]{2,1,0:T(8,128)(2,1)}, u32[]{:S(2)}, u32[]{:S(2)}) collective-permute-start(bf16[3,32,1152]{2,1,0:T(8,128)(2,1)S(1)} %bitcast_dynamic-update-slice_fusion.10), channel_id=1, source_target_pairs={{0,1},{1,2},{2,3},{3,0},{4,5},{5,6},{6,7},{7,4},{8,9},{9,10},{10,1... | collective-permute-start | bytes 663560 | tf_op jit(solution)/shard_map/ppermute | solution.py:368
  15.2 66.8 %collective-permute-start.4 = (bf16[528,1024]{1,0:T(8,128)(2,1)S(1)}, bf16[528,1024]{1,0:T(8,128)(2,1)}, u32[]{:S(2)}, u32[]{:S(2)}) collective-permute-start(bf16[528,1024]{1,0:T(8,128)(2,1)S(1)} %get-tuple-element.264), channel_id=1, source_target_pairs={{1,2},{2,4},{3,6},{4,1},{5,3},{6,5},{9,10},{10,12},{11,14},{12,9},... | collective-permute-start | bytes 3244040 | tf_op jit(solution)/shard_map/ppermute | solution.py:608
  18.6 63.3 %collective-permute-start.5 = (bf16[528,1024]{1,0:T(8,128)(2,1)}, bf16[528,1024]{1,0:T(8,128)(2,1)S(1)}, u32[]{:S(2)}, u32[]{:S(2)}) collective-permute-start(bf16[528,1024]{1,0:T(8,128)(2,1)} %get-tuple-element.263), channel_id=1, source_target_pairs={{0,2},{1,0},{2,6},{3,4},{4,3},{5,1},{6,7},{7,5},{8,10},{9,8},{10,1... | collective-permute-start | bytes 3244040 | tf_op jit(solution)/shard_map/ppermute | solution.py:608
  21.0 9.3 %collective-permute-start.13 = (bf16[4,32,1152]{2,1,0:T(8,128)(2,1)}, bf16[4,32,1152]{2,1,0:T(8,128)(2,1)S(1)}, u32[]{:S(2)}, u32[]{:S(2)}) collective-permute-start(bf16[4,32,1152]{2,1,0:T(8,128)(2,1)} %get-tuple-element.334), channel_id=1, source_target_pairs={{0,8},{4,12},{8,0},{12,4},{16,24},{20,28},{24,16},{28,20},{1,9},{5... | collective-permute-start | bytes 884744 | tf_op jit(solution)/shard_map/ppermute | solution.py:363
  23.3 42.3 %collective-permute-start.6 = (bf16[6,32,1152]{2,1,0:T(8,128)(2,1)S(1)}, bf16[6,32,1152]{2,1,0:T(8,128)(2,1)S(1)}, u32[]{:S(2)}, u32[]{:S(2)}) collective-permute-start(bf16[6,32,1152]{2,1,0:T(8,128)(2,1)S(1)} %pad_maximum_fusion.6), channel_id=1, source_target_pairs={{0,8},{4,12},{8,0},{12,4},{16,24},{20,28},{24,16},{28,20},{1,9},{5... | collective-permute-start | bytes 1327112 | tf_op jit(solution)/shard_map/ppermute | solution.py:363
  24.0 34.9 %collective-permute-start.2 = (bf16[3,32,1152]{2,1,0:T(8,128)(2,1)}, bf16[3,32,1152]{2,1,0:T(8,128)(2,1)S(1)}, u32[]{:S(2)}, u32[]{:S(2)}) collective-permute-start(bf16[3,32,1152]{2,1,0:T(8,128)(2,1)} %collective-permute-done.1), channel_id=1, source_target_pairs={{0,1},{1,2},{2,3},{3,0},{4,5},{5,6},{6,7},{7,4},{8,9},{9,10},{10,1... | collective-permute-start | bytes 663560 | tf_op jit(solution)/shard_map/ppermute | solution.py:368
  30.3 48.6 %collective-permute-start.7 = (bf16[6,32,1152]{2,1,0:T(8,128)(2,1)S(1)}, bf16[6,32,1152]{2,1,0:T(8,128)(2,1)S(1)}, u32[]{:S(2)}, u32[]{:S(2)}) collective-permute-start(bf16[6,32,1152]{2,1,0:T(8,128)(2,1)S(1)} %pad_maximum_fusion.6), channel_id=1, source_target_pairs={{0,16},{4,20},{8,24},{12,28},{16,0},{20,4},{24,8},{28,12},{1,17},{... | collective-permute-start | bytes 1327112 | tf_op jit(solution)/shard_map/ppermute | solution.py:363
  59.6 21.5 %collective-permute-start.8 = (bf16[6,32,1152]{2,1,0:T(8,128)(2,1)S(1)}, bf16[6,32,1152]{2,1,0:T(8,128)(2,1)}, u32[]{:S(2)}, u32[]{:S(2)}) collective-permute-start(bf16[6,32,1152]{2,1,0:T(8,128)(2,1)S(1)} %pad_maximum_fusion.6), channel_id=1, source_target_pairs={{0,24},{4,28},{8,16},{12,20},{16,8},{20,12},{24,0},{28,4},{1,25},{... | collective-permute-start | bytes 1327112 | tf_op jit(solution)/shard_map/ppermute | solution.py:363
  65.6 16.3 %collective-permute-start.3 = (bf16[3,32,1152]{2,1,0:T(8,128)(2,1)}, bf16[3,32,1152]{2,1,0:T(8,128)(2,1)S(1)}, u32[]{:S(2)}, u32[]{:S(2)}) collective-permute-start(bf16[3,32,1152]{2,1,0:T(8,128)(2,1)} %copy-done.71), channel_id=1, source_target_pairs={{0,1},{1,2},{2,3},{3,0},{4,5},{5,6},{6,7},{7,4},{8,9},{9,10},{10,1... | collective-permute-start | bytes 663560 | tf_op jit(solution)/shard_map/ppermute | solution.py:368
  79.0 47.5 %collective-permute-start.14 = (bf16[400,1152]{1,0:T(8,128)(2,1)}, bf16[400,1152]{1,0:T(8,128)(2,1)S(1)}, u32[]{:S(2)}, u32[]{:S(2)}) collective-permute-start(bf16[400,1152]{1,0:T(8,128)(2,1)} %shard_map.230.refs_0_), channel_id=1, source_target_pairs={{0,1},{1,2},{2,3},{3,0},{4,5},{5,6},{6,7},{7,4},{8,9},{9,10},{10,1... | collective-permute-start | bytes 2764808 | tf_op jit(solution)/shard_map/ppermute | solution.py:368
  81.1 45.3 %collective-permute-start.15 = (bf16[400,1152]{1,0:T(8,128)(2,1)}, bf16[400,1152]{1,0:T(8,128)(2,1)S(1)}, u32[]{:S(2)}, u32[]{:S(2)}) collective-permute-start(bf16[400,1152]{1,0:T(8,128)(2,1)} %shard_map.230.refs_0_), channel_id=1, source_target_pairs={{0,16},{4,20},{8,24},{12,28},{16,0},{20,4},{24,8},{28,12},{1,17},{... | collective-permute-start | bytes 2764808 | tf_op jit(solution)/shard_map/ppermute | solution.py:363
  82.0 38.6 %collective-permute-start.10 = (bf16[6,32,1152]{2,1,0:T(8,128)(2,1)S(1)}, bf16[6,32,1152]{2,1,0:T(8,128)(2,1)S(1)}, u32[]{:S(2)}, u32[]{:S(2)}) collective-permute-start(bf16[6,32,1152]{2,1,0:T(8,128)(2,1)S(1)} %constant_dynamic-update-slice_fusion), channel_id=1, source_target_pairs={{0,16},{4,20},{8,24},{12,28},{16,0},{20,4},{24,8},{28,12},{1,17},{... | collective-permute-start | bytes 1327112 | tf_op jit(solution)/shard_map/ppermute | solution.py:363
  82.7 38.1 %collective-permute-start.11 = (bf16[6,32,1152]{2,1,0:T(8,128)(2,1)S(1)}, bf16[6,32,1152]{2,1,0:T(8,128)(2,1)S(1)}, u32[]{:S(2)}, u32[]{:S(2)}) collective-permute-start(bf16[6,32,1152]{2,1,0:T(8,128)(2,1)S(1)} %constant_dynamic-update-slice_fusion), channel_id=1, source_target_pairs={{0,24},{4,28},{8,16},{12,20},{16,8},{20,12},{24,0},{28,4},{1,25},{... | collective-permute-start | bytes 1327112 | tf_op jit(solution)/shard_map/ppermute | solution.py:363
  83.5 40.3 %collective-permute-start.9 = (bf16[6,32,1152]{2,1,0:T(8,128)(2,1)S(1)}, bf16[6,32,1152]{2,1,0:T(8,128)(2,1)S(1)}, u32[]{:S(2)}, u32[]{:S(2)}) collective-permute-start(bf16[6,32,1152]{2,1,0:T(8,128)(2,1)S(1)} %constant_dynamic-update-slice_fusion), channel_id=1, source_target_pairs={{0,8},{4,12},{8,0},{12,4},{16,24},{20,28},{24,16},{28,20},{1,9},{5... | collective-permute-start | bytes 1327112 | tf_op jit(solution)/shard_map/ppermute | solution.py:363
  120.6 32.9 %collective-permute-start.18 = (bf16[512,1024]{1,0:T(8,128)(2,1)}, bf16[512,1024]{1,0:T(8,128)(2,1)}, u32[]{:S(2)}, u32[]{:S(2)}) collective-permute-start(bf16[512,1024]{1,0:T(8,128)(2,1)} %bitcast.91.refs_10_), channel_id=1, source_target_pairs={{0,8},{4,12},{8,0},{12,4},{16,24},{20,28},{24,16},{28,20},{1,9},{5... | collective-permute-start | bytes 3145736 | tf_op jit(solution)/shard_map/ppermute | solution.py:363
  120.8 32.7 %collective-permute-start.19 = (bf16[512,1024]{1,0:T(8,128)(2,1)}, bf16[512,1024]{1,0:T(8,128)(2,1)}, u32[]{:S(2)}, u32[]{:S(2)}) collective-permute-start(bf16[512,1024]{1,0:T(8,128)(2,1)} %bitcast.91.refs_10_), channel_id=1, source_target_pairs={{0,4},{4,0},{8,12},{12,8},{16,20},{20,16},{24,28},{28,24},{1,5},{5... | collective-permute-start | bytes 3145736 | tf_op jit(solution)/shard_map/ppermute | solution.py:363
  123.7 3.9 collective-permute-start.12
  130.8 24.0 %collective-permute-start.16 = (bf16[400,1152]{1,0:T(8,128)(2,1)}, bf16[400,1152]{1,0:T(8,128)(2,1)}, u32[]{:S(2)}, u32[]{:S(2)}) collective-permute-start(bf16[400,1152]{1,0:T(8,128)(2,1)} %copy-done.62), channel_id=1, source_target_pairs={{0,1},{1,2},{2,3},{3,0},{4,5},{5,6},{6,7},{7,4},{8,9},{9,10},{10,1... | collective-permute-start | bytes 2764808 | tf_op jit(solution)/shard_map/ppermute | solution.py:368
  134.8 21.6 %collective-permute-start.17 = (bf16[400,1152]{1,0:T(8,128)(2,1)}, bf16[400,1152]{1,0:T(8,128)(2,1)}, u32[]{:S(2)}, u32[]{:S(2)}) collective-permute-start(bf16[400,1152]{1,0:T(8,128)(2,1)} %copy-done.62), channel_id=1, source_target_pairs={{0,16},{4,20},{8,24},{12,28},{16,0},{20,4},{24,8},{28,12},{1,17},{... | collective-permute-start | bytes 2764808 | tf_op jit(solution)/shard_map/ppermute | solution.py:363
  136.5 19.9 %collective-permute-start.20 = (bf16[512,1024]{1,0:T(8,128)(2,1)}, bf16[512,1024]{1,0:T(8,128)(2,1)}, u32[]{:S(2)}, u32[]{:S(2)}) collective-permute-start(bf16[512,1024]{1,0:T(8,128)(2,1)} %slice.537), channel_id=1, source_target_pairs={{0,4},{4,0},{8,12},{12,8},{16,20},{20,16},{24,28},{28,24},{1,5},{5... | collective-permute-start | bytes 3145736 | tf_op jit(solution)/shard_map/ppermute | solution.py:363
  157.3 7.9 %collective-permute-start.21 = (bf16[512,512]{1,0:T(8,128)(2,1)}, bf16[512,512]{1,0:T(8,128)(2,1)S(1)}, u32[]{:S(2)}, u32[]{:S(2)}) collective-permute-start(bf16[512,512]{1,0:T(8,128)(2,1)} %broadcast_select_fusion.7), channel_id=1, source_target_pairs={{0,4},{4,0},{8,12},{12,8},{16,20},{20,16},{24,28},{28,24},{1,5},{5... | collective-permute-start | bytes 1572872 | tf_op jit(solution)/shard_map/ppermute | solution.py:363
  158.9 24.0 %collective-permute-start.22 = (bf16[400,1152]{1,0:T(8,128)(2,1)}, bf16[400,1152]{1,0:T(8,128)(2,1)S(1)}, u32[]{:S(2)}, u32[]{:S(2)}) collective-permute-start(bf16[400,1152]{1,0:T(8,128)(2,1)} %collective-permute-done.16.refs_4_), channel_id=1, source_target_pairs={{0,1},{1,2},{2,3},{3,0},{4,5},{5,6},{6,7},{7,4},{8,9},{9,10},{10,1... | collective-permute-start | bytes 2764808 | tf_op jit(solution)/shard_map/ppermute | solution.py:368
  161.0 22.0 %collective-permute-start.23 = (bf16[400,1152]{1,0:T(8,128)(2,1)}, bf16[400,1152]{1,0:T(8,128)(2,1)S(1)}, u32[]{:S(2)}, u32[]{:S(2)}) collective-permute-start(bf16[400,1152]{1,0:T(8,128)(2,1)} %collective-permute-done.16.refs_4_), channel_id=1, source_target_pairs={{0,16},{4,20},{8,24},{12,28},{16,0},{20,4},{24,8},{28,12},{1,17},{... | collective-permute-start | bytes 2764808 | tf_op jit(solution)/shard_map/ppermute | solution.py:363
  162.3 20.7 %collective-permute-start.24 = (bf16[512,1024]{1,0:T(8,128)(2,1)}, bf16[512,1024]{1,0:T(8,128)(2,1)S(1)}, u32[]{:S(2)}, u32[]{:S(2)}) collective-permute-start(bf16[512,1024]{1,0:T(8,128)(2,1)} %collective-permute-done.18.refs_10_), channel_id=1, source_target_pairs={{0,4},{4,0},{8,12},{12,8},{16,20},{20,16},{24,28},{28,24},{1,5},{5... | collective-permute-start | bytes 3145736 | tf_op jit(solution)/shard_map/ppermute | solution.py:363
  183.0 23.9 %collective-permute-start.25 = (bf16[512,1024]{1,0:T(8,128)(2,1)S(1)}, bf16[512,1024]{1,0:T(8,128)(2,1)}, u32[]{:S(2)}, u32[]{:S(2)}) collective-permute-start(bf16[512,1024]{1,0:T(8,128)(2,1)S(1)} %maximum_select_fusion.1.refs_8_), channel_id=1, source_target_pairs={{0,8},{4,12},{8,0},{12,4},{16,24},{20,28},{24,16},{28,20},{1,9},{5... | collective-permute-start | bytes 3145736 | tf_op jit(solution)/shard_map/ppermute | solution.py:363
  183.3 23.6 %collective-permute-start.26 = (bf16[512,1024]{1,0:T(8,128)(2,1)S(1)}, bf16[512,1024]{1,0:T(8,128)(2,1)S(1)}, u32[]{:S(2)}, u32[]{:S(2)}) collective-permute-start(bf16[512,1024]{1,0:T(8,128)(2,1)S(1)} %maximum_select_fusion.1.refs_8_), channel_id=1, source_target_pairs={{0,4},{4,0},{8,12},{12,8},{16,20},{20,16},{24,28},{28,24},{1,5},{5... | collective-permute-start | bytes 3145736 | tf_op jit(solution)/shard_map/ppermute | solution.py:363
  184.7 22.2 %collective-permute-start.27 = (bf16[400,1152]{1,0:T(8,128)(2,1)S(1)}, bf16[400,1152]{1,0:T(8,128)(2,1)S(1)}, u32[]{:S(2)}, u32[]{:S(2)}) collective-permute-start(bf16[400,1152]{1,0:T(8,128)(2,1)S(1)} %collective-permute-done.22.refs_6_), channel_id=1, source_target_pairs={{0,16},{4,20},{8,24},{12,28},{16,0},{20,4},{24,8},{28,12},{1,17},{... | collective-permute-start | bytes 2764808 | tf_op jit(solution)/shard_map/ppermute | solution.py:363
  206.9 4.5 collective-permute-start.28
  242.0 3.0 collective-permute-start.29
  242.5 5.2 %collective-permute-start.30 = (bf16[512,1024]{1,0:T(8,128)(2,1)}, bf16[512,1024]{1,0:T(8,128)(2,1)}, u32[]{:S(2)}, u32[]{:S(2)}) collective-permute-start(bf16[512,1024]{1,0:T(8,128)(2,1)} %get-tuple-element.165), channel_id=1, source_target_pairs={{0,4},{4,0},{8,12},{12,8},{16,20},{20,16},{24,28},{28,24},{1,5},{5... | collective-permute-start | bytes 3145736 | tf_op jit(solution)/shard_map/ppermute | solution.py:363
  247.7 33.2 %collective-permute-start.31 = (bf16[512,1024]{1,0:T(8,128)(2,1)}, bf16[512,1024]{1,0:T(8,128)(2,1)}, u32[]{:S(2)}, u32[]{:S(2)}) collective-permute-start(bf16[512,1024]{1,0:T(8,128)(2,1)} %add_convert_fusion.2), channel_id=1, source_target_pairs={{0,8},{4,12},{8,0},{12,4},{16,24},{20,28},{24,16},{28,20},{1,9},{5... | collective-permute-start | bytes 3145736 | tf_op jit(solution)/shard_map/ppermute | solution.py:363
  278.4 25.9 %collective-permute-start.33 = (bf16[512,1024]{1,0:T(8,128)(2,1)}, bf16[512,1024]{1,0:T(8,128)(2,1)S(1)}, u32[]{:S(2)}, u32[]{:S(2)}) collective-permute-start(bf16[512,1024]{1,0:T(8,128)(2,1)} %get-tuple-element.195), channel_id=1, source_target_pairs={{0,4},{4,0},{8,12},{12,8},{16,20},{20,16},{24,28},{28,24},{1,5},{5... | collective-permute-start | bytes 3145736 | tf_op jit(solution)/shard_map/ppermute | solution.py:363
  289.6 14.7 %collective-permute-start.32 = (bf16[512,1024]{1,0:T(8,128)(2,1)S(1)}, bf16[512,1024]{1,0:T(8,128)(2,1)S(1)}, u32[]{:S(2)}, u32[]{:S(2)}) collective-permute-start(bf16[512,1024]{1,0:T(8,128)(2,1)S(1)} %copy-done.89), channel_id=1, source_target_pairs={{0,4},{4,0},{8,12},{12,8},{16,20},{20,16},{24,28},{28,24},{1,5},{5... | collective-permute-start | bytes 3145736 | tf_op jit(solution)/shard_map/ppermute | solution.py:363
  289.7 24.4 %collective-permute-start.34 = (bf16[512,1024]{1,0:T(8,128)(2,1)S(1)}, bf16[512,1024]{1,0:T(8,128)(2,1)S(1)}, u32[]{:S(2)}, u32[]{:S(2)}) collective-permute-start(bf16[512,1024]{1,0:T(8,128)(2,1)S(1)} %add_convert_fusion.1), channel_id=1, source_target_pairs={{0,8},{4,12},{8,0},{12,4},{16,24},{20,28},{24,16},{28,20},{1,9},{5... | collective-permute-start | bytes 3145736 | tf_op jit(solution)/shard_map/ppermute | solution.py:363
  323.3 12.2 %collective-permute-start.35 = (bf16[512,1024]{1,0:T(8,128)(2,1)}, bf16[512,1024]{1,0:T(8,128)(2,1)}, u32[]{:S(2)}, u32[]{:S(2)}) collective-permute-start(bf16[512,1024]{1,0:T(8,128)(2,1)} %get-tuple-element.273), channel_id=1, source_target_pairs={{0,4},{4,0},{8,12},{12,8},{16,20},{20,16},{24,28},{28,24},{1,5},{5... | collective-permute-start | bytes 3145736 | tf_op jit(solution)/shard_map/ppermute | solution.py:363
  327.4 13.2 %collective-permute-start.37 = (bf16[256,1024]{1,0:T(8,128)(2,1)S(1)}, bf16[256,1024]{1,0:T(8,128)(2,1)S(1)}, u32[]{:S(2)}, u32[]{:S(2)}) collective-permute-start(bf16[256,1024]{1,0:T(8,128)(2,1)S(1)} %get-tuple-element.282), channel_id=1, source_target_pairs={{1,4},{2,1},{3,5},{4,2},{5,6},{6,3},{9,12},{10,9},{11,13},{12,10},... | collective-permute-start | bytes 1572872 | tf_op jit(solution)/shard_map/ppermute | solution.py:608
  329.6 20.5 %collective-permute-start.38 = (bf16[256,1024]{1,0:T(8,128)(2,1)S(1)}, bf16[256,1024]{1,0:T(8,128)(2,1)S(1)}, u32[]{:S(2)}, u32[]{:S(2)}) collective-permute-start(bf16[256,1024]{1,0:T(8,128)(2,1)S(1)} %get-tuple-element.281), channel_id=1, source_target_pairs={{0,1},{1,5},{2,0},{3,4},{4,3},{5,7},{6,2},{7,6},{8,9},{9,13},{10,8... | collective-permute-start | bytes 1572872 | tf_op jit(solution)/shard_map/ppermute | solution.py:608
  332.3 22.6 %collective-permute-start.36 = (bf16[400,1152]{1,0:T(8,128)(2,1)S(1)}, bf16[400,1152]{1,0:T(8,128)(2,1)S(1)}, u32[]{:S(2)}, u32[]{:S(2)}) collective-permute-start(bf16[400,1152]{1,0:T(8,128)(2,1)S(1)} %copy-done.35), channel_id=1, source_target_pairs={{0,16},{4,20},{8,24},{12,28},{16,0},{20,4},{24,8},{28,12},{1,17},{... | collective-permute-start | bytes 2764808 | tf_op jit(solution)/shard_map/ppermute | solution.py:363
  333.6 56.5 %collective-permute-start.41 = (bf16[400,1152]{1,0:T(8,128)(2,1)}, bf16[400,1152]{1,0:T(8,128)(2,1)}, u32[]{:S(2)}, u32[]{:S(2)}) collective-permute-start(bf16[400,1152]{1,0:T(8,128)(2,1)} %get-tuple-element.215), channel_id=1, source_target_pairs={{0,16},{4,20},{8,24},{12,28},{16,0},{20,4},{24,8},{28,12},{1,17},{... | collective-permute-start | bytes 2764808 | tf_op jit(solution)/shard_map/ppermute | solution.py:363
  356.0 34.1 %collective-permute-start.40 = (bf16[400,1152]{1,0:T(8,128)(2,1)}, bf16[400,1152]{1,0:T(8,128)(2,1)}, u32[]{:S(2)}, u32[]{:S(2)}) collective-permute-start(bf16[400,1152]{1,0:T(8,128)(2,1)} %add_convert_fusion.9), channel_id=1, source_target_pairs={{0,1},{1,2},{2,3},{3,0},{4,5},{5,6},{6,7},{7,4},{8,9},{9,10},{10,1... | collective-permute-start | bytes 2764808 | tf_op jit(solution)/shard_map/ppermute | solution.py:368
  357.9 32.2 %collective-permute-start.39 = (bf16[2,4,32,1024]{3,2,1,0:T(8,128)(2,1)}, bf16[2,4,32,1024]{3,2,1,0:T(8,128)(2,1)}, u32[]{:S(2)}, u32[]{:S(2)}) collective-permute-start(bf16[2,4,32,1024]{3,2,1,0:T(8,128)(2,1)} %pad_maximum_fusion.3), channel_id=1, source_target_pairs={{0,8},{4,12},{8,0},{12,4},{16,24},{20,28},{24,16},{28,20},{1,9},{5... | collective-permute-start | bytes 1572872 | tf_op jit(solution)/shard_map/ppermute | solution.py:363
  359.7 59.7 %collective-permute-start.49 = (bf16[400,1152]{1,0:T(8,128)(2,1)}, bf16[400,1152]{1,0:T(8,128)(2,1)}, u32[]{:S(2)}, u32[]{:S(2)}) collective-permute-start(bf16[400,1152]{1,0:T(8,128)(2,1)} %get-tuple-element.232), channel_id=1, source_target_pairs={{0,16},{4,20},{8,24},{12,28},{16,0},{20,4},{24,8},{28,12},{1,17},{... | collective-permute-start | bytes 2764808 | tf_op jit(solution)/shard_map/ppermute | solution.py:363
  392.0 35.3 %collective-permute-start.48 = (bf16[400,1152]{1,0:T(8,128)(2,1)S(1)}, bf16[400,1152]{1,0:T(8,128)(2,1)S(1)}, u32[]{:S(2)}, u32[]{:S(2)}) collective-permute-start(bf16[400,1152]{1,0:T(8,128)(2,1)S(1)} %add_convert_fusion.7), channel_id=1, source_target_pairs={{0,1},{1,2},{2,3},{3,0},{4,5},{5,6},{6,7},{7,4},{8,9},{9,10},{10,1... | collective-permute-start | bytes 2764808 | tf_op jit(solution)/shard_map/ppermute | solution.py:368
  393.7 10.7 %collective-permute-start.43 = (bf16[4,32,1024]{2,1,0:T(8,128)(2,1)S(1)}, bf16[4,32,1024]{2,1,0:T(8,128)(2,1)S(1)}, u32[]{:S(2)}, u32[]{:S(2)}) collective-permute-start(bf16[4,32,1024]{2,1,0:T(8,128)(2,1)S(1)} %fusion.48), channel_id=1, source_target_pairs={{0,16},{4,20},{8,24},{12,28},{16,0},{20,4},{24,8},{28,12},{1,17},{... | collective-permute-start | bytes 786440 | tf_op jit(solution)/shard_map/ppermute | solution.py:363
  399.9 5.7 %collective-permute-start.42 = (bf16[512,1024]{1,0:T(8,128)(2,1)S(1)}, bf16[512,1024]{1,0:T(8,128)(2,1)S(1)}, u32[]{:S(2)}, u32[]{:S(2)}) collective-permute-start(bf16[512,1024]{1,0:T(8,128)(2,1)S(1)} %fusion.23), channel_id=1, source_target_pairs={{0,4},{4,0},{8,12},{12,8},{16,20},{20,16},{24,28},{28,24},{1,5},{5... | collective-permute-start | bytes 3145736 | tf_op jit(solution)/shard_map/ppermute | solution.py:363
  402.5 13.6 %collective-permute-start.44 = (bf16[2,2,2,32,1024]{4,3,2,1,0:T(8,128)(2,1)S(1)}, bf16[2,2,2,32,1024]{4,3,2,1,0:T(8,128)(2,1)S(1)}, u32[]{:S(2)}, u32[]{:S(2)}) collective-permute-start(bf16[2,2,2,32,1024]{4,3,2,1,0:T(8,128)(2,1)S(1)} %pad_maximum_fusion.4), channel_id=1, source_target_pairs={{0,8},{4,12},{8,0},{12,4},{16,24},{20,28},{24,16},{28,20},{1,9},{5... | collective-permute-start | bytes 1572872 | tf_op jit(solution)/shard_map/ppermute | solution.py:363
  404.4 22.9 %collective-permute-start.46 = (bf16[2,2,2,32,1024]{4,3,2,1,0:T(8,128)(2,1)S(1)}, bf16[2,2,2,32,1024]{4,3,2,1,0:T(8,128)(2,1)S(1)}, u32[]{:S(2)}, u32[]{:S(2)}) collective-permute-start(bf16[2,2,2,32,1024]{4,3,2,1,0:T(8,128)(2,1)S(1)} %pad_maximum_fusion.5), channel_id=1, source_target_pairs={{0,8},{4,12},{8,0},{12,4},{16,24},{20,28},{24,16},{28,20},{1,9},{5... | collective-permute-start | bytes 1572872 | tf_op jit(solution)/shard_map/ppermute | solution.py:363
  416.1 2.2 collective-permute-start.47
  417.5 9.8 %collective-permute-start.45 = (bf16[2,2,32,1024]{3,2,1,0:T(8,128)(2,1)S(1)}, bf16[2,2,32,1024]{3,2,1,0:T(8,128)(2,1)S(1)}, u32[]{:S(2)}, u32[]{:S(2)}) collective-permute-start(bf16[2,2,32,1024]{3,2,1,0:T(8,128)(2,1)S(1)} %fusion.49), channel_id=1, source_target_pairs={{0,16},{4,20},{8,24},{12,28},{16,0},{20,4},{24,8},{28,12},{1,17},{... | collective-permute-start | bytes 786440 | tf_op jit(solution)/shard_map/ppermute | solution.py:363
  418.7 60.4 %collective-permute-start.57 = (bf16[400,1152]{1,0:T(8,128)(2,1)S(1)}, bf16[400,1152]{1,0:T(8,128)(2,1)S(1)}, u32[]{:S(2)}, u32[]{:S(2)}) collective-permute-start(bf16[400,1152]{1,0:T(8,128)(2,1)S(1)} %copy-done.33), channel_id=1, source_target_pairs={{0,16},{4,20},{8,24},{12,28},{16,0},{20,4},{24,8},{28,12},{1,17},{... | collective-permute-start | bytes 2764808 | tf_op jit(solution)/shard_map/ppermute | solution.py:363
  419.4 59.8 %collective-permute-start.58 = (bf16[256,1024]{1,0:T(8,128)(2,1)S(1)}, bf16[256,1024]{1,0:T(8,128)(2,1)S(1)}, u32[]{:S(2)}, u32[]{:S(2)}) collective-permute-start(bf16[256,1024]{1,0:T(8,128)(2,1)S(1)} %get-tuple-element.278), channel_id=1, source_target_pairs={{1,4},{2,1},{3,5},{4,2},{5,6},{6,3},{9,12},{10,9},{11,13},{12,10},... | collective-permute-start | bytes 1572872 | tf_op jit(solution)/shard_map/ppermute | solution.py:608
  428.9 49.6 %collective-permute-start.55 = (bf16[400,1152]{1,0:T(8,128)(2,1)S(1)}, bf16[400,1152]{1,0:T(8,128)(2,1)S(1)}, u32[]{:S(2)}, u32[]{:S(2)}) collective-permute-start(bf16[400,1152]{1,0:T(8,128)(2,1)S(1)} %add_convert_fusion.5), channel_id=1, source_target_pairs={{0,1},{1,2},{2,3},{3,0},{4,5},{5,6},{6,7},{7,4},{8,9},{9,10},{10,1... | collective-permute-start | bytes 2764808 | tf_op jit(solution)/shard_map/ppermute | solution.py:368
  430.3 2.8 collective-permute-start.50
  433.1 12.4 %collective-permute-start.51 = (f32[24,128]{1,0:T(8,128)S(1)}, f32[24,128]{1,0:T(8,128)S(1)}, u32[]{:S(2)}, u32[]{:S(2)}) collective-permute-start(f32[24,128]{1,0:T(8,128)S(1)} %add.770), channel_id=1, source_target_pairs={{0,16},{4,20},{8,24},{12,28},{16,0},{20,4},{24,8},{28,12},{1,17},{... | collective-permute-start | bytes 36872 | tf_op jit(solution)/shard_map/ppermute | solution.py:363
  433.6 26.6 %collective-permute-start.53 = (bf16[2,2,32,1024]{3,2,1,0:T(8,128)(2,1)S(1)}, bf16[2,2,32,1024]{3,2,1,0:T(8,128)(2,1)S(1)}, u32[]{:S(2)}, u32[]{:S(2)}) collective-permute-start(bf16[2,2,32,1024]{3,2,1,0:T(8,128)(2,1)S(1)} %fusion.50), channel_id=1, source_target_pairs={{0,16},{4,20},{8,24},{12,28},{16,0},{20,4},{24,8},{28,12},{1,17},{... | collective-permute-start | bytes 786440 | tf_op jit(solution)/shard_map/ppermute | solution.py:363
  445.8 11.5 %collective-permute-start.52 = (bf16[112,1024]{1,0:T(8,128)(2,1)S(1)}, bf16[112,1024]{1,0:T(8,128)(2,1)S(1)}, u32[]{:S(2)}, u32[]{:S(2)}) collective-permute-start(bf16[112,1024]{1,0:T(8,128)(2,1)S(1)} %fusion.51), channel_id=1, source_target_pairs={{0,1},{1,2},{2,3},{3,0},{4,5},{5,6},{6,7},{7,4},{8,9},{9,10},{10,1... | collective-permute-start | bytes 688136 | tf_op jit(solution)/shard_map/ppermute | solution.py:368
  457.3 21.8 %collective-permute-start.59 = (bf16[256,1024]{1,0:T(8,128)(2,1)S(1)}, bf16[256,1024]{1,0:T(8,128)(2,1)S(1)}, u32[]{:S(2)}, u32[]{:S(2)}) collective-permute-start(bf16[256,1024]{1,0:T(8,128)(2,1)S(1)} %get-tuple-element.277), channel_id=1, source_target_pairs={{0,1},{1,5},{2,0},{3,4},{4,3},{5,7},{6,2},{7,6},{8,9},{9,13},{10,8... | collective-permute-start | bytes 1572872 | tf_op jit(solution)/shard_map/ppermute | solution.py:608
  460.3 18.1 %collective-permute-start.54 = (bf16[112,1024]{1,0:T(8,128)(2,1)S(1)}, bf16[112,1024]{1,0:T(8,128)(2,1)S(1)}, u32[]{:S(2)}, u32[]{:S(2)}) collective-permute-start(bf16[112,1024]{1,0:T(8,128)(2,1)S(1)} %fusion.46), channel_id=1, source_target_pairs={{0,1},{1,2},{2,3},{3,0},{4,5},{5,6},{6,7},{7,4},{8,9},{9,10},{10,1... | collective-permute-start | bytes 688136 | tf_op jit(solution)/shard_map/ppermute | solution.py:368
  478.5 8.6 %collective-permute-start.56 = (bf16[112,1024]{1,0:T(8,128)(2,1)S(1)}, bf16[112,1024]{1,0:T(8,128)(2,1)S(1)}, u32[]{:S(2)}, u32[]{:S(2)}) collective-permute-start(bf16[112,1024]{1,0:T(8,128)(2,1)S(1)} %fusion.44), channel_id=1, source_target_pairs={{0,1},{1,2},{2,3},{3,0},{4,5},{5,6},{6,7},{7,4},{8,9},{9,10},{10,1... | collective-permute-start | bytes 688136 | tf_op jit(solution)/shard_map/ppermute | solution.py:368
  490.3 5.4 %collective-permute-start.61 = (bf16[32,2304]{1,0:T(8,128)(2,1)S(1)}, bf16[32,2304]{1,0:T(8,128)(2,1)S(1)}, u32[]{:S(2)}, u32[]{:S(2)}) collective-permute-start(bf16[32,2304]{1,0:T(8,128)(2,1)S(1)} %get-tuple-element.295), channel_id=1, source_target_pairs={{0,8},{4,12},{8,0},{12,4},{16,24},{20,28},{24,16},{28,20},{1,9},{5... | collective-permute-start | bytes 442376 | tf_op jit(solution)/shard_map/ppermute | solution.py:363
  490.6 5.1 %collective-permute-start.62 = (bf16[32,2304]{1,0:T(8,128)(2,1)S(1)}, bf16[32,2304]{1,0:T(8,128)(2,1)S(1)}, u32[]{:S(2)}, u32[]{:S(2)}) collective-permute-start(bf16[32,2304]{1,0:T(8,128)(2,1)S(1)} %get-tuple-element.297), channel_id=1, source_target_pairs={{0,4},{4,0},{8,12},{12,8},{16,20},{20,16},{24,28},{28,24},{1,5},{5... | collective-permute-start | bytes 442376 | tf_op jit(solution)/shard_map/ppermute | solution.py:363
  491.1 8.1 %collective-permute-start.63 = (bf16[32,2304]{1,0:T(8,128)(2,1)S(1)}, bf16[32,2304]{1,0:T(8,128)(2,1)S(1)}, u32[]{:S(2)}, u32[]{:S(2)}) collective-permute-start(bf16[32,2304]{1,0:T(8,128)(2,1)S(1)} %get-tuple-element.296), channel_id=1, source_target_pairs={{0,12},{4,8},{8,4},{12,0},{16,28},{20,24},{24,20},{28,16},{1,13},{... | collective-permute-start | bytes 442376 | tf_op jit(solution)/shard_map/ppermute | solution.py:363
  492.3 1.3 collective-permute-start.60
  (93 other events, 675.2 us)
